TPU v7x, 32 devices: a whole 2x2x4 slice. The times are simulated.
32 devices in a mesh: dp: 8 (over z, y), seq: 4 (over x, core).
Axes of the slice: x: 2, y: 2, z: 4, core: 2. Of those that a mesh axis runs over, the one named last changes fastest.
Arguments:
- tokens: bfloat16 [16, 512, 768], P('dp', 'seq'), may hold values from -6 to 6
- segment_ids: int32 [16, 512], P('dp'), may hold values from 0 to 7, never falling along the last dimension, each value on 1 to 128 neighbouring positions
- padding: int32 [16, 512], P('dp'), may hold values 0 or 1
- w_qkv: bfloat16 [768, 2304], replicated, may hold values from -0.21875 to 0.21875
- b_query: float32 [768], replicated, may hold values from -3 to 3
- b_value: float32 [768], replicated, may hold values from -3 to 3
- w_out: bfloat16 [768, 768], replicated, may hold values from -0.625 to 0.625
- b_out: float32 [768], replicated, may hold values from -3 to 3
- ln1_gain: float32 [768], replicated, may hold values from 0.1 to 1.9
- ln1_bias: float32 [768], replicated, may hold values from -3 to 3
- w_in: bfloat16 [768, 3072], replicated, may hold values from -0.21875 to 0.21875
- b_in: float32 [3072], replicated, may hold values from -3 to 3
- w_back: bfloat16 [3072, 768], replicated, may hold values from -0.109375 to 0.109375
- b_back: float32 [768], replicated, may hold values from -3 to 3
- ln2_gain: float32 [768], replicated, may hold values from 0.1 to 1.9
- ln2_bias: float32 [768], replicated, may hold values from -3 to 3
- out_grad: bfloat16 [16, 512, 768], P('dp', 'seq'), may hold values from -6 to 6
Outputs:
- layer_output: bfloat16 [16, 512, 768], P('dp', 'seq')
- input_grad: bfloat16 [16, 512, 768], P('dp', 'seq')
- grad_w_qkv: float32 [768, 2304], P('dp', 'seq')
- grad_b_query: float32 [768], replicated
- grad_b_value: float32 [768], replicated
- grad_w_out: float32 [768, 768], P('dp', 'seq')
- grad_b_out: float32 [768], replicated
- grad_ln1_gain: float32 [768], replicated
- grad_ln1_bias: float32 [768], replicated
- grad_w_in: float32 [768, 3072], P('dp', 'seq')
- grad_b_in: float32 [3072], replicated
- grad_w_back: float32 [3072, 768], P('dp', 'seq')
- grad_b_back: float32 [768], replicated
- grad_ln2_gain: float32 [768], replicated
- grad_ln2_bias: float32 [768], replicated
Inputs may be any that keep to these rules, and one draw needn't show every extreme that they name: `segment_ids`: along a row the ids never fall, and each id covers 1 to 128 consecutive tokens.
All inputs are finite; a program needn't handle non-finite values. No bound on the sum of `padding` on one device may be relied on, other than what follows from the above.
Results may differ from a plain program's by a relative error of at most 0.015.
Values may be sent and summed in bfloat16 or wider, within the bound.
No kernel may reach another device: no remote copies, remote signals or barrier semaphores. Data moves between devices by JAX's collectives and lax.ppermute only.
A program may use at most 128 MiB of HBM per device.

v0:
```python
import functools

import jax
import jax.numpy as jnp
from jax import lax
from jax.experimental import pallas as pl
from jax.experimental.pallas import tpu as pltpu
from jax.sharding import PartitionSpec as P

HEADS = 12
HDIM = 64
PAIR = 2 * HDIM
LN_EPS = 1e-12
FAR = -1e9
SUM_ROWS = 16
BOTH = ("dp", "seq")
BF = jnp.bfloat16
F32 = jnp.float32
HBM = pl.BlockSpec(memory_space=pltpu.HBM)
VMEM = pl.BlockSpec(memory_space=pltpu.VMEM)
SMEM = pl.BlockSpec(memory_space=pltpu.SMEM)


def dot(a, b, ca=1, cb=0):
    return lax.dot_general(a, b, (((ca,), (cb,)), ((), ())), preferred_element_type=F32)


def mean_of(v):
    return jnp.mean(v, axis=-1, keepdims=True)


def norm_parts(values):
    center = values - mean_of(values)
    inverse = lax.rsqrt(mean_of(center * center) + LN_EPS)
    return center * inverse, inverse


def norm_pull(upstream, normed, inverse, gain):
    scaled = upstream * gain
    return (scaled - mean_of(scaled) - normed * mean_of(scaled * normed)) * inverse


def col_sum(v):
    return jnp.sum(v, axis=0, keepdims=True)


def mask_of(me, groups, ids_ref, row, loc):
    own = pl.ds(pl.multiple_of(me * loc, loc), loc)
    seg_ref, pad_ref = ids_ref.at[0], ids_ref.at[1]
    seg_t = jnp.broadcast_to(seg_ref[row : row + 1, own].astype(F32), (loc, loc)).T
    pad_t = jnp.broadcast_to(pad_ref[row : row + 1, own].astype(F32), (loc, loc)).T
    eye = lax.broadcasted_iota(jnp.int32, (loc, loc), 0) == lax.broadcasted_iota(
        jnp.int32, (loc, loc), 1
    )
    keys, queries = [], []
    for block in range(3):
        at = me + block - 1
        out_of = jnp.where((at < 0) | (at >= groups), FAR, 0.0).astype(F32)
        at = jnp.clip(at, 0, groups - 1)
        span = pl.ds(pl.multiple_of(at * loc, loc), loc)
        seg_b = seg_ref[row : row + 1, span].astype(F32)
        pad_b = pad_ref[row : row + 1, span].astype(F32)
        same = seg_t == seg_b
        seen, seen_t = pad_b == 0.0, pad_t == 0.0
        if block == 1:
            seen, seen_t = seen | eye, seen_t | eye
        keys.append(jnp.where(same & seen, 0.0, FAR) + out_of)
        queries.append(jnp.where(same & seen_t, 0.0, FAR) + out_of)
    return jnp.concatenate(keys, axis=1), jnp.concatenate(queries, axis=1)


def split_pair(v, low):
    zero = jnp.zeros_like(v)
    return jnp.concatenate([jnp.where(low, v, zero), jnp.where(low, zero, v)], axis=0)


def join_pair(v, low):
    half = v.shape[0] // 2
    return jnp.where(low, v[:half], v[half:])


def own_kernel(
    groups, me_ref, ids_ref, tok_ref, vec_ref, wqkv, qkv_ref, mask_ref, mask_t_ref
):
    me = me_ref[0]
    rows, width = tok_ref.shape
    loc = rows // 2
    for row in range(2):
        mask_ref[row], mask_t_ref[row] = mask_of(me, groups, ids_ref, row, loc)
    vec = vec_ref[...].reshape(1, -1)
    biases = (vec[:, :width], 0.0, vec[:, width : 2 * width])
    for part in range(3):
        cols = slice(part * width, (part + 1) * width)
        qkv_ref[:, cols] = (dot(tok_ref[...], wqkv[:, cols]) + biases[part]).astype(BF)


def forward_kernel(
    groups,
    me_ref,
    tok_prev,
    tok_next,
    tok_own,
    own_ref,
    mask_ref,
    vec_ref,
    vec2_ref,
    b_in_ref,
    wqkv,
    og_hbm,
    wout_hbm,
    win_hbm,
    wback_hbm,
    qkv_ref,
    acts_ref,
    feed_ref,
    slope_ref,
    lse_ref,
    normed_ref,
    inv_ref,
    gtwo_ref,
    out_ref,
    keep_ref,
    small_ref,
    wout,
    win,
    wback,
    ctx_ref,
    og_ref,
    sems,
):
    me = me_ref[0]
    rows, width = tok_own.shape
    loc = rows // 2
    ff = win.shape[1]
    pairs = ((wout_hbm, wout), (win_hbm, win), (wback_hbm, wback), (og_hbm, og_ref))
    copies = [pltpu.make_async_copy(a, b, sems.at[i]) for i, (a, b) in enumerate(pairs)]
    for copy in copies:
        copy.start()
    vec, vec2 = vec_ref[...].reshape(1, -1), vec2_ref[...].reshape(1, -1)
    b_query, b_value, b_out, gain1 = (vec[:, i * width : (i + 1) * width] for i in range(4))
    shift1, b_back, gain2, shift2 = (vec2[:, i * width : (i + 1) * width] for i in range(4))
    b_in = b_in_ref[...].reshape(1, -1)
    b_qkv = (b_query, 0.0, b_value)
    for part in range(3):
        cols = slice(part * width, (part + 1) * width)
        for block, tok in enumerate((tok_prev, tok_next)):
            qkv_ref[block, :, cols] = (dot(tok[...], wqkv[:, cols]) + b_qkv[part]).astype(BF)
    blocks = (qkv_ref.at[0], own_ref, qkv_ref.at[1])
    low = lax.broadcasted_iota(jnp.int32, (loc, PAIR), 1) < HDIM
    lanes = lax.broadcasted_iota(jnp.int32, (loc, 128), 1)

    def attend(p, totals):
        spans = [pl.ds(pl.multiple_of(p * PAIR + part * width, PAIR), PAIR) for part in range(3)]
        result = []
        for row in range(2):
            at = slice(row * loc, (row + 1) * loc)
            q2 = split_pair(own_ref[at, spans[0]], low) * jnp.asarray(HDIM**-0.5, BF)
            k3 = jnp.concatenate([b[at, spans[1]] for b in blocks], axis=0)
            v3 = jnp.concatenate([b[at, spans[2]] for b in blocks], axis=0)
            mask = mask_ref[row]
            scores = dot(q2, k3, 1, 1) + jnp.concatenate([mask, mask], axis=0)
            top = jnp.max(scores, axis=-1, keepdims=True)
            powers = jnp.exp(scores - top)
            total = jnp.sum(powers, axis=-1, keepdims=True)
            probs = (powers * (1.0 / total)).astype(BF)
            ctx_ref[at, pl.ds(pl.multiple_of(p * PAIR, PAIR), PAIR)] = join_pair(
                dot(probs, v3), low
            ).astype(BF)
            lse = top + jnp.log(total)
            old = totals[row]
            old = jnp.where(lanes == 2 * p, lse[:loc], old)
            result.append(jnp.where(lanes == 2 * p + 1, lse[loc:], old))
        return tuple(result)

    zero = jnp.zeros((loc, 128), F32)
    totals = lax.fori_loop(0, HEADS // 2, attend, (zero, zero))
    lse_ref[:loc, :] = totals[0]
    lse_ref[loc:, :] = totals[1]
    context = ctx_ref[...]
    acts_ref[:, ff + width : ff + 2 * width] = context
    copies[0].wait()
    branch = dot(context, wout[...]) + b_out
    normed, inverse = norm_parts(tok_own[...].astype(F32) + branch)
    normed_ref[...] = normed
    inv_ref[...] = inverse
    first = normed * gain1 + shift1
    first_low = first.astype(BF)
    acts_ref[:, ff : ff + width] = first_low
    copies[1].wait()
    copies[2].wait()
    feed = first + b_back
    for c in range(ff // width):
        cols = slice(c * width, (c + 1) * width)
        before = dot(first_low, win[:, cols]) + b_in[:, cols]
        cdf = 0.5 + 0.5 * lax.erf(before * (0.5**0.5))
        hidden = (before * cdf).astype(BF)
        acts_ref[:, cols] = hidden
        bell = jnp.exp(-0.5 * before * before) * (0.3989422804014327)
        slope_ref[:, cols] = (cdf + before * bell).astype(BF)
        feed = feed + dot(hidden, wback[cols, :])
    normed2, inverse2 = norm_parts(feed)
    out_ref[...] = (normed2 * gain2 + shift2).astype(BF)
    copies[3].wait()
    upstream = og_ref[...].astype(F32)
    grad_two = norm_pull(upstream, normed2, inverse2, gain2)
    gtwo_ref[...] = grad_two
    feed_grad = grad_two.astype(BF)
    feed_ref[...] = feed_grad
    small_ref[0:1, :] = col_sum(feed_grad.astype(F32))
    small_ref[1:2, :] = col_sum(upstream * normed2)
    small_ref[2:3, :] = col_sum(upstream)
    base = ff + 2 * width
    block = width // groups
    for s in range(groups):
        rel = s ^ me
        piece = feed_grad[:, s * block : (s + 1) * block]
        for i in range(groups // 2):

            @pl.when(rel == 2 * i)
            def _():
                keep_ref[:, i * block : (i + 1) * block] = piece

            @pl.when(rel == 2 * i + 1)
            def _():
                acts_ref[:, base + i * block : base + (i + 1) * block] = piece


def backward_kernel(
    groups,
    me_ref,
    feed_ref,
    slope_ref,
    gtwo_ref,
    normed_ref,
    inv_ref,
    acts_ref,
    lse_ref,
    vec_ref,
    wback_hbm,
    win_hbm,
    wout_hbm,
    keep_ref,
    send_ref,
    msg_ref,
    gone_ref,
    small_ref,
    wback,
    win,
    wout,
    sems,
):
    me = me_ref[0]
    rows, width = feed_ref.shape
    ff = win.shape[1]
    block = ff // groups
    spans = [pl.ds(pl.multiple_of((i ^ me) * block, block), block) for i in range(groups)]
    copies = []
    for i, span in enumerate(spans):
        copies += [
            pltpu.make_async_copy(wback_hbm.at[span], wback.at[span], sems.at[2 * i]),
            pltpu.make_async_copy(win_hbm.at[:, span], win.at[:, span], sems.at[2 * i + 1]),
        ]
    copies += [
        pltpu.make_async_copy(wout_hbm, wout, sems.at[2 * groups]),
    ]
    for copy in copies:
        copy.start()
    feed_grad = feed_ref[...]
    first_grad = gtwo_ref[...]
    for i, span in enumerate(spans):
        s = i ^ me
        copies[2 * i].wait()
        copies[2 * i + 1].wait()
        hidden_grad = dot(feed_grad, wback[span, :], 1, 1)
        before_grad = (hidden_grad * slope_ref[:, span].astype(F32)).astype(BF)
        small_ref[pl.ds(s, 1), :] = col_sum(before_grad.astype(F32))
        target = send_ref if i % 2 else keep_ref
        target[:, (i // 2) * block : (i // 2 + 1) * block] = before_grad
        first_grad = first_grad + dot(before_grad, win[:, span], 1, 1)
    copies[-1].wait()
    normed = normed_ref[...]
    grad_one = norm_pull(first_grad, normed, inv_ref[...], vec_ref[3 * width :].reshape(1, -1))
    gone_ref[...] = grad_one
    branch_grad = grad_one.astype(BF)
    small_ref[4:5, :] = col_sum(branch_grad.astype(F32))
    small_ref[5:6, :] = col_sum(first_grad * normed)
    small_ref[6:7, :] = col_sum(first_grad)
    context_grad = dot(branch_grad, wout[...], 1, 1).astype(BF)
    msg_ref[:, :width] = context_grad
    product = context_grad.astype(F32) * acts_ref[:, ff + width : ff + 2 * width].astype(F32)
    lanes = lax.broadcasted_iota(jnp.int32, (rows, 128), 1)
    low = lanes < HDIM
    delta = jnp.zeros((rows, 128), F32)
    for p in range(HEADS // 2):
        tile = product[:, p * PAIR : (p + 1) * PAIR]
        both = jnp.sum(tile, axis=-1, keepdims=True)
        even = jnp.sum(jnp.where(low, tile, 0.0), axis=-1, keepdims=True)
        delta = jnp.where(lanes == 2 * p, even, delta)
        delta = jnp.where(lanes == 2 * p + 1, both - even, delta)
    packed = jnp.zeros((rows, 128), F32)
    shift = 0
    for value in (lse_ref[...], delta):
        for _ in range(3):
            term = value.astype(BF).astype(F32)
            packed = packed + (pltpu.roll(term, shift, 1) if shift else term)
            value = value - term
            shift += 16
    msg_ref[:, width:] = packed.astype(BF)
    base = 2 * block
    small = width // groups
    for s in range(groups):
        rel = s ^ me
        piece = branch_grad[:, s * small : (s + 1) * small]
        for i in range(groups // 2):

            @pl.when(rel == 2 * i)
            def _():
                keep_ref[:, base + i * small : base + (i + 1) * small] = piece

            @pl.when(rel == 2 * i + 1)
            def _():
                send_ref[:, base + i * small : base + (i + 1) * small] = piece


def attend_back_kernel(
    groups,
    me_ref,
    mask_ref,
    mask_t_ref,
    near_ref,
    own_ref,
    msg_prev,
    msg_own,
    msg_next,
    small1_ref,
    small2_ref,
    all_ref,
    keep_ref,
    send_ref,
    send2_ref,
    sums_ref,
    info_t_ref,
):
    me = me_ref[0]
    rows = msg_own.shape[0]
    width = own_ref.shape[1] // 3
    loc = rows // 2
    msgs = (msg_prev, msg_own, msg_next)
    blocks = (near_ref.at[0], own_ref, near_ref.at[1])
    own_info = []
    for row in range(2):
        at = slice(row * loc, (row + 1) * loc)
        for b in range(3):
            raw = msgs[b][at, width:].astype(F32)
            info = raw + pltpu.roll(raw, 112, 1) + pltpu.roll(raw, 96, 1)
            if b == 1:
                own_info.append(info)
            info_t_ref[row, b] = info.T
    low = lax.broadcasted_iota(jnp.int32, (loc, PAIR), 1) < HDIM
    lanes = lax.broadcasted_iota(jnp.int32, (loc, 128), 1)
    scale = jnp.asarray(HDIM**-0.5, BF)

    def column(info, lane):
        return jnp.sum(jnp.where(lanes == lane, info, 0.0), axis=-1, keepdims=True)

    def heads(p, carry):
        spans = [pl.ds(pl.multiple_of(p * PAIR + part * width, PAIR), PAIR) for part in range(3)]
        for row in range(2):
            at = slice(row * loc, (row + 1) * loc)
            info = own_info[row]
            lse2 = jnp.concatenate([column(info, 2 * p), column(info, 2 * p + 1)], axis=0)
            delta2 = jnp.concatenate([column(info, 48 + 2 * p), column(info, 49 + 2 * p)], axis=0)
            q3 = jnp.concatenate([b[at, spans[0]] for b in blocks], axis=0)
            k3 = jnp.concatenate([b[at, spans[1]] for b in blocks], axis=0)
            v3 = jnp.concatenate([b[at, spans[2]] for b in blocks], axis=0)
            u3 = jnp.concatenate([m[at, spans[0]] for m in msgs], axis=0)
            mask = mask_ref[row]
            scores = dot(split_pair(q3[loc : 2 * loc], low) * scale, k3, 1, 1)
            probs = jnp.exp(scores + jnp.concatenate([mask, mask], axis=0) - lse2)
            prob_grad = dot(split_pair(u3[loc : 2 * loc], low), v3, 1, 1)
            score_grad = (probs * (prob_grad - delta2)).astype(BF)
            query_grad = join_pair(dot(score_grad, k3), low) * HDIM**-0.5
            all_ref[at, spans[0]] = query_grad.astype(BF)

            def line(which):
                halves = []
                for h in range(2):
                    parts = [info_t_ref[row, b, pl.ds(which + 2 * p + h, 1), :] for b in range(3)]
                    halves.append(
                        jnp.broadcast_to(jnp.concatenate(parts, axis=1), (loc, 3 * loc))
                    )
                return jnp.concatenate(halves, axis=0)

            mask_t = mask_t_ref[row]
            scores_t = dot(split_pair(k3[loc : 2 * loc], low) * scale, q3, 1, 1)
            probs_t = jnp.exp(scores_t + jnp.concatenate([mask_t, mask_t], axis=0) - line(0))
            value_grad = join_pair(dot(probs_t.astype(BF), u3), low)
            prob_grad_t = dot(split_pair(v3[loc : 2 * loc], low), u3, 1, 1)
            score_grad_t = (probs_t * (prob_grad_t - line(48))).astype(BF)
            key_grad = join_pair(dot(score_grad_t, q3), low) * HDIM**-0.5
            all_ref[at, spans[1]] = key_grad.astype(BF)
            all_ref[at, spans[2]] = value_grad.astype(BF)
        return carry

    lax.fori_loop(0, HEADS // 2, heads, 0)
    value_at = 2 * width
    sums_ref[...] = jnp.concatenate(
        [
            small1_ref[...],
            small2_ref[...],
            col_sum(all_ref[:, :width].astype(F32)),
            col_sum(all_ref[:, value_at:].astype(F32)),
            jnp.zeros((SUM_ROWS - 12, width), F32),
        ],
        axis=0,
    )
    send_ref[loc:, :] = jnp.zeros((2 * SUM_ROWS, send_ref.shape[1]), BF)
    pack_sums(sums_ref[...], send_ref, loc)
    block = 3 * width // groups
    for s in range(groups):
        rel = s ^ me
        piece = all_ref[:, s * block : (s + 1) * block]
        for i in range(groups // 2):

            @pl.when(rel == 2 * i)
            def _():
                keep_ref[:, i * block : (i + 1) * block] = piece

            @pl.when(rel == 2 * i + 1)
            def _():
                send_ref[:loc, i * block : (i + 1) * block] = piece[:loc]
                send2_ref[:, i * block : (i + 1) * block] = piece[loc:]


def pack_sums(value, ref, at):
    high = value.astype(BF)
    ref[at : at + SUM_ROWS, : value.shape[1]] = high
    ref[at + SUM_ROWS : at + 2 * SUM_ROWS, : value.shape[1]] = (value - high.astype(F32)).astype(BF)


def read_sums(ref, at, width):
    high = ref[at : at + SUM_ROWS, :width].astype(F32)
    return high + ref[at + SUM_ROWS : at + 2 * SUM_ROWS, :width].astype(F32)


def turn_rows(d, dp, tmp_ref, turned_ref, block_rows, part):
    rows = block_rows // 2
    for j, rel in enumerate(low_first(dp)):
        start = pl.multiple_of((rel ^ d) * block_rows + part * rows, rows)
        turned_ref[j * rows : (j + 1) * rows, :] = tmp_ref[pl.ds(start, rows), :]


def low_first(dp):
    bits = dp.bit_length() - 1
    return [sum(((j >> (bits - 1 - k)) & 1) << k for k in range(bits)) for j in range(dp)]


def both_left(mine, peer):
    return jnp.concatenate([mine.T, peer.T], axis=1)


def by_halves(pieces, base, width):
    return [
        jnp.concatenate([r[:, base + x * width : base + (x + 1) * width] for r in pieces], axis=0)
        for x in range(2)
    ]


def put(result, part, x, keeps, sends):
    total = result.shape[0]
    half = total // 2
    if part == 0:
        (sends if x else keeps)[0][:total] = result
    else:
        keeps[1][x * half : (x + 1) * half] = result[:half]
        sends[1][x * half : (x + 1) * half] = result[half:]


def in_kernel(dp, d_ref, acts, acts_peer, mine, peer, keep0, send0, keep1, send1, tmp, *turned):
    width = acts.shape[1]
    tmp[...] = both_left(acts[...], acts_peer[...])
    wide = (mine.shape[1] - width // 2) // 2
    rights = by_halves((mine, peer), 0, wide)
    for part in range(2):
        turn_rows(d_ref[0], dp, tmp, turned[part], width // dp, part)
        for x in range(2):
            result = dot(turned[part][...], rights[x]).astype(BF)
            put(result, part, x, (keep0, keep1), (send0, send1))


def qkv_kernel(
    dp,
    ids_ref,
    tok,
    tok_prev,
    tok_next,
    ctx,
    ctx_peer,
    mine,
    peer,
    peer2,
    out_mine,
    out_peer,
    sums_ref,
    keep0,
    send0,
    keep1,
    send1,
    total_ref,
    tmp,
    tmp2,
    *turned,
):
    rows, width = tok.shape
    d = ids_ref[0]
    other = jnp.where(ids_ref[1] % 2 == 0, tok_next[...], tok_prev[...])
    tmp[...] = both_left(tok[...], other)
    tmp2[...] = both_left(ctx[...], ctx_peer[...])
    half = peer2.shape[0]
    rights = by_halves((mine, peer.at[:half], peer2), 0, mine.shape[1] // 2)
    outs = by_halves((out_mine, out_peer), 0, out_mine.shape[1] // 2)
    for part in range(2):
        turn_rows(d, dp, tmp, turned[part], width // dp, part)
        turn_rows(d, dp, tmp2, turned[2 + part], width // dp, part)
        for x in range(2):
            result = jnp.concatenate(
                [dot(turned[part][...], rights[x]), dot(turned[2 + part][...], outs[x])], axis=1
            ).astype(BF)
            put(result, part, x, (keep0, keep1), (send0, send1))
    total = sums_ref[...] + read_sums(peer, half, width)
    total_ref[...] = total
    pack_sums(total, send0, keep0.shape[0])


def back_kernel(dp, d_ref, hid, hid_peer, feed, feed_peer, keep0, send0, keep1, send1):
    d = d_ref[0]
    chunk = hid.shape[1] // dp
    side = feed.shape[1] // 2
    rows = side // 4
    turned = [feed[...].T, feed_peer[...].T]
    first, second, *rest = HALVING["back"]
    orders = [(first, second, *rest), (second, first, *rest)]
    for rel in range(dp):
        span = pl.ds(pl.multiple_of((rel ^ d) * chunk, chunk), chunk)
        result = (dot(turned[0], hid[:, span]) + dot(turned[1], hid_peer[:, span])).astype(BF)
        for x in range(2):
            bits = 2 * x + 4 * rel
            for part, refs in enumerate(((keep0, send0), (keep1, send1))):
                at = 0
                for bit in orders[part]:
                    at = 2 * at + ((bits >> bit) & 1)
                ref, at = refs[at // dp], at % dp
                for h in range(2):
                    start = x * side + h * 2 * rows + part * rows
                    ref[at * rows : (at + 1) * rows, h * chunk : (h + 1) * chunk] = result[
                        start : start + rows
                    ]


def total_of(keep, got):
    return keep[...].astype(F32) + got[: keep.shape[0]].astype(F32)


def step_sums(sums_ref, got, at, total_ref, send, send_at):
    total = sums_ref[...] + read_sums(got, at, sums_ref.shape[1])
    total_ref[...] = total
    if send is not None:
        pack_sums(total, send, send_at)


def first_step(keep0, got0, keep1, got1, *refs):
    if len(refs) == 6:
        sums_ref, new0, send0, new1, send1, total_ref = refs
        step_sums(sums_ref, got0, keep0.shape[0], total_ref, send0, keep0.shape[0] // 2)
    else:
        new0, send0, new1, send1 = refs
    half = keep0.shape[0] // 2
    for keep, got, new, send in ((keep0, got0, new0, send0), (keep1, got1, new1, send1)):
        total = total_of(keep, got).astype(BF)
        new[...] = total[:half]
        send[:half] = total[half:]


def second_step(rows, keep0, got0, keep1, got1, *refs):
    if len(refs) == 4:
        sums_ref, new, send, total_ref = refs
        step_sums(sums_ref, got0, keep0.shape[0], total_ref, send, new.shape[0])
    else:
        new, send = refs
    half = keep0.shape[0] // 2
    for part, (keep, got) in enumerate(((keep0, got0), (keep1, got1))):
        total = total_of(keep, got).astype(BF)
        for b in range(half // rows):
            at = (2 * b + part) * rows
            new[at : at + rows] = total[b * rows : (b + 1) * rows]
            send[at : at + rows] = total[half + b * rows : half + (b + 1) * rows]


def third_step(keep, got, *refs):
    if len(refs) == 4:
        sums_ref, new, send, total_ref = refs
        step_sums(sums_ref, got, keep.shape[0], total_ref, send, new.shape[0])
    else:
        new, send = refs
    half = keep.shape[0] // 2
    total = total_of(keep, got).astype(BF)
    new[...] = total[:half]
    send[:half] = total[half:]


def last_step(kind, keep, got, *refs):
    total = total_of(keep, got)
    if kind == "back":
        chunk = total.shape[1] // 2
        refs[0][...] = jnp.concatenate([total[:, :chunk].T, total[:, chunk:].T], axis=1)
    elif kind == "in":
        refs[0][...] = total
    else:
        sums_ref, qkv_ref, out_ref, total_ref = refs
        qkv_ref[...] = total[:, : qkv_ref.shape[1]]
        out_ref[...] = total[:, qkv_ref.shape[1] :]
        step_sums(sums_ref, got, keep.shape[0], total_ref, None, 0)


HALVING = {"back": (2, 3, 1, 4), "in": (1, 2, 3, 4), "qkv": (1, 2, 3, 4)}


def flip(value, bit):
    count = lax.axis_size("dp") * lax.axis_size("seq")
    return lax.ppermute(value, BOTH, [(i, i ^ (1 << bit)) for i in range(count)])


class Reduction:
    def __init__(self, kind, parts, sums=None):
        self.kind, self.keeps, self.sums = kind, parts[0::2], sums
        self.at, self.result = 0, None
        self.gots = tuple(flip(v, b) for v, b in zip(parts[1::2], HALVING[kind]))

    def step(self, outs):
        extra = 0 if self.sums is None else 2 * SUM_ROWS
        total = self.keeps[0].shape[0]
        width = self.keeps[0].shape[1]
        half = total // 2
        operands = [v for pair in zip(self.keeps, self.gots) for v in pair]
        sums = () if self.sums is None else (shape_of(SUM_ROWS, width, dtype=F32),)
        if self.at == 0:
            kernel = first_step
            shapes = (half, half + extra, half, half)
        elif self.at == 1:
            kernel = functools.partial(second_step, outs["rows"])
            shapes = (total, total + extra)
        else:
            kernel, shapes = third_step, (half, half + extra)
        shapes = tuple(shape_of(n, width) for n in shapes) + sums
        last = self.at > 1 and "last" in outs
        if last:
            kernel = functools.partial(last_step, self.kind)
            shapes = tuple(shape_of(*dims, dtype=F32) for dims in outs["last"]) + sums
        if self.sums is not None:
            operands.append(self.sums)
        result = pl.pallas_call(
            kernel,
            name=f"add_{self.kind}_{self.at}",
            cost_estimate=cost(1),
            out_shape=shapes,
            in_specs=[VMEM] * len(operands),
            out_specs=(VMEM,) * len(shapes),
            compiler_params=params(12),
        )(*operands)
        if self.sums is not None:
            self.sums = result[-1]
        self.at += 1
        if last:
            self.result = result
            return
        self.keeps = result[0 : len(shapes) - len(sums) : 2]
        sends = result[1 : len(shapes) - len(sums) : 2]
        bits = HALVING[self.kind]
        bits = bits[1::-1] if self.at == 1 else bits[self.at :]
        self.gots = tuple(flip(v, b) for v, b in zip(sends, bits))


def wait_for(unit, done):
    got, *rest = unit.gots
    if done.result is None:
        keep, *others = done.keeps
        got, keep = lax.optimization_barrier((got, keep))
        done.keeps = (keep, *others)
    else:
        first, *others = done.result
        got, first = lax.optimization_barrier((got, first))
        done.result = (first, *others)
    unit.gots = (got, *rest)


def plain_reduce(left, right):
    dp = lax.axis_size("dp")
    part = jnp.einsum("tk,xtw->xkw", left, right, preferred_element_type=F32).astype(BF)
    part = part[0].astype(F32) + flip(part[1], 1).astype(F32)
    part = part.reshape(dp, left.shape[1] // dp, right.shape[2]).astype(BF)
    part = jnp.take(part, jnp.arange(dp) ^ lax.axis_index("dp"), axis=0)
    for bit in reversed(range(dp.bit_length() - 1)):
        half = part.shape[0] // 2
        part = part[:half].astype(F32) + flip(part[half:], 2 + bit).astype(F32)
        part = part.astype(BF) if bit else part
    return part[0]


def plain_sum(value, low):
    count = lax.axis_size("dp") * lax.axis_size("seq")
    for bit in range(low, count.bit_length() - 1):
        value = value + flip(value, bit)
    return value


def shape_of(*dims, dtype=BF):
    return jax.ShapeDtypeStruct(dims, dtype)


def cost(us):
    return pl.CostEstimate(flops=int(us * 1e6), bytes_accessed=int(us * 1e4), transcendentals=0)


def params(mib):
    return pltpu.CompilerParams(vmem_limit_bytes=mib << 20)


def local(
    tokens,
    segment_ids,
    padding,
    w_qkv,
    b_query,
    b_value,
    w_out,
    b_out,
    ln1_gain,
    ln1_bias,
    w_in,
    b_in,
    w_back,
    b_back,
    ln2_gain,
    ln2_bias,
    out_grad,
):
    seqs, loc, width = tokens.shape
    groups, dp = lax.axis_size("seq"), lax.axis_size("dp")
    dp_bits = dp.bit_length() - 1
    ff = w_in.shape[1]
    rows = seqs * loc
    me = lax.axis_index("seq").astype(jnp.int32).reshape(1)
    d = lax.axis_index("dp").astype(jnp.int32).reshape(1)
    up = [(i, i + 1) for i in range(groups - 1)]
    down = [(i + 1, i) for i in range(groups - 1)]

    def around(value):
        return lax.ppermute(value, "seq", up), lax.ppermute(value, "seq", down)

    flat = tokens.reshape(rows, width)
    tok_prev, tok_next = around(flat)
    vec1 = jnp.concatenate([b_query, b_value, b_out, ln1_gain])
    vec2 = jnp.concatenate([ln1_bias, b_back, ln2_gain, ln2_bias])
    ids = jnp.stack([segment_ids, padding])
    own_qkv, mask, mask_t = pl.pallas_call(
        functools.partial(own_kernel, groups),
        name="own_projections",
        cost_estimate=cost(4),
        out_shape=(
            shape_of(rows, 3 * width),
            shape_of(seqs, loc, 3 * loc, dtype=F32),
            shape_of(seqs, loc, 3 * loc, dtype=F32),
        ),
        in_specs=[SMEM] + [VMEM] * 4,
        out_specs=(VMEM,) * 3,
        compiler_params=params(50),
    )(me, ids, flat, vec1, w_qkv)
    extra = width // groups * 2
    acts_width = ff + 2 * width + extra
    near_qkv, acts, feed_grad, slope, lse, normed, inverse, grad_two, result, feed_keep, small1 = (
        pl.pallas_call(
            functools.partial(forward_kernel, groups),
            name="layer_forward",
            cost_estimate=cost(16),
            out_shape=(
                shape_of(2, rows, 3 * width),
                shape_of(rows, acts_width),
                shape_of(rows, width),
                shape_of(rows, ff),
                shape_of(rows, 128, dtype=F32),
                shape_of(rows, width, dtype=F32),
                shape_of(rows, 1, dtype=F32),
                shape_of(rows, width, dtype=F32),
                shape_of(rows, width),
                shape_of(rows, extra),
                shape_of(3, width, dtype=F32),
            ),
            in_specs=[SMEM] + [VMEM] * 9 + [HBM] * 4,
            out_specs=(VMEM,) * 11,
            scratch_shapes=[
                pltpu.VMEM((width, width), BF),
                pltpu.VMEM((width, ff), BF),
                pltpu.VMEM((ff, width), BF),
                pltpu.VMEM((rows, width), BF),
                pltpu.VMEM((rows, width), BF),
                pltpu.SemaphoreType.DMA((4,)),
            ],
            compiler_params=params(46),
        )(
            me,
            tok_prev,
            tok_next,
            flat,
            own_qkv,
            mask,
            vec1,
            vec2,
            b_in,
            w_qkv,
            out_grad.reshape(rows, width),
            w_out,
            w_in,
            w_back,
        )
    )
    acts_peer = flip(acts, 0)

    side = 2 * (ff // groups) + extra
    grads_keep, grads_send, msg, grad_one, small2 = pl.pallas_call(
        functools.partial(backward_kernel, groups),
        name="layer_backward",
            cost_estimate=cost(8),
        out_shape=(
            shape_of(rows, side),
            shape_of(rows, side),
            shape_of(rows, width + 128),
            shape_of(rows, width, dtype=F32),
            shape_of(7, width, dtype=F32),
        ),
        in_specs=[SMEM] + [VMEM] * 8 + [HBM] * 3,
        out_specs=(VMEM,) * 5,
        scratch_shapes=[
            pltpu.VMEM((ff, width), BF),
            pltpu.VMEM((width, ff), BF),
            pltpu.VMEM((width, width), BF),
            pltpu.SemaphoreType.DMA((2 * groups + 1,)),
        ],
        compiler_params=params(44),
    )(me, feed_grad, slope, grad_two, normed, inverse, acts, lse, vec1, w_back, w_in, w_out)
    msg_prev, msg_next = around(msg)
    grads_peer = flip(grads_send, 0)

    kernels = (width // dp) % 32 == 0 and (ff // dp) % 128 == 0 and dp == 8
    small = width // groups
    wide = ff // groups
    qkv_block = 3 * width // groups
    block_rows = width // dp
    part_rows = dp * block_rows // 2
    base = ff + 2 * width

    def acts_block(i):
        return pl.BlockSpec((rows, width), lambda g: (0, i))

    first_at, ctx_at = ff // width, ff // width + 1
    out_at = 2 * wide // extra
    if kernels:
        back = pl.pallas_call(
            functools.partial(back_kernel, dp),
            name="grad_w_back",
            cost_estimate=cost(3),
            grid=(1,),
            out_shape=(shape_of(part_rows, width),) * 4,
            in_specs=[
                SMEM,
                pl.BlockSpec((rows, ff), lambda i: (0, 0)),
                pl.BlockSpec((rows, ff), lambda i: (0, 0)),
                pl.BlockSpec((rows, extra), lambda i: (0, 0)),
                pl.BlockSpec((rows, extra), lambda i: (0, base // extra)),
            ],
            compiler_params=params(16),
        )(d, acts, acts_peer, feed_keep, acts_peer)
        whole = pl.BlockSpec((rows, side), lambda g: (0, 0))
        inner = pl.pallas_call(
            functools.partial(in_kernel, dp),
            name="grad_w_in",
            cost_estimate=cost(4),
            grid=(1,),
            out_shape=(shape_of(part_rows, wide),) * 4,
            in_specs=[SMEM, acts_block(first_at), acts_block(first_at), whole, whole],
            scratch_shapes=[pltpu.VMEM((width, 2 * rows), BF)]
            + [pltpu.VMEM((width // 2, 2 * rows), BF)] * 2,
            compiler_params=params(16),
        )(d, acts, acts_peer, grads_keep, grads_peer)
        red_back = Reduction("back", back)
        red_in = Reduction("in", inner)
        msg_prev, msg_next, keep_a, keep_b = lax.optimization_barrier(
            (msg_prev, msg_next, red_back.keeps[0], red_in.keeps[0])
        )
        red_back.keeps = (keep_a, red_back.keeps[1])
        red_in.keeps = (keep_b, red_in.keeps[1])

    qkv_grad, qkv_keep, qkv_send, qkv_send2, sums = pl.pallas_call(
        functools.partial(attend_back_kernel, groups),
        name="attend_backward",
        cost_estimate=cost(11),
        out_shape=(
            shape_of(rows, 3 * width),
            shape_of(rows, 2 * qkv_block),
            shape_of(loc + 2 * SUM_ROWS, 2 * qkv_block),
            shape_of(rows - loc, 2 * qkv_block),
            shape_of(SUM_ROWS, width, dtype=F32),
        ),
        in_specs=[SMEM] + [VMEM] * 9,
        out_specs=(VMEM,) * 5,
        scratch_shapes=[pltpu.VMEM((2, 3, 128, loc), F32)],
        compiler_params=params(16),
    )(me, mask, mask_t, near_qkv, own_qkv, msg_prev, msg, msg_next, small1, small2)
    if kernels:
        red_back.step({})
        qkv_send, keep_a = lax.optimization_barrier((qkv_send, red_back.keeps[0]))
        red_back.keeps = (keep_a, red_back.keeps[1])
    qkv_peer, qkv_peer2 = flip(qkv_send, 0), flip(qkv_send2, 0)
    input_grad = grad_one + dot(qkv_grad, w_qkv, 1, 1)
    if kernels:
        red_in.step({})
        *qkv, sums = pl.pallas_call(
            functools.partial(qkv_kernel, dp),
            name="grad_w_qkv_out",
            cost_estimate=cost(3),
            out_shape=(
                shape_of(part_rows, width),
                shape_of(part_rows + 2 * SUM_ROWS, width),
                shape_of(part_rows, width),
                shape_of(part_rows, width),
                shape_of(SUM_ROWS, width, dtype=F32),
            ),
            grid=(1,),
            in_specs=[SMEM]
            + [pl.BlockSpec((rows, width), lambda i: (0, 0))] * 3
            + [acts_block(ctx_at)] * 2
            + [pl.BlockSpec((rows, 2 * qkv_block), lambda i: (0, 0))]
            + [pl.BlockSpec((loc + 2 * SUM_ROWS, 2 * qkv_block), lambda i: (0, 0))]
            + [pl.BlockSpec((rows - loc, 2 * qkv_block), lambda i: (0, 0))]
            + [pl.BlockSpec((rows, extra), lambda i: (0, out_at))] * 2
            + [pl.BlockSpec((SUM_ROWS, width), lambda i: (0, 0))],
            scratch_shapes=[pltpu.VMEM((width, 2 * rows), BF)] * 2
            + [pltpu.VMEM((width // 2, 2 * rows), BF)] * 4,
            compiler_params=params(20),
        )(
            jnp.concatenate([d, me]),
            flat,
            tok_prev,
            tok_next,
            acts,
            acts_peer,
            qkv_keep,
            qkv_peer,
            qkv_peer2,
            grads_keep,
            grads_peer,
            sums,
        )
        qkv[3], keep_b = lax.optimization_barrier((qkv[3], red_in.keeps[0]))
        red_in.keeps = (keep_b, red_in.keeps[1])
        red_qkv = Reduction("qkv", qkv, sums)
        units = (red_back, red_in, red_qkv)
        last = (
            ((ff // dp, small),),
            ((block_rows, wide),),
            ((block_rows, qkv_block), (block_rows, small)),
        )
        done = None
        for k in EVENTS if dp_bits == 3 else [0, 1, 2] * (dp_bits + 1):
            if units[k].at > dp_bits:
                continue
            outs = {"rows": block_rows // 2}
            if units[k].at == dp_bits:
                outs["last"] = last[k]
            if done is not None and done is not units[k]:
                wait_for(units[k], done)
            units[k].step(outs)
            done = units[k]
        g_back = red_back.result[0]
        g_in = red_in.result[0]
        g_qkv, g_out, sums = red_qkv.result
    else:

        def by_x(v, w):
            return v.reshape(v.shape[0], 2, w).transpose(1, 0, 2)

        def pile(a, b):
            return jnp.concatenate([a, b], axis=0)

        feeds = by_x(pile(feed_keep, acts_peer[:, base:]), small)
        g_back = plain_reduce(pile(acts[:, :ff], acts_peer[:, :ff]), feeds)
        grads = pile(grads_keep, grads_peer)
        lefts = pile(acts, acts_peer)
        g_in = plain_reduce(lefts[:, ff : ff + width], by_x(grads[:, : 2 * wide], wide))
        g_out = plain_reduce(lefts[:, ff + width : base], by_x(grads[:, 2 * wide :], small))
        other = jnp.where(me[0] % 2 == 0, tok_next, tok_prev)
        grads = by_x(pile(qkv_keep, pile(qkv_peer[:loc], qkv_peer2)), qkv_block)
        g_qkv = plain_reduce(pile(flat, other), grads)
        sums = plain_sum(sums, 0)
    b_back_g, gain2, shift2 = sums[0], sums[1], sums[2]
    b_in_g = sums[3:7].reshape(-1)
    b_out_g, gain1, shift1, b_q_g, b_v_g = sums[7], sums[8], sums[9], sums[10], sums[11]
    shape = (seqs, loc, width)
    return (
        result.reshape(shape),
        input_grad.reshape(shape).astype(BF),
        g_qkv,
        b_q_g,
        b_v_g,
        g_out,
        b_out_g,
        gain1,
        shift1,
        g_in,
        b_in_g,
        g_back,
        b_back_g,
        gain2,
        shift2,
    )


EVENTS = [0, 1, 0, 2, 1, 2, 0, 1, 2, 2]


def solution(mesh):
    row = P("dp", "seq", None)
    in_specs = (row, P("dp", None), P("dp", None)) + (P(),) * 13 + (row,)
    block = P("dp", "seq")
    out_specs = (row, row, block, P(), P(), block, P(), P(), P(), block, P(), block, P(), P(), P())
    return jax.shard_map(local, mesh=mesh, in_specs=in_specs, out_specs=out_specs, check_vma=False)
```

profile of v0, /device:TPU:0, one launch (start us, length us, event | category | flops | bytes accessed | tf_op | source)
XLA Modules:
  0.0 150.2 jit_solution(15337154399786604382)
XLA Ops:
  0.7 1.4 collective-permute-start.1
  2.1 3.1 %collective-permute-start = (bf16[256,768]{1,0:T(8,128)(2,1)}, bf16[256,768]{1,0:T(8,128)(2,1)S(1)}, u32[]{:S(2)}, u32[]{:S(2)}) collective-permute-start(bf16[256,768]{1,0:T(8,128)(2,1)} %bitcast.11), channel_id=1, source_target_pairs={{0,1},{1,2},{2,3},{4,5},{5,6},{6,7},{8,9},{9,10},{10,11},{12,13},{... | collective-permute-start | bytes 1179656 | tf_op jit(solution)/shard_map/ppermute | solution.py:758
  5.2 0.7 constant_dynamic-update-slice_fusion.3
  5.9 0.7 constant_dynamic-update-slice_fusion.2
  6.6 0.7 constant_dynamic-update-slice_fusion.1
  7.2 0.7 constant_dynamic-update-slice_fusion.vec_ref
  7.9 0.7 pad_add_fusion.ids_ref
  8.6 1.0 copy-done.5
  9.7 3.2 %own_projections.1 = (bf16[256,2304]{1,0:T(8,128)(2,1)S(1)}, f32[2,128,384]{2,1,0:T(8,128)S(1)}, f32[2,128,384]{2,1,0:T(8,128)S(1)}) custom-call(s32[1]{0:T(128)} %bitcast.me_ref, s32[2,2,512]{2,1,0:T(2,128)S(1)} %pad_add_fusion.ids_ref, bf16[256,768]{1,0:T(8,128)(2,1)S(1)} %bitcast.12, f32[3072]{0:T(1024)S(1)} %constant_dynamic-update-slice_fusion.vec_ref, ...), custom_call_target="tpu_custom_call" | custom-call | flops 4000000 | bytes 40000 | tf_op jit(solution)/shard_map/own_projections/pallas_call | solution.py:765
  12.9 0.7 copy-done.18
  13.8 19.0 %layer_forward.1 = (bf16[2,256,2304]{2,1,0:T(8,128)(2,1)}, bf16[256,4992]{1,0:T(8,128)(2,1)}, bf16[256,768]{1,0:T(8,128)(2,1)S(1)}, bf16[256,3072]{1,0:T(8,128)(...) custom-call(s32[1]{0:T(128)} %bitcast.me_ref, ...), custom_call_target="tpu_custom_call" | custom-call | flops 16000000 | bytes 160000 | tf_op jit(solution)/shard_map/layer_forward/pallas_call | solution.py:781
  32.9 2.6 %collective-permute-start.4 = (bf16[256,4992]{1,0:T(8,128)(2,1)}, bf16[256,4992]{1,0:T(8,128)(2,1)}, u32[]{:S(2)}, u32[]{:S(2)}) collective-permute-start(bf16[256,4992]{1,0:T(8,128)(2,1)} %get-tuple-element.114.acts_ref.hid.acts.ctx), channel_id=1, source_target_pairs={{0,1},{1,0},{2,3},{3,2},{4,5},{5,4},{6,7},{7,6},{8,9},{9,8},{10,11... | collective-permute-start | bytes 7667720 | tf_op jit(solution)/shard_map/ppermute | solution.py:630
  35.5 1.4 copy-done.9
  36.9 9.7 %layer_backward.1 = (bf16[256,1920]{1,0:T(8,128)(2,1)S(1)}, bf16[256,1920]{1,0:T(8,128)(2,1)}, bf16[256,896]{1,0:T(8,128)(2,1)}, f32[256,768]{1,0:T(8,128)S(1)}, f32[7,768]{1,0:T(8,128)S(1)}) custom-call(s32[1]{0:T(128)} %bitcast.me_ref, bf16[256,768]{1,0:T(8,128)(2,1)S(1)} %get-tuple-element.109.feed_ref, bf16[256,3072]{1,0:T(8,128)(2,1)S(1)} %copy-done.9, ...), custom_call_target="tpu_custom_call" | custom-call | flops 8000000 | bytes 80000 | tf_op jit(solution)/shard_map/layer_backward/pallas_call | solution.py:829
  46.7 0.9 copy-done.16
  47.6 0.6 copy-done.23
  48.2 1.3 collective-permute-start.3
  49.5 0.9 copy-done.22
  50.4 3.3 %grad_w_back.1 = (bf16[384,768]{1,0:T(8,128)(2,1)S(1)}, bf16[384,768]{1,0:T(8,128)(2,1)S(1)}, bf16[384,768]{1,0:T(8,128)(2,1)S(1)}, bf16[384,768]{1,0:T(8,128)(2,1)S(1)}) custom-call(s32[1]{0:T(128)} %bitcast.6.d_ref, bf16[256,4992]{1,0:T(8,128)(2,1)S(1)} %copy-done, bf16[256,4992]{1,0:T(8,128)(2,1)} %collective-permute-done.4.hid_peer.feed_peer.acts_peer.ctx_peer, ...), custom_call_target="tpu_custom_call" | custom-call | flops 3000000 | bytes 30000 | tf_op jit(solution)/shard_map/grad_w_back/pallas_call | solution.py:867
  53.8 1.6 %collective-permute-start.9 = (bf16[384,768]{1,0:T(8,128)(2,1)S(1)}, bf16[384,768]{1,0:T(8,128)(2,1)S(1)}, u32[]{:S(2)}, u32[]{:S(2)}) collective-permute-start(bf16[384,768]{1,0:T(8,128)(2,1)S(1)} %get-tuple-element.137), channel_id=1, source_target_pairs={{0,4},{1,5},{2,6},{3,7},{4,0},{5,1},{6,2},{7,3},{8,12},{9,13},{10,... | collective-permute-start | bytes 1769480 | tf_op jit(solution)/shard_map/ppermute | solution.py:630
  55.4 1.6 %collective-permute-start.10 = (bf16[384,768]{1,0:T(8,128)(2,1)S(1)}, bf16[384,768]{1,0:T(8,128)(2,1)S(1)}, u32[]{:S(2)}, u32[]{:S(2)}) collective-permute-start(bf16[384,768]{1,0:T(8,128)(2,1)S(1)} %get-tuple-element.139), channel_id=1, source_target_pairs={{0,8},{1,9},{2,10},{3,11},{4,12},{5,13},{6,14},{7,15},{8,0},{9,1},... | collective-permute-start | bytes 1769480 | tf_op jit(solution)/shard_map/ppermute | solution.py:630
  57.0 2.5 %collective-permute-start.2 = (bf16[256,896]{1,0:T(8,128)(2,1)}, bf16[256,896]{1,0:T(8,128)(2,1)S(1)}, u32[]{:S(2)}, u32[]{:S(2)}) collective-permute-start(bf16[256,896]{1,0:T(8,128)(2,1)} %get-tuple-element.119.msg_own), channel_id=1, source_target_pairs={{0,1},{1,2},{2,3},{4,5},{5,6},{6,7},{8,9},{9,10},{10,11},{12,13},{... | collective-permute-start | bytes 1376264 | tf_op jit(solution)/shard_map/ppermute | solution.py:758
  59.5 3.1 %grad_w_in.1 = (bf16[384,768]{1,0:T(8,128)(2,1)S(1)}, bf16[384,768]{1,0:T(8,128)(2,1)S(1)}, bf16[384,768]{1,0:T(8,128)(2,1)S(1)}, bf16[384,768]{1,0:T(8,128)(2,1)S(1)}) custom-call(s32[1]{0:T(128)} %bitcast.6.d_ref, bf16[256,4992]{1,0:T(8,128)(2,1)S(1)} %copy-done, bf16[256,4992]{1,0:T(8,128)(2,1)} %collective-permute-done.4.hid_peer.feed_peer.acts_peer.ctx_peer, ...), custom_call_target="tpu_custom_call" | custom-call | flops 4000000 | bytes 40000 | tf_op jit(solution)/shard_map/grad_w_in/pallas_call | solution.py:883
  62.6 2.2 %collective-permute-start.6 = (bf16[384,768]{1,0:T(8,128)(2,1)S(1)}, bf16[384,768]{1,0:T(8,128)(2,1)S(1)}, u32[]{:S(2)}, u32[]{:S(2)}) collective-permute-start(bf16[384,768]{1,0:T(8,128)(2,1)S(1)} %get-tuple-element.131), channel_id=1, source_target_pairs={{0,2},{1,3},{2,0},{3,1},{4,6},{5,7},{6,4},{7,5},{8,10},{9,11},{10,... | collective-permute-start | bytes 1769480 | tf_op jit(solution)/shard_map/ppermute | solution.py:630
  64.8 0.5 collective-permute-start.7
  65.4 11.2 %attend_backward.1 = (bf16[256,2304]{1,0:T(8,128)(2,1)S(1)}, bf16[256,1152]{1,0:T(8,128)(2,1)S(1)}, bf16[160,1152]{1,0:T(8,128)(2,1)S(1)}, bf16[128,1152]{1,0:T(8,128)(2,1)S(1)}, f32[16,768]{1,0:T(8,128)S(1)}) custom-call(s32[1]{0:T(128)} %bitcast.me_ref, f32[2,128,384]{2,1,0:T(8,128)S(1)} %copy-done.15, f32[2,128,384]{2,1,0:T(8,128)S(1)} %copy-done.19, ...), custom_call_target="tpu_custom_call" | custom-call | flops 11000000 | bytes 110000 | tf_op jit(solution)/shard_map/attend_backward/pallas_call | solution.py:902
  76.6 0.3 add_back_0.1
  76.9 3.3 %collective-permute-start.14 = (bf16[160,1152]{1,0:T(8,128)(2,1)S(1)}, bf16[160,1152]{1,0:T(8,128)(2,1)S(1)}, u32[]{:S(2)}, u32[]{:S(2)}) collective-permute-start(bf16[160,1152]{1,0:T(8,128)(2,1)S(1)} %get-tuple-element.149), channel_id=1, source_target_pairs={{0,1},{1,0},{2,3},{3,2},{4,5},{5,4},{6,7},{7,6},{8,9},{9,8},{10,11... | collective-permute-start | bytes 1105928 | tf_op jit(solution)/shard_map/ppermute | solution.py:630
  80.4 1.6 %collective-permute-done.15.peer2 = bf16[128,1152]{1,0:T(8,128)(2,1)S(1)} collective-permute-done((bf16[128,1152]{1,0:T(8,128)(2,1)S(1)}, bf16[128,1152]{1,0:T(8,128)(2,1)S(1)}, u32[]{:S(2)}, u32[]{:S(2)}) %collective-permute-start.15) | collective-permute-done | bytes 294944 | tf_op jit(solution)/shard_map/ppermute | solution.py:630
  82.0 3.2 %grad_w_qkv_out.1 = (bf16[384,768]{1,0:T(8,128)(2,1)S(1)}, bf16[416,768]{1,0:T(8,128)(2,1)S(1)}, bf16[384,768]{1,0:T(8,128)(2,1)S(1)}, bf16[384,768]{1,0:T(8,128)(2,1)S(1)}, f32[16,768]{1,0:T(8,128)S(1)}) custom-call(s32[2]{0:T(128)S(1)} %pad_add_fusion.1.ids_ref, bf16[256,768]{1,0:T(8,128)(2,1)S(1)} %bitcast.14, bf16[256,768]{1,0:T(8,128)(2,1)S(1)} %copy-done.13, ...), custom_call_target="tpu_custom_call" | custom-call | flops 3000000 | bytes 30000 | tf_op jit(solution)/shard_map/grad_w_qkv_out/pallas_call | solution.py:926
  85.2 2.7 %collective-permute-start.19 = (bf16[416,768]{1,0:T(8,128)(2,1)S(1)}, bf16[416,768]{1,0:T(8,128)(2,1)S(1)}, u32[]{:S(2)}, u32[]{:S(2)}) collective-permute-start(bf16[416,768]{1,0:T(8,128)(2,1)S(1)} %get-tuple-element.163), channel_id=1, source_target_pairs={{0,2},{1,3},{2,0},{3,1},{4,6},{5,7},{6,4},{7,5},{8,10},{9,11},{10,... | collective-permute-start | bytes 1916936 | tf_op jit(solution)/shard_map/ppermute | solution.py:630
  87.9 0.5 collective-permute-start.11
  88.4 0.5 collective-permute-start.12
  88.9 0.3 add_in_0.1
  89.2 1.6 %collective-permute-start.20 = (bf16[384,768]{1,0:T(8,128)(2,1)S(1)}, bf16[384,768]{1,0:T(8,128)(2,1)S(1)}, u32[]{:S(2)}, u32[]{:S(2)}) collective-permute-start(bf16[384,768]{1,0:T(8,128)(2,1)S(1)} %get-tuple-element.167), channel_id=1, source_target_pairs={{0,4},{1,5},{2,6},{3,7},{4,0},{5,1},{6,2},{7,3},{8,12},{9,13},{10,... | collective-permute-start | bytes 1769480 | tf_op jit(solution)/shard_map/ppermute | solution.py:630
  90.7 0.5 collective-permute-start.8
  91.2 5.4 %collective-permute-done.11.got0 = bf16[192,768]{1,0:T(8,128)(2,1)S(1)} collective-permute-done((bf16[192,768]{1,0:T(8,128)(2,1)S(1)}, bf16[192,768]{1,0:T(8,128)(2,1)S(1)}, u32[]{:S(2)}, u32[]{:S(2)}) %collective-permute-start.11) | collective-permute-done | bytes 294944 | tf_op jit(solution)/shard_map/ppermute | solution.py:630
  96.7 0.4 collective-permute-start.16
  97.0 1.3 collective-permute-done.12.got1
  98.3 0.1 add_back_1.1
  98.4 0.5 collective-permute-start.13
  98.9 16.9 %collective-permute-done.8.got0 = bf16[192,768]{1,0:T(8,128)(2,1)S(1)} collective-permute-done((bf16[192,768]{1,0:T(8,128)(2,1)S(1)}, bf16[192,768]{1,0:T(8,128)(2,1)S(1)}, u32[]{:S(2)}, u32[]{:S(2)}) %collective-permute-start.8) | collective-permute-done | bytes 294944 | tf_op jit(solution)/shard_map/ppermute | solution.py:630
  115.8 0.1 add_in_1.1
  116.1 0.3 add_qkv_0.1
  116.4 0.6 collective-permute-start.21
  117.0 1.6 %collective-permute-start.18 = (bf16[192,768]{1,0:T(8,128)(2,1)S(1)}, bf16[192,768]{1,0:T(8,128)(2,1)S(1)}, u32[]{:S(2)}, u32[]{:S(2)}) collective-permute-start(bf16[192,768]{1,0:T(8,128)(2,1)S(1)} %get-tuple-element.161), channel_id=1, source_target_pairs={{0,8},{1,9},{2,10},{3,11},{4,12},{5,13},{6,14},{7,15},{8,0},{9,1},... | collective-permute-start | bytes 884744 | tf_op jit(solution)/shard_map/ppermute | solution.py:630
  118.6 0.4 collective-permute-start.22
  118.9 2.5 %collective-permute-start.17 = (bf16[96,768]{1,0:T(8,128)(2,1)S(1)}, bf16[96,768]{1,0:T(8,128)(2,1)S(1)}, u32[]{:S(2)}, u32[]{:S(2)}) collective-permute-start(bf16[96,768]{1,0:T(8,128)(2,1)S(1)} %get-tuple-element.160), channel_id=1, source_target_pairs={{0,16},{1,17},{2,18},{3,19},{4,20},{5,21},{6,22},{7,23},{8,24},{9,... | collective-permute-start | bytes 442376 | tf_op jit(solution)/shard_map/ppermute | solution.py:630
  121.5 6.2 %collective-permute-done.18.got = bf16[192,768]{1,0:T(8,128)(2,1)S(1)} collective-permute-done((bf16[192,768]{1,0:T(8,128)(2,1)S(1)}, bf16[192,768]{1,0:T(8,128)(2,1)S(1)}, u32[]{:S(2)}, u32[]{:S(2)}) %collective-permute-start.18) | collective-permute-done | bytes 294944 | tf_op jit(solution)/shard_map/ppermute | solution.py:630
  127.7 2.0 %collective-permute-start.24 = (bf16[96,768]{1,0:T(8,128)(2,1)S(1)}, bf16[96,768]{1,0:T(8,128)(2,1)S(1)}, u32[]{:S(2)}, u32[]{:S(2)}) collective-permute-start(bf16[96,768]{1,0:T(8,128)(2,1)S(1)} %get-tuple-element.183), channel_id=1, source_target_pairs={{0,16},{1,17},{2,18},{3,19},{4,20},{5,21},{6,22},{7,23},{8,24},{9,... | collective-permute-start | bytes 442376 | tf_op jit(solution)/shard_map/ppermute | solution.py:630
  129.7 0.1 add_qkv_1.1
  129.9 2.7 %collective-permute-start.23 = (bf16[224,768]{1,0:T(8,128)(2,1)S(1)}, bf16[224,768]{1,0:T(8,128)(2,1)S(1)}, u32[]{:S(2)}, u32[]{:S(2)}) collective-permute-start(bf16[224,768]{1,0:T(8,128)(2,1)S(1)} %get-tuple-element.181), channel_id=1, source_target_pairs={{0,8},{1,9},{2,10},{3,11},{4,12},{5,13},{6,14},{7,15},{8,0},{9,1},... | collective-permute-start | bytes 1032200 | tf_op jit(solution)/shard_map/ppermute | solution.py:630
  132.6 1.1 fusion
  133.7 0.3 add_back_3.1
  134.0 1.4 collective-permute-done.24.got
  135.4 0.7 add_in_3.1
  136.1 3.2 %collective-permute-done.23.got = bf16[224,768]{1,0:T(8,128)(2,1)S(1)} collective-permute-done((bf16[224,768]{1,0:T(8,128)(2,1)S(1)}, bf16[224,768]{1,0:T(8,128)(2,1)S(1)}, u32[]{:S(2)}, u32[]{:S(2)}) %collective-permute-start.23) | collective-permute-done | bytes 344096 | tf_op jit(solution)/shard_map/ppermute | solution.py:630
  139.4 2.6 %collective-permute-start.25 = (bf16[128,768]{1,0:T(8,128)(2,1)S(1)}, bf16[128,768]{1,0:T(8,128)(2,1)S(1)}, u32[]{:S(2)}, u32[]{:S(2)}) collective-permute-start(bf16[128,768]{1,0:T(8,128)(2,1)S(1)} %get-tuple-element.190), channel_id=1, source_target_pairs={{0,16},{1,17},{2,18},{3,19},{4,20},{5,21},{6,22},{7,23},{8,24},{9,... | collective-permute-start | bytes 589832 | tf_op jit(solution)/shard_map/ppermute | solution.py:630
  141.9 0.8 add_convert_fusion
  142.8 0.9 copy.32
  143.7 4.5 %collective-permute-done.25.got = bf16[128,768]{1,0:T(8,128)(2,1)S(1)} collective-permute-done((bf16[128,768]{1,0:T(8,128)(2,1)S(1)}, bf16[128,768]{1,0:T(8,128)(2,1)S(1)}, u32[]{:S(2)}, u32[]{:S(2)}) %collective-permute-start.25) | collective-permute-done | bytes 196640 | tf_op jit(solution)/shard_map/ppermute | solution.py:630
  148.1 0.8 add_qkv_3.1
  148.9 0.7 slice_reduce_fusion
  149.6 0.6 reshape.55
  (87 shorter events, 0.6 us)
Async XLA Ops:
  0.6 13.1 %copy-start.1 = (bf16[768,768]{1,0:T(8,128)(2,1)S(1)}, bf16[768,768]{1,0:T(8,128)(2,1)}, u32[]{:S(2)}) copy-start(bf16[768,768]{1,0:T(8,128)(2,1)} %wout_hbm.3) | copy-start | bytes 3538948
  0.7 13.0 %collective-permute-start.1 = (bf16[256,768]{1,0:T(8,128)(2,1)}, bf16[256,768]{1,0:T(8,128)(2,1)S(1)}, u32[]{:S(2)}, u32[]{:S(2)}) collective-permute-start(bf16[256,768]{1,0:T(8,128)(2,1)} %bitcast.10), channel_id=1, source_target_pairs={{1,0},{2,1},{3,2},{5,4},{6,5},{7,6},{9,8},{10,9},{11,10},{13,12},{... | collective-permute-start | bytes 1179656 | tf_op jit(solution)/shard_map/ppermute | solution.py:758
  2.1 11.6 %collective-permute-start = (bf16[256,768]{1,0:T(8,128)(2,1)}, bf16[256,768]{1,0:T(8,128)(2,1)S(1)}, u32[]{:S(2)}, u32[]{:S(2)}) collective-permute-start(bf16[256,768]{1,0:T(8,128)(2,1)} %bitcast.11), channel_id=1, source_target_pairs={{0,1},{1,2},{2,3},{4,5},{5,6},{6,7},{8,9},{9,10},{10,11},{12,13},{... | collective-permute-start | bytes 1179656 | tf_op jit(solution)/shard_map/ppermute | solution.py:758
  8.6 1.0 copy-start.5
  9.6 4.0 %copy-start.29 = (f32[768]{0:T(1024)S(1)}, f32[768]{0:T(1024)}, u32[]{:S(2)}) copy-start(f32[768]{0:T(1024)} %param.32) | copy-start | bytes 9220
  9.6 4.0 %copy-start.30 = (f32[768]{0:T(1024)S(1)}, f32[768]{0:T(1024)}, u32[]{:S(2)}) copy-start(f32[768]{0:T(1024)} %param.31) | copy-start | bytes 9220
  9.6 4.0 %copy-start.31 = (f32[768]{0:T(1024)S(1)}, f32[768]{0:T(1024)}, u32[]{:S(2)}) copy-start(f32[768]{0:T(1024)} %param.30) | copy-start | bytes 9220
  9.6 4.0 %copy-start.32 = (f32[768]{0:T(1024)S(1)}, f32[768]{0:T(1024)}, u32[]{:S(2)}) copy-start(f32[768]{0:T(1024)} %param.26) | copy-start | bytes 9220
  9.7 4.1 %copy-start.6 = (bf16[2,128,768]{2,1,0:T(8,128)(2,1)S(1)}, bf16[2,128,768]{2,1,0:T(8,128)(2,1)}, u32[]{:S(2)}) copy-start(bf16[2,128,768]{2,1,0:T(8,128)(2,1)} %param.17) | copy-start | bytes 1179652
  9.7 4.1 %copy-start.20 = (bf16[2,128,768]{2,1,0:T(8,128)(2,1)S(1)}, bf16[2,128,768]{2,1,0:T(8,128)(2,1)}, u32[]{:S(2)}) copy-start(bf16[2,128,768]{2,1,0:T(8,128)(2,1)} %param.33) | copy-start | bytes 1179652
  9.7 4.1 %copy-start.25 = (f32[3072]{0:T(1024)S(1)}, f32[3072]{0:T(1024)}, u32[]{:S(2)}) copy-start(f32[3072]{0:T(1024)} %b_in_ref.1) | copy-start | bytes 36868
  12.9 0.7 copy-start.18
  13.6 19.2 %copy-start.3 = (bf16[256,2304]{1,0:T(8,128)(2,1)}, bf16[256,2304]{1,0:T(8,128)(2,1)S(1)}, u32[]{:S(2)}) copy-start(bf16[256,2304]{1,0:T(8,128)(2,1)S(1)} %get-tuple-element.106.own_ref) | copy-start | bytes 3538948
  13.7 19.2 %copy-start.14 = (f32[2,128,384]{2,1,0:T(8,128)}, f32[2,128,384]{2,1,0:T(8,128)S(1)}, u32[]{:S(2)}) copy-start(f32[2,128,384]{2,1,0:T(8,128)S(1)} %get-tuple-element.107.mask_ref) | copy-start | bytes 1179652
  13.7 19.2 %copy-start.10 = (bf16[256,768]{1,0:T(8,128)(2,1)}, bf16[256,768]{1,0:T(8,128)(2,1)S(1)}, u32[]{:S(2)}) copy-start(bf16[256,768]{1,0:T(8,128)(2,1)S(1)} %collective-permute-done.1.tok_next) | copy-start | bytes 1179652
  13.7 19.1 %copy-start.12 = (bf16[256,768]{1,0:T(8,128)(2,1)}, bf16[256,768]{1,0:T(8,128)(2,1)S(1)}, u32[]{:S(2)}) copy-start(bf16[256,768]{1,0:T(8,128)(2,1)S(1)} %collective-permute-done.tok_prev) | copy-start | bytes 1179652
  13.8 21.7 %copy-start.2 = (bf16[768,768]{1,0:T(8,128)(2,1)S(1)}, bf16[768,768]{1,0:T(8,128)(2,1)}, u32[]{:S(2)}) copy-start(bf16[768,768]{1,0:T(8,128)(2,1)} %wout_hbm.3) | copy-start | bytes 3538948
  32.9 13.8 %copy-start.21 = (bf16[256,384]{1,0:T(8,128)(2,1)}, bf16[256,384]{1,0:T(8,128)(2,1)S(1)}, u32[]{:S(2)}) copy-start(bf16[256,384]{1,0:T(8,128)(2,1)S(1)} %get-tuple-element.120.feed) | copy-start | bytes 589828
  32.9 13.8 %copy-start.26 = (f32[3,768]{1,0:T(4,128)}, f32[3,768]{1,0:T(4,128)S(1)}, u32[]{:S(2)}) copy-start(f32[3,768]{1,0:T(4,128)S(1)} %get-tuple-element.127.small1_ref) | copy-start | bytes 27652
  32.9 16.6 %collective-permute-start.4 = (bf16[256,4992]{1,0:T(8,128)(2,1)}, bf16[256,4992]{1,0:T(8,128)(2,1)}, u32[]{:S(2)}, u32[]{:S(2)}) collective-permute-start(bf16[256,4992]{1,0:T(8,128)(2,1)} %get-tuple-element.114.acts_ref.hid.acts.ctx), channel_id=1, source_target_pairs={{0,1},{1,0},{2,3},{3,2},{4,5},{5,4},{6,7},{7,6},{8,9},{9,8},{10,11... | collective-permute-start | bytes 7667720 | tf_op jit(solution)/shard_map/ppermute | solution.py:630
  35.5 1.4 copy-start.9
  36.9 12.6 %copy-start = (bf16[256,4992]{1,0:T(8,128)(2,1)S(1)}, bf16[256,4992]{1,0:T(8,128)(2,1)}, u32[]{:S(2)}) copy-start(bf16[256,4992]{1,0:T(8,128)(2,1)} %get-tuple-element.114.acts_ref.hid.acts.ctx) | copy-start | bytes 7667716
  46.7 0.9 copy-start.16
  47.6 0.6 copy-start.23
  48.2 11.3 %collective-permute-start.5 = (bf16[256,1920]{1,0:T(8,128)(2,1)}, bf16[256,1920]{1,0:T(8,128)(2,1)}, u32[]{:S(2)}, u32[]{:S(2)}) collective-permute-start(bf16[256,1920]{1,0:T(8,128)(2,1)} %get-tuple-element.123), channel_id=1, source_target_pairs={{0,1},{1,0},{2,3},{3,2},{4,5},{5,4},{6,7},{7,6},{8,9},{9,8},{10,11... | collective-permute-start | bytes 2949128 | tf_op jit(solution)/shard_map/ppermute | solution.py:630
  48.2 16.6 %collective-permute-start.3 = (bf16[256,896]{1,0:T(8,128)(2,1)}, bf16[256,896]{1,0:T(8,128)(2,1)}, u32[]{:S(2)}, u32[]{:S(2)}) collective-permute-start(bf16[256,896]{1,0:T(8,128)(2,1)} %get-tuple-element.119.msg_own), channel_id=1, source_target_pairs={{1,0},{2,1},{3,2},{5,4},{6,5},{7,6},{9,8},{10,9},{11,10},{13,12},{... | collective-permute-start | bytes 1376264 | tf_op jit(solution)/shard_map/ppermute | solution.py:758
  49.5 0.9 copy-start.22
  53.8 22.8 %collective-permute-start.9 = (bf16[384,768]{1,0:T(8,128)(2,1)S(1)}, bf16[384,768]{1,0:T(8,128)(2,1)S(1)}, u32[]{:S(2)}, u32[]{:S(2)}) collective-permute-start(bf16[384,768]{1,0:T(8,128)(2,1)S(1)} %get-tuple-element.137), channel_id=1, source_target_pairs={{0,4},{1,5},{2,6},{3,7},{4,0},{5,1},{6,2},{7,3},{8,12},{9,13},{10,... | collective-permute-start | bytes 1769480 | tf_op jit(solution)/shard_map/ppermute | solution.py:630
  55.4 21.3 %collective-permute-start.10 = (bf16[384,768]{1,0:T(8,128)(2,1)S(1)}, bf16[384,768]{1,0:T(8,128)(2,1)S(1)}, u32[]{:S(2)}, u32[]{:S(2)}) collective-permute-start(bf16[384,768]{1,0:T(8,128)(2,1)S(1)} %get-tuple-element.139), channel_id=1, source_target_pairs={{0,8},{1,9},{2,10},{3,11},{4,12},{5,13},{6,14},{7,15},{8,0},{9,1},... | collective-permute-start | bytes 1769480 | tf_op jit(solution)/shard_map/ppermute | solution.py:630
  57.0 8.4 %collective-permute-start.2 = (bf16[256,896]{1,0:T(8,128)(2,1)}, bf16[256,896]{1,0:T(8,128)(2,1)S(1)}, u32[]{:S(2)}, u32[]{:S(2)}) collective-permute-start(bf16[256,896]{1,0:T(8,128)(2,1)} %get-tuple-element.119.msg_own), channel_id=1, source_target_pairs={{0,1},{1,2},{2,3},{4,5},{5,6},{6,7},{8,9},{9,10},{10,11},{12,13},{... | collective-permute-start | bytes 1376264 | tf_op jit(solution)/shard_map/ppermute | solution.py:758
  59.5 5.9 %copy-start.4 = (bf16[256,2304]{1,0:T(8,128)(2,1)S(1)}, bf16[256,2304]{1,0:T(8,128)(2,1)}, u32[]{:S(2)}) copy-start(bf16[256,2304]{1,0:T(8,128)(2,1)} %copy-done.3) | copy-start | bytes 3538948
  59.5 5.9 %copy-start.8 = (bf16[2,256,2304]{2,1,0:T(8,128)(2,1)S(1)}, bf16[2,256,2304]{2,1,0:T(8,128)(2,1)}, u32[]{:S(2)}) copy-start(bf16[2,256,2304]{2,1,0:T(8,128)(2,1)} %get-tuple-element.118.near_ref) | copy-start | bytes 7077892
  59.5 5.9 %copy-start.15 = (f32[2,128,384]{2,1,0:T(8,128)S(1)}, f32[2,128,384]{2,1,0:T(8,128)}, u32[]{:S(2)}) copy-start(f32[2,128,384]{2,1,0:T(8,128)} %copy-done.14) | copy-start | bytes 1179652
  59.5 5.9 %copy-start.19 = (f32[2,128,384]{2,1,0:T(8,128)S(1)}, f32[2,128,384]{2,1,0:T(8,128)}, u32[]{:S(2)}) copy-start(f32[2,128,384]{2,1,0:T(8,128)} %copy-done.18) | copy-start | bytes 1179652
  59.5 5.9 %copy-start.24 = (f32[7,768]{1,0:T(8,128)S(1)}, f32[7,768]{1,0:T(8,128)}, u32[]{:S(2)}) copy-start(f32[7,768]{1,0:T(8,128)} %copy-done.23) | copy-start | bytes 64516
  59.5 5.9 %copy-start.27 = (f32[3,768]{1,0:T(4,128)S(1)}, f32[3,768]{1,0:T(4,128)}, u32[]{:S(2)}) copy-start(f32[3,768]{1,0:T(4,128)} %copy-done.26) | copy-start | bytes 27652
  62.6 26.2 %collective-permute-start.6 = (bf16[384,768]{1,0:T(8,128)(2,1)S(1)}, bf16[384,768]{1,0:T(8,128)(2,1)S(1)}, u32[]{:S(2)}, u32[]{:S(2)}) collective-permute-start(bf16[384,768]{1,0:T(8,128)(2,1)S(1)} %get-tuple-element.131), channel_id=1, source_target_pairs={{0,2},{1,3},{2,0},{3,1},{4,6},{5,7},{6,4},{7,5},{8,10},{9,11},{10,... | collective-permute-start | bytes 1769480 | tf_op jit(solution)/shard_map/ppermute | solution.py:630
  64.8 24.0 %collective-permute-start.7 = (bf16[384,768]{1,0:T(8,128)(2,1)S(1)}, bf16[384,768]{1,0:T(8,128)(2,1)S(1)}, u32[]{:S(2)}, u32[]{:S(2)}) collective-permute-start(bf16[384,768]{1,0:T(8,128)(2,1)S(1)} %get-tuple-element.133), channel_id=1, source_target_pairs={{0,4},{1,5},{2,6},{3,7},{4,0},{5,1},{6,2},{7,3},{8,12},{9,13},{10,... | collective-permute-start | bytes 1769480 | tf_op jit(solution)/shard_map/ppermute | solution.py:630
  76.6 5.4 %copy-start.7 = (bf16[2,128,768]{2,1,0:T(8,128)(2,1)S(1)}, bf16[2,128,768]{2,1,0:T(8,128)(2,1)}, u32[]{:S(2)}) copy-start(bf16[2,128,768]{2,1,0:T(8,128)(2,1)} %param.17) | copy-start | bytes 1179652
  76.6 5.4 %copy-start.11 = (bf16[256,768]{1,0:T(8,128)(2,1)S(1)}, bf16[256,768]{1,0:T(8,128)(2,1)}, u32[]{:S(2)}) copy-start(bf16[256,768]{1,0:T(8,128)(2,1)} %copy-done.10) | copy-start | bytes 1179652
  76.6 5.4 %copy-start.13 = (bf16[256,768]{1,0:T(8,128)(2,1)S(1)}, bf16[256,768]{1,0:T(8,128)(2,1)}, u32[]{:S(2)}) copy-start(bf16[256,768]{1,0:T(8,128)(2,1)} %copy-done.12) | copy-start | bytes 1179652
  76.9 5.0 %collective-permute-start.14 = (bf16[160,1152]{1,0:T(8,128)(2,1)S(1)}, bf16[160,1152]{1,0:T(8,128)(2,1)S(1)}, u32[]{:S(2)}, u32[]{:S(2)}) collective-permute-start(bf16[160,1152]{1,0:T(8,128)(2,1)S(1)} %get-tuple-element.149), channel_id=1, source_target_pairs={{0,1},{1,0},{2,3},{3,2},{4,5},{5,4},{6,7},{7,6},{8,9},{9,8},{10,11... | collective-permute-start | bytes 1105928 | tf_op jit(solution)/shard_map/ppermute | solution.py:630
  80.2 1.7 %collective-permute-start.15 = (bf16[128,1152]{1,0:T(8,128)(2,1)S(1)}, bf16[128,1152]{1,0:T(8,128)(2,1)S(1)}, u32[]{:S(2)}, u32[]{:S(2)}) collective-permute-start(bf16[128,1152]{1,0:T(8,128)(2,1)S(1)} %get-tuple-element.150), channel_id=1, source_target_pairs={{0,1},{1,0},{2,3},{3,2},{4,5},{5,4},{6,7},{7,6},{8,9},{9,8},{10,11... | collective-permute-start | bytes 884744 | tf_op jit(solution)/shard_map/ppermute | solution.py:630
  85.2 30.9 %collective-permute-start.19 = (bf16[416,768]{1,0:T(8,128)(2,1)S(1)}, bf16[416,768]{1,0:T(8,128)(2,1)S(1)}, u32[]{:S(2)}, u32[]{:S(2)}) collective-permute-start(bf16[416,768]{1,0:T(8,128)(2,1)S(1)} %get-tuple-element.163), channel_id=1, source_target_pairs={{0,2},{1,3},{2,0},{3,1},{4,6},{5,7},{6,4},{7,5},{8,10},{9,11},{10,... | collective-permute-start | bytes 1916936 | tf_op jit(solution)/shard_map/ppermute | solution.py:630
  87.9 8.8 %collective-permute-start.11 = (bf16[192,768]{1,0:T(8,128)(2,1)S(1)}, bf16[192,768]{1,0:T(8,128)(2,1)S(1)}, u32[]{:S(2)}, u32[]{:S(2)}) collective-permute-start(bf16[192,768]{1,0:T(8,128)(2,1)S(1)} %get-tuple-element.142), channel_id=1, source_target_pairs={{0,8},{1,9},{2,10},{3,11},{4,12},{5,13},{6,14},{7,15},{8,0},{9,1},... | collective-permute-start | bytes 884744 | tf_op jit(solution)/shard_map/ppermute | solution.py:630
  88.4 9.9 %collective-permute-start.12 = (bf16[192,768]{1,0:T(8,128)(2,1)S(1)}, bf16[192,768]{1,0:T(8,128)(2,1)S(1)}, u32[]{:S(2)}, u32[]{:S(2)}) collective-permute-start(bf16[192,768]{1,0:T(8,128)(2,1)S(1)} %get-tuple-element.144), channel_id=1, source_target_pairs={{0,4},{1,5},{2,6},{3,7},{4,0},{5,1},{6,2},{7,3},{8,12},{9,13},{10,... | collective-permute-start | bytes 884744 | tf_op jit(solution)/shard_map/ppermute | solution.py:630
  89.2 26.9 %collective-permute-start.20 = (bf16[384,768]{1,0:T(8,128)(2,1)S(1)}, bf16[384,768]{1,0:T(8,128)(2,1)S(1)}, u32[]{:S(2)}, u32[]{:S(2)}) collective-permute-start(bf16[384,768]{1,0:T(8,128)(2,1)S(1)} %get-tuple-element.167), channel_id=1, source_target_pairs={{0,4},{1,5},{2,6},{3,7},{4,0},{5,1},{6,2},{7,3},{8,12},{9,13},{10,... | collective-permute-start | bytes 1769480 | tf_op jit(solution)/shard_map/ppermute | solution.py:630
  90.7 25.1 %collective-permute-start.8 = (bf16[192,768]{1,0:T(8,128)(2,1)S(1)}, bf16[192,768]{1,0:T(8,128)(2,1)S(1)}, u32[]{:S(2)}, u32[]{:S(2)}) collective-permute-start(bf16[192,768]{1,0:T(8,128)(2,1)S(1)} %get-tuple-element.134), channel_id=1, source_target_pairs={{0,4},{1,5},{2,6},{3,7},{4,0},{5,1},{6,2},{7,3},{8,12},{9,13},{10,... | collective-permute-start | bytes 884744 | tf_op jit(solution)/shard_map/ppermute | solution.py:630
  96.7 19.1 %collective-permute-start.16 = (bf16[192,768]{1,0:T(8,128)(2,1)S(1)}, bf16[192,768]{1,0:T(8,128)(2,1)S(1)}, u32[]{:S(2)}, u32[]{:S(2)}) collective-permute-start(bf16[192,768]{1,0:T(8,128)(2,1)S(1)} %get-tuple-element.157), channel_id=1, source_target_pairs={{0,2},{1,3},{2,0},{3,1},{4,6},{5,7},{6,4},{7,5},{8,10},{9,11},{10,... | collective-permute-start | bytes 884744 | tf_op jit(solution)/shard_map/ppermute | solution.py:630
  98.4 17.5 %collective-permute-start.13 = (bf16[192,768]{1,0:T(8,128)(2,1)S(1)}, bf16[192,768]{1,0:T(8,128)(2,1)S(1)}, u32[]{:S(2)}, u32[]{:S(2)}) collective-permute-start(bf16[192,768]{1,0:T(8,128)(2,1)S(1)} %get-tuple-element.147), channel_id=1, source_target_pairs={{0,2},{1,3},{2,0},{3,1},{4,6},{5,7},{6,4},{7,5},{8,10},{9,11},{10,... | collective-permute-start | bytes 884744 | tf_op jit(solution)/shard_map/ppermute | solution.py:630
  116.0 16.7 %copy-start.28 = (bf16[768,2304]{1,0:T(8,128)(2,1)S(1)}, bf16[768,2304]{1,0:T(8,128)(2,1)}, u32[]{:S(2)}) copy-start(bf16[768,2304]{1,0:T(8,128)(2,1)} %wqkv.3) | copy-start | bytes 10616836
  116.4 13.3 %collective-permute-start.21 = (bf16[224,768]{1,0:T(8,128)(2,1)S(1)}, bf16[224,768]{1,0:T(8,128)(2,1)S(1)}, u32[]{:S(2)}, u32[]{:S(2)}) collective-permute-start(bf16[224,768]{1,0:T(8,128)(2,1)S(1)} %get-tuple-element.171), channel_id=1, source_target_pairs={{0,4},{1,5},{2,6},{3,7},{4,0},{5,1},{6,2},{7,3},{8,12},{9,13},{10,... | collective-permute-start | bytes 1032200 | tf_op jit(solution)/shard_map/ppermute | solution.py:630
  117.0 10.7 %collective-permute-start.18 = (bf16[192,768]{1,0:T(8,128)(2,1)S(1)}, bf16[192,768]{1,0:T(8,128)(2,1)S(1)}, u32[]{:S(2)}, u32[]{:S(2)}) collective-permute-start(bf16[192,768]{1,0:T(8,128)(2,1)S(1)} %get-tuple-element.161), channel_id=1, source_target_pairs={{0,8},{1,9},{2,10},{3,11},{4,12},{5,13},{6,14},{7,15},{8,0},{9,1},... | collective-permute-start | bytes 884744 | tf_op jit(solution)/shard_map/ppermute | solution.py:630
  118.6 11.2 %collective-permute-start.22 = (bf16[192,768]{1,0:T(8,128)(2,1)S(1)}, bf16[192,768]{1,0:T(8,128)(2,1)S(1)}, u32[]{:S(2)}, u32[]{:S(2)}) collective-permute-start(bf16[192,768]{1,0:T(8,128)(2,1)S(1)} %get-tuple-element.177), channel_id=1, source_target_pairs={{0,2},{1,3},{2,0},{3,1},{4,6},{5,7},{6,4},{7,5},{8,10},{9,11},{10,... | collective-permute-start | bytes 884744 | tf_op jit(solution)/shard_map/ppermute | solution.py:630
  118.9 14.8 %collective-permute-start.17 = (bf16[96,768]{1,0:T(8,128)(2,1)S(1)}, bf16[96,768]{1,0:T(8,128)(2,1)S(1)}, u32[]{:S(2)}, u32[]{:S(2)}) collective-permute-start(bf16[96,768]{1,0:T(8,128)(2,1)S(1)} %get-tuple-element.160), channel_id=1, source_target_pairs={{0,16},{1,17},{2,18},{3,19},{4,20},{5,21},{6,22},{7,23},{8,24},{9,... | collective-permute-start | bytes 442376 | tf_op jit(solution)/shard_map/ppermute | solution.py:630
  127.7 7.7 %collective-permute-start.24 = (bf16[96,768]{1,0:T(8,128)(2,1)S(1)}, bf16[96,768]{1,0:T(8,128)(2,1)S(1)}, u32[]{:S(2)}, u32[]{:S(2)}) collective-permute-start(bf16[96,768]{1,0:T(8,128)(2,1)S(1)} %get-tuple-element.183), channel_id=1, source_target_pairs={{0,16},{1,17},{2,18},{3,19},{4,20},{5,21},{6,22},{7,23},{8,24},{9,... | collective-permute-start | bytes 442376 | tf_op jit(solution)/shard_map/ppermute | solution.py:630
  129.9 9.4 %collective-permute-start.23 = (bf16[224,768]{1,0:T(8,128)(2,1)S(1)}, bf16[224,768]{1,0:T(8,128)(2,1)S(1)}, u32[]{:S(2)}, u32[]{:S(2)}) collective-permute-start(bf16[224,768]{1,0:T(8,128)(2,1)S(1)} %get-tuple-element.181), channel_id=1, source_target_pairs={{0,8},{1,9},{2,10},{3,11},{4,12},{5,13},{6,14},{7,15},{8,0},{9,1},... | collective-permute-start | bytes 1032200 | tf_op jit(solution)/shard_map/ppermute | solution.py:630
  132.6 9.3 %copy-start.17 = (f32[256,768]{1,0:T(8,128)S(1)}, f32[256,768]{1,0:T(8,128)}, u32[]{:S(2)}) copy-start(f32[256,768]{1,0:T(8,128)} %copy-done.16) | copy-start | bytes 2359300
  139.4 8.7 %collective-permute-start.25 = (bf16[128,768]{1,0:T(8,128)(2,1)S(1)}, bf16[128,768]{1,0:T(8,128)(2,1)S(1)}, u32[]{:S(2)}, u32[]{:S(2)}) collective-permute-start(bf16[128,768]{1,0:T(8,128)(2,1)S(1)} %get-tuple-element.190), channel_id=1, source_target_pairs={{0,16},{1,17},{2,18},{3,19},{4,20},{5,21},{6,22},{7,23},{8,24},{9,... | collective-permute-start | bytes 589832 | tf_op jit(solution)/shard_map/ppermute | solution.py:630
where the time goes:
time: 151 us; the launch traced here: 150 us
  Pallas kernels  56 us (37%)
  waiting for transfers between devices  40.4 us (27%)
  starting transfers between devices  39.1 us (26%)
  local copies, waits for them, and re-layouts  10.6 us (7%)
  other arithmetic  1.63 us (1%)
    ppermute x22, waiting for transfers between devices, flip(): return lax.ppermute(value, BOTH, [(i, i ^ 1 << bit) for i in range(count)])  40.4 us
    ppermute x22, starting transfers between devices, flip(): return lax.ppermute(value, BOTH, [(i, i ^ 1 << bit) for i in range(count)])  30.8 us
    pallas_call x1, Pallas kernels, local(): pl.pallas_call(functools.partial(forward_kernel, groups), name='layer_for...  19 us
    pallas_call x1, Pallas kernels, local(): pl.pallas_call(functools.partial(attend_back_kernel, groups), name='atten...  11.2 us
    pallas_call x1, Pallas kernels, local(): pl.pallas_call(functools.partial(backward_kernel, groups), name='layer_ba...  9.72 us
    unnamed x70, local copies, waits for them, and re-layouts  8.64 us
    ppermute x4, starting transfers between devices, around(): return (lax.ppermute(value, 'seq', up), lax.ppermute(value, 'seq', down))  8.25 us
    pallas_call x1, Pallas kernels, local(): pl.pallas_call(functools.partial(back_kernel, dp), name='grad_w_back', co...  3.34 us
  transfers between devices with their start and end apart: 26, of which 8 were waited for; matrix products, arithmetic and copies ran while one was open for 4% of the time, Pallas kernels for 24%

commit v1 on v0

--- a/solution.py
+++ b/solution.py
@@ -80,16 +80,22 @@
 
 
 def own_kernel(
-    groups, me_ref, ids_ref, tok_ref, vec_ref, wqkv, qkv_ref, mask_ref, mask_t_ref
+    groups, me_ref, ids_ref, tok_ref, vec_ref, wqkv_hbm, qkv_ref, mask_ref, mask_t_ref, wqkv, sems
 ):
     me = me_ref[0]
     rows, width = tok_ref.shape
     loc = rows // 2
+    copies = []
+    for part in range(3):
+        cols = pl.ds(part * width, width)
+        copies.append(pltpu.make_async_copy(wqkv_hbm.at[:, cols], wqkv.at[:, cols], sems.at[part]))
+        copies[-1].start()
     for row in range(2):
         mask_ref[row], mask_t_ref[row] = mask_of(me, groups, ids_ref, row, loc)
     vec = vec_ref[...].reshape(1, -1)
     biases = (vec[:, :width], 0.0, vec[:, width : 2 * width])
     for part in range(3):
+        copies[part].wait()
         cols = slice(part * width, (part + 1) * width)
         qkv_ref[:, cols] = (dot(tok_ref[...], wqkv[:, cols]) + biases[part]).astype(BF)
 
@@ -173,7 +179,7 @@
         return tuple(result)
 
     zero = jnp.zeros((loc, 128), F32)
-    totals = lax.fori_loop(0, HEADS // 2, attend, (zero, zero))
+    totals = lax.fori_loop(0, HEADS // 2, attend, (zero, zero), unroll=3)
     lse_ref[:loc, :] = totals[0]
     lse_ref[loc:, :] = totals[1]
     context = ctx_ref[...]
@@ -236,48 +242,30 @@
     acts_ref,
     lse_ref,
     vec_ref,
-    wback_hbm,
-    win_hbm,
-    wout_hbm,
+    wout,
+    win,
+    wback,
     keep_ref,
     send_ref,
     msg_ref,
     gone_ref,
     small_ref,
-    wback,
-    win,
-    wout,
-    sems,
 ):
     me = me_ref[0]
     rows, width = feed_ref.shape
     ff = win.shape[1]
     block = ff // groups
     spans = [pl.ds(pl.multiple_of((i ^ me) * block, block), block) for i in range(groups)]
-    copies = []
-    for i, span in enumerate(spans):
-        copies += [
-            pltpu.make_async_copy(wback_hbm.at[span], wback.at[span], sems.at[2 * i]),
-            pltpu.make_async_copy(win_hbm.at[:, span], win.at[:, span], sems.at[2 * i + 1]),
-        ]
-    copies += [
-        pltpu.make_async_copy(wout_hbm, wout, sems.at[2 * groups]),
-    ]
-    for copy in copies:
-        copy.start()
     feed_grad = feed_ref[...]
     first_grad = gtwo_ref[...]
     for i, span in enumerate(spans):
         s = i ^ me
-        copies[2 * i].wait()
-        copies[2 * i + 1].wait()
         hidden_grad = dot(feed_grad, wback[span, :], 1, 1)
         before_grad = (hidden_grad * slope_ref[:, span].astype(F32)).astype(BF)
         small_ref[pl.ds(s, 1), :] = col_sum(before_grad.astype(F32))
         target = send_ref if i % 2 else keep_ref
         target[:, (i // 2) * block : (i // 2 + 1) * block] = before_grad
         first_grad = first_grad + dot(before_grad, win[:, span], 1, 1)
-    copies[-1].wait()
     normed = normed_ref[...]
     grad_one = norm_pull(first_grad, normed, inv_ref[...], vec_ref[3 * width :].reshape(1, -1))
     gone_ref[...] = grad_one
@@ -402,7 +390,7 @@
             all_ref[at, spans[2]] = value_grad.astype(BF)
         return carry
 
-    lax.fori_loop(0, HEADS // 2, heads, 0)
+    lax.fori_loop(0, HEADS // 2, heads, 0, unroll=3)
     value_at = 2 * width
     sums_ref[...] = jnp.concatenate(
         [
@@ -762,7 +750,7 @@
     vec1 = jnp.concatenate([b_query, b_value, b_out, ln1_gain])
     vec2 = jnp.concatenate([ln1_bias, b_back, ln2_gain, ln2_bias])
     ids = jnp.stack([segment_ids, padding])
-    own_qkv, mask, mask_t = pl.pallas_call(
+    own_qkv, mask, mask_t, wqkv = pl.pallas_call(
         functools.partial(own_kernel, groups),
         name="own_projections",
         cost_estimate=cost(4),
@@ -770,14 +758,16 @@
             shape_of(rows, 3 * width),
             shape_of(seqs, loc, 3 * loc, dtype=F32),
             shape_of(seqs, loc, 3 * loc, dtype=F32),
+            shape_of(*w_qkv.shape),
         ),
-        in_specs=[SMEM] + [VMEM] * 4,
-        out_specs=(VMEM,) * 3,
-        compiler_params=params(50),
+        in_specs=[SMEM] + [VMEM] * 3 + [HBM],
+        out_specs=(VMEM,) * 4,
+        scratch_shapes=[pltpu.SemaphoreType.DMA((3,))],
+        compiler_params=params(48),
     )(me, ids, flat, vec1, w_qkv)
     extra = width // groups * 2
     acts_width = ff + 2 * width + extra
-    near_qkv, acts, feed_grad, slope, lse, normed, inverse, grad_two, result, feed_keep, small1 = (
+    near_qkv, acts, feed_grad, slope, lse, normed, inverse, grad_two, result, feed_keep, small1, *weights = (
         pl.pallas_call(
             functools.partial(forward_kernel, groups),
             name="layer_forward",
@@ -794,18 +784,16 @@
                 shape_of(rows, width),
                 shape_of(rows, extra),
                 shape_of(3, width, dtype=F32),
+                *(shape_of(*w.shape) for w in (w_out, w_in, w_back)),
             ),
             in_specs=[SMEM] + [VMEM] * 9 + [HBM] * 4,
-            out_specs=(VMEM,) * 11,
+            out_specs=(VMEM,) * 14,
             scratch_shapes=[
-                pltpu.VMEM((width, width), BF),
-                pltpu.VMEM((width, ff), BF),
-                pltpu.VMEM((ff, width), BF),
                 pltpu.VMEM((rows, width), BF),
                 pltpu.VMEM((rows, width), BF),
                 pltpu.SemaphoreType.DMA((4,)),
             ],
-            compiler_params=params(46),
+            compiler_params=params(24),
         )(
             me,
             tok_prev,
@@ -816,7 +804,7 @@
             vec1,
             vec2,
             b_in,
-            w_qkv,
+            wqkv,
             out_grad.reshape(rows, width),
             w_out,
             w_in,
@@ -837,16 +825,10 @@
             shape_of(rows, width, dtype=F32),
             shape_of(7, width, dtype=F32),
         ),
-        in_specs=[SMEM] + [VMEM] * 8 + [HBM] * 3,
+        in_specs=[SMEM] + [VMEM] * 11,
         out_specs=(VMEM,) * 5,
-        scratch_shapes=[
-            pltpu.VMEM((ff, width), BF),
-            pltpu.VMEM((width, ff), BF),
-            pltpu.VMEM((width, width), BF),
-            pltpu.SemaphoreType.DMA((2 * groups + 1,)),
-        ],
-        compiler_params=params(44),
-    )(me, feed_grad, slope, grad_two, normed, inverse, acts, lse, vec1, w_back, w_in, w_out)
+        compiler_params=params(12),
+    )(me, feed_grad, slope, grad_two, normed, inverse, acts, lse, vec1, *weights)
     msg_prev, msg_next = around(msg)
     grads_peer = flip(grads_send, 0)
 
@@ -879,6 +861,7 @@
             ],
             compiler_params=params(16),
         )(d, acts, acts_peer, feed_keep, acts_peer)
+        grads_keep, msg_prev, msg_next = lax.optimization_barrier((grads_keep, msg_prev, msg_next))
         whole = pl.BlockSpec((rows, side), lambda g: (0, 0))
         inner = pl.pallas_call(
             functools.partial(in_kernel, dp),

time: 151 us -> 137 us (0.907)
  Pallas kernels: 56 us -> 45.6 us
  starting transfers between devices: 39.1 us -> 35.5 us
  waiting for transfers between devices: 40.4 us -> 42.8 us
  local copies, waits for them, and re-layouts: 10.6 us -> 8.53 us
    pallas_call x1, Pallas kernels: 19 us -> 13.8 us  [local(): pl.pallas_call(functools.partial(forward_kernel, groups), name='layer_for...]
    pallas_call x1, Pallas kernels: 9.72 us -> 5.37 us  [local(): pl.pallas_call(functools.partial(backward_kernel, groups), name='layer_ba...]
    ppermute x22, starting transfers between devices: 30.8 us -> 27.3 us  [flip(): return lax.ppermute(value, BOTH, [(i, i ^ 1 << bit) for i in range(count)])]
    ppermute x22, waiting for transfers between devices: 40.4 us -> 42.8 us  [flip(): return lax.ppermute(value, BOTH, [(i, i ^ 1 << bit) for i in range(count)])]
    unnamed x70 -> x64, local copies, waits for them, and re-layouts: 8.64 us -> 6.56 us
  transfers between devices with their start and end apart: 26 -> 26, of which waited for: 8 -> 9; matrix products, arithmetic and copies ran while one was open for 4% -> 5% of each run, Pallas kernels for 24% -> 22%
where the time goes in v1:
time: 137 us; the launch traced here: 136 us
  Pallas kernels  45.6 us (33%)
  waiting for transfers between devices  42.8 us (31%)
  starting transfers between devices  35.5 us (26%)
  local copies, waits for them, and re-layouts  8.53 us (6%)
  other arithmetic  1.63 us (1%)
    ppermute x22, waiting for transfers between devices, flip(): return lax.ppermute(value, BOTH, [(i, i ^ 1 << bit) for i in range(count)])  42.8 us
    ppermute x22, starting transfers between devices, flip(): return lax.ppermute(value, BOTH, [(i, i ^ 1 << bit) for i in range(count)])  27.3 us
    pallas_call x1, Pallas kernels, local(): pl.pallas_call(functools.partial(forward_kernel, groups), name='layer_for...  13.8 us
    pallas_call x1, Pallas kernels, local(): pl.pallas_call(functools.partial(attend_back_kernel, groups), name='atten...  10.4 us
    ppermute x4, starting transfers between devices, around(): return (lax.ppermute(value, 'seq', up), lax.ppermute(value, 'seq', down))  8.22 us
    unnamed x64, local copies, waits for them, and re-layouts  6.56 us
    pallas_call x1, Pallas kernels, local(): pl.pallas_call(functools.partial(backward_kernel, groups), name='layer_ba...  5.37 us
    pallas_call x1, Pallas kernels, local(): pl.pallas_call(functools.partial(back_kernel, dp), name='grad_w_back', co...  3.34 us
  transfers between devices with their start and end apart: 26, of which 9 were waited for; matrix products, arithmetic and copies ran while one was open for 5% of the time, Pallas kernels for 22%

profile of v1, /device:TPU:0, one launch (start us, length us, event | category | flops | bytes accessed | tf_op | source)
XLA Modules:
  0.0 136.4 jit_solution(4663924227609289670)
XLA Ops:
  0.7 2.5 %collective-permute-start = (bf16[256,768]{1,0:T(8,128)(2,1)}, bf16[256,768]{1,0:T(8,128)(2,1)S(1)}, u32[]{:S(2)}, u32[]{:S(2)}) collective-permute-start(bf16[256,768]{1,0:T(8,128)(2,1)} %bitcast.10), channel_id=1, source_target_pairs={{0,1},{1,2},{2,3},{4,5},{5,6},{6,7},{8,9},{9,10},{10,11},{12,13},{... | collective-permute-start | bytes 1179656 | tf_op jit(solution)/shard_map/ppermute | solution.py:746
  3.2 1.3 collective-permute-start.1
  4.5 0.7 constant_dynamic-update-slice_fusion.3
  5.2 0.7 constant_dynamic-update-slice_fusion.2
  5.9 0.7 constant_dynamic-update-slice_fusion.1
  6.6 0.7 constant_dynamic-update-slice_fusion.vec_ref
  7.3 0.7 pad_add_fusion.ids_ref
  8.0 1.0 copy-done.2
  9.0 3.1 %own_projections.1 = (bf16[256,2304]{1,0:T(8,128)(2,1)S(1)}, f32[2,128,384]{2,1,0:T(8,128)S(1)}, f32[2,128,384]{2,1,0:T(8,128)S(1)}, bf16[768,2304]{1,0:T(8,128)(2,1)S(1)}) custom-call(s32[1]{0:T(128)} %bitcast.me_ref, s32[2,2,512]{2,1,0:T(2,128)S(1)} %pad_add_fusion.ids_ref, bf16[256,768]{1,0:T(8,128)(2,1)S(1)} %bitcast.12, ...), custom_call_target="tpu_custom_call" | custom-call | flops 4000000 | bytes 40000 | tf_op jit(solution)/shard_map/own_projections/pallas_call | solution.py:753
  12.2 13.8 %layer_forward.1 = (bf16[2,256,2304]{2,1,0:T(8,128)(2,1)S(1)}, bf16[256,4992]{1,0:T(8,128)(2,1)S(1)}, bf16[256,768]{1,0:T(8,128)(2,1)S(1)}, bf16[256,3072]{1,0:T...) custom-call(s32[1]{0:T(128)} %bitcast.me_ref, ...), custom_call_target="tpu_custom_call" | custom-call | flops 16000000 | bytes 160000 | tf_op jit(solution)/shard_map/layer_forward/pallas_call | solution.py:771
  26.1 3.3 %collective-permute-start.4 = (bf16[256,4992]{1,0:T(8,128)(2,1)S(1)}, bf16[256,4992]{1,0:T(8,128)(2,1)}, u32[]{:S(2)}, u32[]{:S(2)}) collective-permute-start(bf16[256,4992]{1,0:T(8,128)(2,1)S(1)} %get-tuple-element.122.acts_ref.hid.acts.ctx), channel_id=1, source_target_pairs={{0,1},{1,0},{2,3},{3,2},{4,5},{5,4},{6,7},{7,6},{8,9},{9,8},{10,11... | collective-permute-start | bytes 7667720 | tf_op jit(solution)/shard_map/ppermute | solution.py:618
  29.4 5.4 %layer_backward.1 = (bf16[256,1920]{1,0:T(8,128)(2,1)S(1)}, bf16[256,1920]{1,0:T(8,128)(2,1)}, bf16[256,896]{1,0:T(8,128)(2,1)}, f32[256,768]{1,0:T(8,128)S(1)}, f32[7,768]{1,0:T(8,128)S(1)}) custom-call(s32[1]{0:T(128)} %bitcast.me_ref, bf16[256,768]{1,0:T(8,128)(2,1)S(1)} %get-tuple-element.117.feed_ref, ...), custom_call_target="tpu_custom_call" | custom-call | flops 8000000 | bytes 80000 | tf_op jit(solution)/shard_map/layer_backward/pallas_call | solution.py:817
  34.8 1.0 copy-done.13
  35.8 0.6 copy-done.20
  36.4 3.1 %collective-permute-start.2 = (bf16[256,896]{1,0:T(8,128)(2,1)}, bf16[256,896]{1,0:T(8,128)(2,1)}, u32[]{:S(2)}, u32[]{:S(2)}) collective-permute-start(bf16[256,896]{1,0:T(8,128)(2,1)} %get-tuple-element.131.msg_own), channel_id=1, source_target_pairs={{0,1},{1,2},{2,3},{4,5},{5,6},{6,7},{8,9},{9,10},{10,11},{12,13},{... | collective-permute-start | bytes 1376264 | tf_op jit(solution)/shard_map/ppermute | solution.py:746
  39.5 1.3 collective-permute-start.3
  40.9 0.9 copy-done.19
  41.8 3.3 %grad_w_back.1 = (bf16[384,768]{1,0:T(8,128)(2,1)S(1)}, bf16[384,768]{1,0:T(8,128)(2,1)S(1)}, bf16[384,768]{1,0:T(8,128)(2,1)S(1)}, bf16[384,768]{1,0:T(8,128)(2,1)S(1)}) custom-call(s32[1]{0:T(128)} %bitcast.6.d_ref, bf16[256,4992]{1,0:T(8,128)(2,1)S(1)} %get-tuple-element.122.acts_ref.hid.acts.ctx, ...), custom_call_target="tpu_custom_call" | custom-call | flops 3000000 | bytes 30000 | tf_op jit(solution)/shard_map/grad_w_back/pallas_call | solution.py:849
  45.1 1.7 %collective-permute-start.10 = (bf16[384,768]{1,0:T(8,128)(2,1)S(1)}, bf16[384,768]{1,0:T(8,128)(2,1)S(1)}, u32[]{:S(2)}, u32[]{:S(2)}) collective-permute-start(bf16[384,768]{1,0:T(8,128)(2,1)S(1)} %get-tuple-element.153), channel_id=1, source_target_pairs={{0,8},{1,9},{2,10},{3,11},{4,12},{5,13},{6,14},{7,15},{8,0},{9,1},... | collective-permute-start | bytes 1769480 | tf_op jit(solution)/shard_map/ppermute | solution.py:618
  46.8 1.5 %collective-permute-start.9 = (bf16[384,768]{1,0:T(8,128)(2,1)S(1)}, bf16[384,768]{1,0:T(8,128)(2,1)S(1)}, u32[]{:S(2)}, u32[]{:S(2)}) collective-permute-start(bf16[384,768]{1,0:T(8,128)(2,1)S(1)} %get-tuple-element.151), channel_id=1, source_target_pairs={{0,4},{1,5},{2,6},{3,7},{4,0},{5,1},{6,2},{7,3},{8,12},{9,13},{10,... | collective-permute-start | bytes 1769480 | tf_op jit(solution)/shard_map/ppermute | solution.py:618
  48.4 3.1 %grad_w_in.1 = (bf16[384,768]{1,0:T(8,128)(2,1)S(1)}, bf16[384,768]{1,0:T(8,128)(2,1)S(1)}, bf16[384,768]{1,0:T(8,128)(2,1)S(1)}, bf16[384,768]{1,0:T(8,128)(2,1)S(1)}) custom-call(s32[1]{0:T(128)} %bitcast.6.d_ref, bf16[256,4992]{1,0:T(8,128)(2,1)S(1)} %get-tuple-element.122.acts_ref.hid.acts.ctx, ...), custom_call_target="tpu_custom_call" | custom-call | flops 4000000 | bytes 40000 | tf_op jit(solution)/shard_map/grad_w_in/pallas_call | solution.py:866
  51.5 3.3 %collective-permute-start.6 = (bf16[384,768]{1,0:T(8,128)(2,1)S(1)}, bf16[384,768]{1,0:T(8,128)(2,1)S(1)}, u32[]{:S(2)}, u32[]{:S(2)}) collective-permute-start(bf16[384,768]{1,0:T(8,128)(2,1)S(1)} %get-tuple-element.145), channel_id=1, source_target_pairs={{0,2},{1,3},{2,0},{3,1},{4,6},{5,7},{6,4},{7,5},{8,10},{9,11},{10,... | collective-permute-start | bytes 1769480 | tf_op jit(solution)/shard_map/ppermute | solution.py:618
  54.8 0.5 collective-permute-start.7
  55.3 10.4 %attend_backward.1 = (bf16[256,2304]{1,0:T(8,128)(2,1)S(1)}, bf16[256,1152]{1,0:T(8,128)(2,1)S(1)}, bf16[160,1152]{1,0:T(8,128)(2,1)S(1)}, bf16[128,1152]{1,0:T(8,128)(2,1)S(1)}, f32[16,768]{1,0:T(8,128)S(1)}) custom-call(s32[1]{0:T(128)} %bitcast.me_ref, f32[2,128,384]{2,1,0:T(8,128)S(1)} %copy-done.11, f32[2,128,384]{2,1,0:T(8,128)S(1)} %copy-done.16, ...), custom_call_target="tpu_custom_call" | custom-call | flops 11000000 | bytes 110000 | tf_op jit(solution)/shard_map/attend_backward/pallas_call | solution.py:885
  65.8 0.3 add_back_0.1
  66.1 0.1 collective-permute-start.14
  66.2 0.5 collective-permute-start.15
  66.8 1.5 %collective-permute-done.15.peer2 = bf16[128,1152]{1,0:T(8,128)(2,1)S(1)} collective-permute-done((bf16[128,1152]{1,0:T(8,128)(2,1)S(1)}, bf16[128,1152]{1,0:T(8,128)(2,1)S(1)}, u32[]{:S(2)}, u32[]{:S(2)}) %collective-permute-start.15) | collective-permute-done | bytes 294944 | tf_op jit(solution)/shard_map/ppermute | solution.py:618
  68.3 3.2 %grad_w_qkv_out.1 = (bf16[384,768]{1,0:T(8,128)(2,1)S(1)}, bf16[416,768]{1,0:T(8,128)(2,1)S(1)}, bf16[384,768]{1,0:T(8,128)(2,1)S(1)}, bf16[384,768]{1,0:T(8,128)(2,1)S(1)}, f32[16,768]{1,0:T(8,128)S(1)}) custom-call(s32[2]{0:T(128)S(1)} %pad_add_fusion.1.ids_ref, bf16[256,768]{1,0:T(8,128)(2,1)S(1)} %bitcast.14, bf16[256,768]{1,0:T(8,128)(2,1)S(1)} %copy-done.7, ...), custom_call_target="tpu_custom_call" | custom-call | flops 3000000 | bytes 30000 | tf_op jit(solution)/shard_map/grad_w_qkv_out/pallas_call | solution.py:909
  71.5 1.4 %collective-permute-start.19 = (bf16[416,768]{1,0:T(8,128)(2,1)S(1)}, bf16[416,768]{1,0:T(8,128)(2,1)S(1)}, u32[]{:S(2)}, u32[]{:S(2)}) collective-permute-start(bf16[416,768]{1,0:T(8,128)(2,1)S(1)} %get-tuple-element.177), channel_id=1, source_target_pairs={{0,2},{1,3},{2,0},{3,1},{4,6},{5,7},{6,4},{7,5},{8,10},{9,11},{10,... | collective-permute-start | bytes 1916936 | tf_op jit(solution)/shard_map/ppermute | solution.py:618
  73.0 1.6 %collective-permute-start.11 = (bf16[192,768]{1,0:T(8,128)(2,1)S(1)}, bf16[192,768]{1,0:T(8,128)(2,1)S(1)}, u32[]{:S(2)}, u32[]{:S(2)}) collective-permute-start(bf16[192,768]{1,0:T(8,128)(2,1)S(1)} %get-tuple-element.156), channel_id=1, source_target_pairs={{0,8},{1,9},{2,10},{3,11},{4,12},{5,13},{6,14},{7,15},{8,0},{9,1},... | collective-permute-start | bytes 884744 | tf_op jit(solution)/shard_map/ppermute | solution.py:618
  74.5 0.5 collective-permute-start.12
  75.1 0.3 collective-permute-done.7.got1
  75.4 0.3 add_in_0.1
  75.6 1.5 %collective-permute-start.20 = (bf16[384,768]{1,0:T(8,128)(2,1)S(1)}, bf16[384,768]{1,0:T(8,128)(2,1)S(1)}, u32[]{:S(2)}, u32[]{:S(2)}) collective-permute-start(bf16[384,768]{1,0:T(8,128)(2,1)S(1)} %get-tuple-element.181), channel_id=1, source_target_pairs={{0,4},{1,5},{2,6},{3,7},{4,0},{5,1},{6,2},{7,3},{8,12},{9,13},{10,... | collective-permute-start | bytes 1769480 | tf_op jit(solution)/shard_map/ppermute | solution.py:618
  77.2 0.6 collective-permute-start.8
  77.8 4.2 %collective-permute-done.11.got0 = bf16[192,768]{1,0:T(8,128)(2,1)S(1)} collective-permute-done((bf16[192,768]{1,0:T(8,128)(2,1)S(1)}, bf16[192,768]{1,0:T(8,128)(2,1)S(1)}, u32[]{:S(2)}, u32[]{:S(2)}) %collective-permute-start.11) | collective-permute-done | bytes 294944 | tf_op jit(solution)/shard_map/ppermute | solution.py:618
  82.0 0.4 collective-permute-start.16
  82.4 2.1 %collective-permute-done.12.got1 = bf16[192,768]{1,0:T(8,128)(2,1)S(1)} collective-permute-done((bf16[192,768]{1,0:T(8,128)(2,1)S(1)}, bf16[192,768]{1,0:T(8,128)(2,1)S(1)}, u32[]{:S(2)}, u32[]{:S(2)}) %collective-permute-start.12) | collective-permute-done | bytes 294944 | tf_op jit(solution)/shard_map/ppermute | solution.py:618
  84.4 0.1 add_back_1.1
  84.6 0.6 collective-permute-start.13
  85.1 17.1 %collective-permute-done.8.got0 = bf16[192,768]{1,0:T(8,128)(2,1)S(1)} collective-permute-done((bf16[192,768]{1,0:T(8,128)(2,1)S(1)}, bf16[192,768]{1,0:T(8,128)(2,1)S(1)}, u32[]{:S(2)}, u32[]{:S(2)}) %collective-permute-start.8) | collective-permute-done | bytes 294944 | tf_op jit(solution)/shard_map/ppermute | solution.py:618
  102.2 0.1 add_in_1.1
  102.5 0.3 add_qkv_0.1
  102.8 0.6 collective-permute-start.21
  103.4 0.4 collective-permute-start.18
  103.8 1.4 %collective-permute-start.22 = (bf16[192,768]{1,0:T(8,128)(2,1)S(1)}, bf16[192,768]{1,0:T(8,128)(2,1)S(1)}, u32[]{:S(2)}, u32[]{:S(2)}) collective-permute-start(bf16[192,768]{1,0:T(8,128)(2,1)S(1)} %get-tuple-element.191), channel_id=1, source_target_pairs={{0,2},{1,3},{2,0},{3,1},{4,6},{5,7},{6,4},{7,5},{8,10},{9,11},{10,... | collective-permute-start | bytes 884744 | tf_op jit(solution)/shard_map/ppermute | solution.py:618
  105.3 2.6 %collective-permute-start.17 = (bf16[96,768]{1,0:T(8,128)(2,1)S(1)}, bf16[96,768]{1,0:T(8,128)(2,1)S(1)}, u32[]{:S(2)}, u32[]{:S(2)}) collective-permute-start(bf16[96,768]{1,0:T(8,128)(2,1)S(1)} %get-tuple-element.174), channel_id=1, source_target_pairs={{0,16},{1,17},{2,18},{3,19},{4,20},{5,21},{6,22},{7,23},{8,24},{9,... | collective-permute-start | bytes 442376 | tf_op jit(solution)/shard_map/ppermute | solution.py:618
  107.8 6.3 %collective-permute-done.18.got = bf16[192,768]{1,0:T(8,128)(2,1)S(1)} collective-permute-done((bf16[192,768]{1,0:T(8,128)(2,1)S(1)}, bf16[192,768]{1,0:T(8,128)(2,1)S(1)}, u32[]{:S(2)}, u32[]{:S(2)}) %collective-permute-start.18) | collective-permute-done | bytes 294944 | tf_op jit(solution)/shard_map/ppermute | solution.py:618
  114.2 1.9 %collective-permute-start.24 = (bf16[96,768]{1,0:T(8,128)(2,1)S(1)}, bf16[96,768]{1,0:T(8,128)(2,1)S(1)}, u32[]{:S(2)}, u32[]{:S(2)}) collective-permute-start(bf16[96,768]{1,0:T(8,128)(2,1)S(1)} %get-tuple-element.197), channel_id=1, source_target_pairs={{0,16},{1,17},{2,18},{3,19},{4,20},{5,21},{6,22},{7,23},{8,24},{9,... | collective-permute-start | bytes 442376 | tf_op jit(solution)/shard_map/ppermute | solution.py:618
  116.0 0.1 add_qkv_1.1
  116.2 0.6 collective-permute-start.23
  116.8 1.1 fusion
  118.0 0.3 add_back_3.1
  118.2 4.2 %collective-permute-done.24.got = bf16[96,768]{1,0:T(8,128)(2,1)S(1)} collective-permute-done((bf16[96,768]{1,0:T(8,128)(2,1)S(1)}, bf16[96,768]{1,0:T(8,128)(2,1)S(1)}, u32[]{:S(2)}, u32[]{:S(2)}) %collective-permute-start.24) | collective-permute-done | bytes 147488 | tf_op jit(solution)/shard_map/ppermute | solution.py:618
  122.4 0.7 add_in_3.1
  123.1 1.9 %collective-permute-done.23.got = bf16[224,768]{1,0:T(8,128)(2,1)S(1)} collective-permute-done((bf16[224,768]{1,0:T(8,128)(2,1)S(1)}, bf16[224,768]{1,0:T(8,128)(2,1)S(1)}, u32[]{:S(2)}, u32[]{:S(2)}) %collective-permute-start.23) | collective-permute-done | bytes 344096 | tf_op jit(solution)/shard_map/ppermute | solution.py:618
  125.1 2.3 %collective-permute-start.25 = (bf16[128,768]{1,0:T(8,128)(2,1)S(1)}, bf16[128,768]{1,0:T(8,128)(2,1)S(1)}, u32[]{:S(2)}, u32[]{:S(2)}) collective-permute-start(bf16[128,768]{1,0:T(8,128)(2,1)S(1)} %get-tuple-element.204), channel_id=1, source_target_pairs={{0,16},{1,17},{2,18},{3,19},{4,20},{5,21},{6,22},{7,23},{8,24},{9,... | collective-permute-start | bytes 589832 | tf_op jit(solution)/shard_map/ppermute | solution.py:618
  127.4 0.8 add_convert_fusion
  128.2 0.9 copy.32
  129.1 5.3 %collective-permute-done.25.got = bf16[128,768]{1,0:T(8,128)(2,1)S(1)} collective-permute-done((bf16[128,768]{1,0:T(8,128)(2,1)S(1)}, bf16[128,768]{1,0:T(8,128)(2,1)S(1)}, u32[]{:S(2)}, u32[]{:S(2)}) %collective-permute-start.25) | collective-permute-done | bytes 196640 | tf_op jit(solution)/shard_map/ppermute | solution.py:618
  134.4 0.8 add_qkv_3.1
  135.1 0.7 slice_reduce_fusion
  135.8 0.6 reshape.55
  (81 shorter events, 0.5 us)
Async XLA Ops:
  0.6 11.4 %copy-start.29 = (f32[768]{0:T(1024)S(1)}, f32[768]{0:T(1024)}, u32[]{:S(2)}) copy-start(f32[768]{0:T(1024)} %param.26) | copy-start | bytes 9220
  0.7 11.4 %copy-start.28 = (f32[768]{0:T(1024)S(1)}, f32[768]{0:T(1024)}, u32[]{:S(2)}) copy-start(f32[768]{0:T(1024)} %param.30) | copy-start | bytes 9220
  0.7 11.4 %copy-start.27 = (f32[768]{0:T(1024)S(1)}, f32[768]{0:T(1024)}, u32[]{:S(2)}) copy-start(f32[768]{0:T(1024)} %param.31) | copy-start | bytes 9220
  0.7 11.4 %copy-start.26 = (f32[768]{0:T(1024)S(1)}, f32[768]{0:T(1024)}, u32[]{:S(2)}) copy-start(f32[768]{0:T(1024)} %param.32) | copy-start | bytes 9220
  0.7 11.5 %copy-start.22 = (f32[3072]{0:T(1024)S(1)}, f32[3072]{0:T(1024)}, u32[]{:S(2)}) copy-start(f32[3072]{0:T(1024)} %b_in_ref.1) | copy-start | bytes 36868
  0.7 11.5 %collective-permute-start = (bf16[256,768]{1,0:T(8,128)(2,1)}, bf16[256,768]{1,0:T(8,128)(2,1)S(1)}, u32[]{:S(2)}, u32[]{:S(2)}) collective-permute-start(bf16[256,768]{1,0:T(8,128)(2,1)} %bitcast.10), channel_id=1, source_target_pairs={{0,1},{1,2},{2,3},{4,5},{5,6},{6,7},{8,9},{9,10},{10,11},{12,13},{... | collective-permute-start | bytes 1179656 | tf_op jit(solution)/shard_map/ppermute | solution.py:746
  3.2 9.0 %collective-permute-start.1 = (bf16[256,768]{1,0:T(8,128)(2,1)}, bf16[256,768]{1,0:T(8,128)(2,1)S(1)}, u32[]{:S(2)}, u32[]{:S(2)}) collective-permute-start(bf16[256,768]{1,0:T(8,128)(2,1)} %bitcast.11), channel_id=1, source_target_pairs={{1,0},{2,1},{3,2},{5,4},{6,5},{7,6},{9,8},{10,9},{11,10},{13,12},{... | collective-permute-start | bytes 1179656 | tf_op jit(solution)/shard_map/ppermute | solution.py:746
  8.0 1.0 copy-start.2
  9.0 3.2 %copy-start.12 = (bf16[768,768]{1,0:T(8,128)(2,1)S(1)}, bf16[768,768]{1,0:T(8,128)(2,1)}, u32[]{:S(2)}) copy-start(bf16[768,768]{1,0:T(8,128)(2,1)} %wout_hbm.1) | copy-start | bytes 3538948
  9.0 3.2 %copy-start.17 = (bf16[2,128,768]{2,1,0:T(8,128)(2,1)S(1)}, bf16[2,128,768]{2,1,0:T(8,128)(2,1)}, u32[]{:S(2)}) copy-start(bf16[2,128,768]{2,1,0:T(8,128)(2,1)} %param.33) | copy-start | bytes 1179652
  12.1 13.9 %copy-start = (bf16[256,2304]{1,0:T(8,128)(2,1)}, bf16[256,2304]{1,0:T(8,128)(2,1)S(1)}, u32[]{:S(2)}) copy-start(bf16[256,2304]{1,0:T(8,128)(2,1)S(1)} %get-tuple-element.113.own_ref) | copy-start | bytes 3538948
  12.1 13.9 %copy-start.10 = (f32[2,128,384]{2,1,0:T(8,128)}, f32[2,128,384]{2,1,0:T(8,128)S(1)}, u32[]{:S(2)}) copy-start(f32[2,128,384]{2,1,0:T(8,128)S(1)} %get-tuple-element.114.mask_ref) | copy-start | bytes 1179652
  12.2 13.9 %copy-start.15 = (f32[2,128,384]{2,1,0:T(8,128)}, f32[2,128,384]{2,1,0:T(8,128)S(1)}, u32[]{:S(2)}) copy-start(f32[2,128,384]{2,1,0:T(8,128)S(1)} %get-tuple-element.128.mask_t_ref) | copy-start | bytes 1179652
  12.2 13.9 %copy-start.6 = (bf16[256,768]{1,0:T(8,128)(2,1)}, bf16[256,768]{1,0:T(8,128)(2,1)S(1)}, u32[]{:S(2)}) copy-start(bf16[256,768]{1,0:T(8,128)(2,1)S(1)} %collective-permute-done.tok_prev) | copy-start | bytes 1179652
  12.2 13.9 %copy-start.8 = (bf16[256,768]{1,0:T(8,128)(2,1)}, bf16[256,768]{1,0:T(8,128)(2,1)S(1)}, u32[]{:S(2)}) copy-start(bf16[256,768]{1,0:T(8,128)(2,1)S(1)} %collective-permute-done.1.tok_next) | copy-start | bytes 1179652
  26.1 8.7 %copy-start.4 = (bf16[2,256,2304]{2,1,0:T(8,128)(2,1)}, bf16[2,256,2304]{2,1,0:T(8,128)(2,1)S(1)}, u32[]{:S(2)}) copy-start(bf16[2,256,2304]{2,1,0:T(8,128)(2,1)S(1)} %get-tuple-element.129.near_ref) | copy-start | bytes 7077892
  26.1 8.7 %copy-start.18 = (bf16[256,384]{1,0:T(8,128)(2,1)}, bf16[256,384]{1,0:T(8,128)(2,1)S(1)}, u32[]{:S(2)}) copy-start(bf16[256,384]{1,0:T(8,128)(2,1)S(1)} %get-tuple-element.134.feed) | copy-start | bytes 589828
  26.1 8.7 %copy-start.23 = (f32[3,768]{1,0:T(4,128)}, f32[3,768]{1,0:T(4,128)S(1)}, u32[]{:S(2)}) copy-start(f32[3,768]{1,0:T(4,128)S(1)} %get-tuple-element.141.small1_ref) | copy-start | bytes 27652
  26.1 14.7 %collective-permute-start.4 = (bf16[256,4992]{1,0:T(8,128)(2,1)S(1)}, bf16[256,4992]{1,0:T(8,128)(2,1)}, u32[]{:S(2)}, u32[]{:S(2)}) collective-permute-start(bf16[256,4992]{1,0:T(8,128)(2,1)S(1)} %get-tuple-element.122.acts_ref.hid.acts.ctx), channel_id=1, source_target_pairs={{0,1},{1,0},{2,3},{3,2},{4,5},{5,4},{6,7},{7,6},{8,9},{9,8},{10,11... | collective-permute-start | bytes 7667720 | tf_op jit(solution)/shard_map/ppermute | solution.py:618
  34.8 1.0 copy-start.13
  35.8 0.6 copy-start.20
  36.4 12.0 %collective-permute-start.5 = (bf16[256,1920]{1,0:T(8,128)(2,1)}, bf16[256,1920]{1,0:T(8,128)(2,1)}, u32[]{:S(2)}, u32[]{:S(2)}) collective-permute-start(bf16[256,1920]{1,0:T(8,128)(2,1)} %get-tuple-element.137), channel_id=1, source_target_pairs={{0,1},{1,0},{2,3},{3,2},{4,5},{5,4},{6,7},{7,6},{8,9},{9,8},{10,11... | collective-permute-start | bytes 2949128 | tf_op jit(solution)/shard_map/ppermute | solution.py:618
  36.4 11.9 %collective-permute-start.2 = (bf16[256,896]{1,0:T(8,128)(2,1)}, bf16[256,896]{1,0:T(8,128)(2,1)}, u32[]{:S(2)}, u32[]{:S(2)}) collective-permute-start(bf16[256,896]{1,0:T(8,128)(2,1)} %get-tuple-element.131.msg_own), channel_id=1, source_target_pairs={{0,1},{1,2},{2,3},{4,5},{5,6},{6,7},{8,9},{9,10},{10,11},{12,13},{... | collective-permute-start | bytes 1376264 | tf_op jit(solution)/shard_map/ppermute | solution.py:746
  39.5 8.8 %collective-permute-start.3 = (bf16[256,896]{1,0:T(8,128)(2,1)}, bf16[256,896]{1,0:T(8,128)(2,1)}, u32[]{:S(2)}, u32[]{:S(2)}) collective-permute-start(bf16[256,896]{1,0:T(8,128)(2,1)} %get-tuple-element.131.msg_own), channel_id=1, source_target_pairs={{1,0},{2,1},{3,2},{5,4},{6,5},{7,6},{9,8},{10,9},{11,10},{13,12},{... | collective-permute-start | bytes 1376264 | tf_op jit(solution)/shard_map/ppermute | solution.py:746
  40.8 0.9 copy-start.19
  45.1 20.7 %collective-permute-start.10 = (bf16[384,768]{1,0:T(8,128)(2,1)S(1)}, bf16[384,768]{1,0:T(8,128)(2,1)S(1)}, u32[]{:S(2)}, u32[]{:S(2)}) collective-permute-start(bf16[384,768]{1,0:T(8,128)(2,1)S(1)} %get-tuple-element.153), channel_id=1, source_target_pairs={{0,8},{1,9},{2,10},{3,11},{4,12},{5,13},{6,14},{7,15},{8,0},{9,1},... | collective-permute-start | bytes 1769480 | tf_op jit(solution)/shard_map/ppermute | solution.py:618
  46.8 19.0 %collective-permute-start.9 = (bf16[384,768]{1,0:T(8,128)(2,1)S(1)}, bf16[384,768]{1,0:T(8,128)(2,1)S(1)}, u32[]{:S(2)}, u32[]{:S(2)}) collective-permute-start(bf16[384,768]{1,0:T(8,128)(2,1)S(1)} %get-tuple-element.151), channel_id=1, source_target_pairs={{0,4},{1,5},{2,6},{3,7},{4,0},{5,1},{6,2},{7,3},{8,12},{9,13},{10,... | collective-permute-start | bytes 1769480 | tf_op jit(solution)/shard_map/ppermute | solution.py:618
  48.3 7.0 %copy-start.1 = (bf16[256,2304]{1,0:T(8,128)(2,1)S(1)}, bf16[256,2304]{1,0:T(8,128)(2,1)}, u32[]{:S(2)}) copy-start(bf16[256,2304]{1,0:T(8,128)(2,1)} %copy-done) | copy-start | bytes 3538948
  48.3 7.0 %copy-start.5 = (bf16[2,256,2304]{2,1,0:T(8,128)(2,1)S(1)}, bf16[2,256,2304]{2,1,0:T(8,128)(2,1)}, u32[]{:S(2)}) copy-start(bf16[2,256,2304]{2,1,0:T(8,128)(2,1)} %copy-done.4) | copy-start | bytes 7077892
  48.3 7.0 %copy-start.11 = (f32[2,128,384]{2,1,0:T(8,128)S(1)}, f32[2,128,384]{2,1,0:T(8,128)}, u32[]{:S(2)}) copy-start(f32[2,128,384]{2,1,0:T(8,128)} %copy-done.10) | copy-start | bytes 1179652
  48.3 7.0 %copy-start.16 = (f32[2,128,384]{2,1,0:T(8,128)S(1)}, f32[2,128,384]{2,1,0:T(8,128)}, u32[]{:S(2)}) copy-start(f32[2,128,384]{2,1,0:T(8,128)} %copy-done.15) | copy-start | bytes 1179652
  48.3 7.0 %copy-start.21 = (f32[7,768]{1,0:T(8,128)S(1)}, f32[7,768]{1,0:T(8,128)}, u32[]{:S(2)}) copy-start(f32[7,768]{1,0:T(8,128)} %copy-done.20) | copy-start | bytes 64516
  48.3 7.0 %copy-start.24 = (f32[3,768]{1,0:T(4,128)S(1)}, f32[3,768]{1,0:T(4,128)}, u32[]{:S(2)}) copy-start(f32[3,768]{1,0:T(4,128)} %copy-done.23) | copy-start | bytes 27652
  51.5 23.6 %collective-permute-start.6 = (bf16[384,768]{1,0:T(8,128)(2,1)S(1)}, bf16[384,768]{1,0:T(8,128)(2,1)S(1)}, u32[]{:S(2)}, u32[]{:S(2)}) collective-permute-start(bf16[384,768]{1,0:T(8,128)(2,1)S(1)} %get-tuple-element.145), channel_id=1, source_target_pairs={{0,2},{1,3},{2,0},{3,1},{4,6},{5,7},{6,4},{7,5},{8,10},{9,11},{10,... | collective-permute-start | bytes 1769480 | tf_op jit(solution)/shard_map/ppermute | solution.py:618
  54.8 20.6 %collective-permute-start.7 = (bf16[384,768]{1,0:T(8,128)(2,1)S(1)}, bf16[384,768]{1,0:T(8,128)(2,1)S(1)}, u32[]{:S(2)}, u32[]{:S(2)}) collective-permute-start(bf16[384,768]{1,0:T(8,128)(2,1)S(1)} %get-tuple-element.147), channel_id=1, source_target_pairs={{0,4},{1,5},{2,6},{3,7},{4,0},{5,1},{6,2},{7,3},{8,12},{9,13},{10,... | collective-permute-start | bytes 1769480 | tf_op jit(solution)/shard_map/ppermute | solution.py:618
  65.8 2.5 %copy-start.3 = (bf16[2,128,768]{2,1,0:T(8,128)(2,1)S(1)}, bf16[2,128,768]{2,1,0:T(8,128)(2,1)}, u32[]{:S(2)}) copy-start(bf16[2,128,768]{2,1,0:T(8,128)(2,1)} %param.17) | copy-start | bytes 1179652
  65.8 2.5 %copy-start.7 = (bf16[256,768]{1,0:T(8,128)(2,1)S(1)}, bf16[256,768]{1,0:T(8,128)(2,1)}, u32[]{:S(2)}) copy-start(bf16[256,768]{1,0:T(8,128)(2,1)} %copy-done.6) | copy-start | bytes 1179652
  65.8 2.5 %copy-start.9 = (bf16[256,768]{1,0:T(8,128)(2,1)S(1)}, bf16[256,768]{1,0:T(8,128)(2,1)}, u32[]{:S(2)}) copy-start(bf16[256,768]{1,0:T(8,128)(2,1)} %copy-done.8) | copy-start | bytes 1179652
  66.1 2.2 %collective-permute-start.14 = (bf16[160,1152]{1,0:T(8,128)(2,1)S(1)}, bf16[160,1152]{1,0:T(8,128)(2,1)S(1)}, u32[]{:S(2)}, u32[]{:S(2)}) collective-permute-start(bf16[160,1152]{1,0:T(8,128)(2,1)S(1)} %get-tuple-element.163), channel_id=1, source_target_pairs={{0,1},{1,0},{2,3},{3,2},{4,5},{5,4},{6,7},{7,6},{8,9},{9,8},{10,11... | collective-permute-start | bytes 1105928 | tf_op jit(solution)/shard_map/ppermute | solution.py:618
  66.2 2.1 %collective-permute-start.15 = (bf16[128,1152]{1,0:T(8,128)(2,1)S(1)}, bf16[128,1152]{1,0:T(8,128)(2,1)S(1)}, u32[]{:S(2)}, u32[]{:S(2)}) collective-permute-start(bf16[128,1152]{1,0:T(8,128)(2,1)S(1)} %get-tuple-element.164), channel_id=1, source_target_pairs={{0,1},{1,0},{2,3},{3,2},{4,5},{5,4},{6,7},{7,6},{8,9},{9,8},{10,11... | collective-permute-start | bytes 884744 | tf_op jit(solution)/shard_map/ppermute | solution.py:618
  71.5 30.9 %collective-permute-start.19 = (bf16[416,768]{1,0:T(8,128)(2,1)S(1)}, bf16[416,768]{1,0:T(8,128)(2,1)S(1)}, u32[]{:S(2)}, u32[]{:S(2)}) collective-permute-start(bf16[416,768]{1,0:T(8,128)(2,1)S(1)} %get-tuple-element.177), channel_id=1, source_target_pairs={{0,2},{1,3},{2,0},{3,1},{4,6},{5,7},{6,4},{7,5},{8,10},{9,11},{10,... | collective-permute-start | bytes 1916936 | tf_op jit(solution)/shard_map/ppermute | solution.py:618
  73.0 9.0 %collective-permute-start.11 = (bf16[192,768]{1,0:T(8,128)(2,1)S(1)}, bf16[192,768]{1,0:T(8,128)(2,1)S(1)}, u32[]{:S(2)}, u32[]{:S(2)}) collective-permute-start(bf16[192,768]{1,0:T(8,128)(2,1)S(1)} %get-tuple-element.156), channel_id=1, source_target_pairs={{0,8},{1,9},{2,10},{3,11},{4,12},{5,13},{6,14},{7,15},{8,0},{9,1},... | collective-permute-start | bytes 884744 | tf_op jit(solution)/shard_map/ppermute | solution.py:618
  74.5 9.9 %collective-permute-start.12 = (bf16[192,768]{1,0:T(8,128)(2,1)S(1)}, bf16[192,768]{1,0:T(8,128)(2,1)S(1)}, u32[]{:S(2)}, u32[]{:S(2)}) collective-permute-start(bf16[192,768]{1,0:T(8,128)(2,1)S(1)} %get-tuple-element.158), channel_id=1, source_target_pairs={{0,4},{1,5},{2,6},{3,7},{4,0},{5,1},{6,2},{7,3},{8,12},{9,13},{10,... | collective-permute-start | bytes 884744 | tf_op jit(solution)/shard_map/ppermute | solution.py:618
  75.6 26.8 %collective-permute-start.20 = (bf16[384,768]{1,0:T(8,128)(2,1)S(1)}, bf16[384,768]{1,0:T(8,128)(2,1)S(1)}, u32[]{:S(2)}, u32[]{:S(2)}) collective-permute-start(bf16[384,768]{1,0:T(8,128)(2,1)S(1)} %get-tuple-element.181), channel_id=1, source_target_pairs={{0,4},{1,5},{2,6},{3,7},{4,0},{5,1},{6,2},{7,3},{8,12},{9,13},{10,... | collective-permute-start | bytes 1769480 | tf_op jit(solution)/shard_map/ppermute | solution.py:618
  77.2 25.0 %collective-permute-start.8 = (bf16[192,768]{1,0:T(8,128)(2,1)S(1)}, bf16[192,768]{1,0:T(8,128)(2,1)S(1)}, u32[]{:S(2)}, u32[]{:S(2)}) collective-permute-start(bf16[192,768]{1,0:T(8,128)(2,1)S(1)} %get-tuple-element.148), channel_id=1, source_target_pairs={{0,4},{1,5},{2,6},{3,7},{4,0},{5,1},{6,2},{7,3},{8,12},{9,13},{10,... | collective-permute-start | bytes 884744 | tf_op jit(solution)/shard_map/ppermute | solution.py:618
  82.0 20.3 %collective-permute-start.16 = (bf16[192,768]{1,0:T(8,128)(2,1)S(1)}, bf16[192,768]{1,0:T(8,128)(2,1)S(1)}, u32[]{:S(2)}, u32[]{:S(2)}) collective-permute-start(bf16[192,768]{1,0:T(8,128)(2,1)S(1)} %get-tuple-element.171), channel_id=1, source_target_pairs={{0,2},{1,3},{2,0},{3,1},{4,6},{5,7},{6,4},{7,5},{8,10},{9,11},{10,... | collective-permute-start | bytes 884744 | tf_op jit(solution)/shard_map/ppermute | solution.py:618
  84.6 17.8 %collective-permute-start.13 = (bf16[192,768]{1,0:T(8,128)(2,1)S(1)}, bf16[192,768]{1,0:T(8,128)(2,1)S(1)}, u32[]{:S(2)}, u32[]{:S(2)}) collective-permute-start(bf16[192,768]{1,0:T(8,128)(2,1)S(1)} %get-tuple-element.161), channel_id=1, source_target_pairs={{0,2},{1,3},{2,0},{3,1},{4,6},{5,7},{6,4},{7,5},{8,10},{9,11},{10,... | collective-permute-start | bytes 884744 | tf_op jit(solution)/shard_map/ppermute | solution.py:618
  102.4 14.4 %copy-start.25 = (bf16[768,2304]{1,0:T(8,128)(2,1)S(1)}, bf16[768,2304]{1,0:T(8,128)(2,1)}, u32[]{:S(2)}) copy-start(bf16[768,2304]{1,0:T(8,128)(2,1)} %wqkv_hbm.1) | copy-start | bytes 10616836
  102.8 13.2 %collective-permute-start.21 = (bf16[224,768]{1,0:T(8,128)(2,1)S(1)}, bf16[224,768]{1,0:T(8,128)(2,1)S(1)}, u32[]{:S(2)}, u32[]{:S(2)}) collective-permute-start(bf16[224,768]{1,0:T(8,128)(2,1)S(1)} %get-tuple-element.185), channel_id=1, source_target_pairs={{0,4},{1,5},{2,6},{3,7},{4,0},{5,1},{6,2},{7,3},{8,12},{9,13},{10,... | collective-permute-start | bytes 1032200 | tf_op jit(solution)/shard_map/ppermute | solution.py:618
  103.4 10.7 %collective-permute-start.18 = (bf16[192,768]{1,0:T(8,128)(2,1)S(1)}, bf16[192,768]{1,0:T(8,128)(2,1)S(1)}, u32[]{:S(2)}, u32[]{:S(2)}) collective-permute-start(bf16[192,768]{1,0:T(8,128)(2,1)S(1)} %get-tuple-element.175), channel_id=1, source_target_pairs={{0,8},{1,9},{2,10},{3,11},{4,12},{5,13},{6,14},{7,15},{8,0},{9,1},... | collective-permute-start | bytes 884744 | tf_op jit(solution)/shard_map/ppermute | solution.py:618
  103.8 12.2 %collective-permute-start.22 = (bf16[192,768]{1,0:T(8,128)(2,1)S(1)}, bf16[192,768]{1,0:T(8,128)(2,1)S(1)}, u32[]{:S(2)}, u32[]{:S(2)}) collective-permute-start(bf16[192,768]{1,0:T(8,128)(2,1)S(1)} %get-tuple-element.191), channel_id=1, source_target_pairs={{0,2},{1,3},{2,0},{3,1},{4,6},{5,7},{6,4},{7,5},{8,10},{9,11},{10,... | collective-permute-start | bytes 884744 | tf_op jit(solution)/shard_map/ppermute | solution.py:618
  105.3 12.7 %collective-permute-start.17 = (bf16[96,768]{1,0:T(8,128)(2,1)S(1)}, bf16[96,768]{1,0:T(8,128)(2,1)S(1)}, u32[]{:S(2)}, u32[]{:S(2)}) collective-permute-start(bf16[96,768]{1,0:T(8,128)(2,1)S(1)} %get-tuple-element.174), channel_id=1, source_target_pairs={{0,16},{1,17},{2,18},{3,19},{4,20},{5,21},{6,22},{7,23},{8,24},{9,... | collective-permute-start | bytes 442376 | tf_op jit(solution)/shard_map/ppermute | solution.py:618
  114.2 8.2 %collective-permute-start.24 = (bf16[96,768]{1,0:T(8,128)(2,1)S(1)}, bf16[96,768]{1,0:T(8,128)(2,1)S(1)}, u32[]{:S(2)}, u32[]{:S(2)}) collective-permute-start(bf16[96,768]{1,0:T(8,128)(2,1)S(1)} %get-tuple-element.197), channel_id=1, source_target_pairs={{0,16},{1,17},{2,18},{3,19},{4,20},{5,21},{6,22},{7,23},{8,24},{9,... | collective-permute-start | bytes 442376 | tf_op jit(solution)/shard_map/ppermute | solution.py:618
  116.2 8.8 %collective-permute-start.23 = (bf16[224,768]{1,0:T(8,128)(2,1)S(1)}, bf16[224,768]{1,0:T(8,128)(2,1)S(1)}, u32[]{:S(2)}, u32[]{:S(2)}) collective-permute-start(bf16[224,768]{1,0:T(8,128)(2,1)S(1)} %get-tuple-element.195), channel_id=1, source_target_pairs={{0,8},{1,9},{2,10},{3,11},{4,12},{5,13},{6,14},{7,15},{8,0},{9,1},... | collective-permute-start | bytes 1032200 | tf_op jit(solution)/shard_map/ppermute | solution.py:618
  116.8 10.6 %copy-start.14 = (f32[256,768]{1,0:T(8,128)S(1)}, f32[256,768]{1,0:T(8,128)}, u32[]{:S(2)}) copy-start(f32[256,768]{1,0:T(8,128)} %copy-done.13) | copy-start | bytes 2359300
  125.1 9.3 %collective-permute-start.25 = (bf16[128,768]{1,0:T(8,128)(2,1)S(1)}, bf16[128,768]{1,0:T(8,128)(2,1)S(1)}, u32[]{:S(2)}, u32[]{:S(2)}) collective-permute-start(bf16[128,768]{1,0:T(8,128)(2,1)S(1)} %get-tuple-element.204), channel_id=1, source_target_pairs={{0,16},{1,17},{2,18},{3,19},{4,20},{5,21},{6,22},{7,23},{8,24},{9,... | collective-permute-start | bytes 589832 | tf_op jit(solution)/shard_map/ppermute | solution.py:618

commit v2 on v1

--- a/solution.py
+++ b/solution.py
@@ -402,7 +402,7 @@
         ],
         axis=0,
     )
-    send_ref[loc:, :] = jnp.zeros((2 * SUM_ROWS, send_ref.shape[1]), BF)
+    send_ref[loc:, :] = jnp.zeros((SUM_ROWS, send_ref.shape[1]), BF)
     pack_sums(sums_ref[...], send_ref, loc)
     block = 3 * width // groups
     for s in range(groups):
@@ -421,26 +421,25 @@
 
 
 def pack_sums(value, ref, at):
-    high = value.astype(BF)
-    ref[at : at + SUM_ROWS, : value.shape[1]] = high
-    ref[at + SUM_ROWS : at + 2 * SUM_ROWS, : value.shape[1]] = (value - high.astype(F32)).astype(BF)
+    ref[at : at + SUM_ROWS, : value.shape[1]] = value.astype(BF)
 
 
 def read_sums(ref, at, width):
-    high = ref[at : at + SUM_ROWS, :width].astype(F32)
-    return high + ref[at + SUM_ROWS : at + 2 * SUM_ROWS, :width].astype(F32)
-
-
-def turn_rows(d, dp, tmp_ref, turned_ref, block_rows, part):
+    return ref[at : at + SUM_ROWS, :width].astype(F32)
+
+
+def turn_rows(order, d, tmp_ref, turned_ref, block_rows, part):
     rows = block_rows // 2
-    for j, rel in enumerate(low_first(dp)):
+    bits = [bit - 2 for bit in order if bit != 1]
+    for j in range(1 << len(bits)):
+        rel = sum(((j >> (len(bits) - 1 - k)) & 1) << bit for k, bit in enumerate(bits))
         start = pl.multiple_of((rel ^ d) * block_rows + part * rows, rows)
         turned_ref[j * rows : (j + 1) * rows, :] = tmp_ref[pl.ds(start, rows), :]
 
 
-def low_first(dp):
-    bits = dp.bit_length() - 1
-    return [sum(((j >> (bits - 1 - k)) & 1) << k for k in range(bits)) for j in range(dp)]
+def orders_of(kind):
+    first, second, *rest = HALVING[kind]
+    return (first, second, *rest), (second, first, *rest)
 
 
 def both_left(mine, peer):
@@ -454,14 +453,15 @@
     ]
 
 
-def put(result, part, x, keeps, sends):
-    total = result.shape[0]
-    half = total // 2
-    if part == 0:
-        (sends if x else keeps)[0][:total] = result
-    else:
-        keeps[1][x * half : (x + 1) * half] = result[:half]
-        sends[1][x * half : (x + 1) * half] = result[half:]
+def put(result, order, x, keep, send):
+    blocks = 1 << (len(order) - 1)
+    rows = result.shape[0] // blocks
+    k = order.index(1)
+    run = blocks >> k
+    for i in range(1 << k):
+        at = (2 * i + x) * run
+        ref, at = (keep, at) if at < blocks else (send, at - blocks)
+        ref[at * rows : (at + run) * rows] = result[i * run * rows : (i + 1) * run * rows]
 
 
 def in_kernel(dp, d_ref, acts, acts_peer, mine, peer, keep0, send0, keep1, send1, tmp, *turned):
@@ -469,11 +469,11 @@
     tmp[...] = both_left(acts[...], acts_peer[...])
     wide = (mine.shape[1] - width // 2) // 2
     rights = by_halves((mine, peer), 0, wide)
-    for part in range(2):
-        turn_rows(d_ref[0], dp, tmp, turned[part], width // dp, part)
+    outs = ((keep0, send0), (keep1, send1))
+    for part, order in enumerate(orders_of("in")):
+        turn_rows(order, d_ref[0], tmp, turned[part], width // dp, part)
         for x in range(2):
-            result = dot(turned[part][...], rights[x]).astype(BF)
-            put(result, part, x, (keep0, keep1), (send0, send1))
+            put(dot(turned[part][...], rights[x]).astype(BF), order, x, *outs[part])
 
 
 def qkv_kernel(
@@ -507,14 +507,15 @@
     half = peer2.shape[0]
     rights = by_halves((mine, peer.at[:half], peer2), 0, mine.shape[1] // 2)
     outs = by_halves((out_mine, out_peer), 0, out_mine.shape[1] // 2)
-    for part in range(2):
-        turn_rows(d, dp, tmp, turned[part], width // dp, part)
-        turn_rows(d, dp, tmp2, turned[2 + part], width // dp, part)
+    refs = ((keep0, send0), (keep1, send1))
+    for part, order in enumerate(orders_of("qkv")):
+        turn_rows(order, d, tmp, turned[part], width // dp, part)
+        turn_rows(order, d, tmp2, turned[2 + part], width // dp, part)
         for x in range(2):
             result = jnp.concatenate(
                 [dot(turned[part][...], rights[x]), dot(turned[2 + part][...], outs[x])], axis=1
             ).astype(BF)
-            put(result, part, x, (keep0, keep1), (send0, send1))
+            put(result, order, x, *refs[part])
     total = sums_ref[...] + read_sums(peer, half, width)
     total_ref[...] = total
     pack_sums(total, send0, keep0.shape[0])
@@ -526,8 +527,7 @@
     side = feed.shape[1] // 2
     rows = side // 4
     turned = [feed[...].T, feed_peer[...].T]
-    first, second, *rest = HALVING["back"]
-    orders = [(first, second, *rest), (second, first, *rest)]
+    orders = orders_of("back")
     for rel in range(dp):
         span = pl.ds(pl.multiple_of((rel ^ d) * chunk, chunk), chunk)
         result = (dot(turned[0], hid[:, span]) + dot(turned[1], hid_peer[:, span])).astype(BF)
@@ -610,7 +610,7 @@
         step_sums(sums_ref, got, keep.shape[0], total_ref, None, 0)
 
 
-HALVING = {"back": (2, 3, 1, 4), "in": (1, 2, 3, 4), "qkv": (1, 2, 3, 4)}
+HALVING = {"back": (2, 3, 1, 4), "in": (1, 3, 2, 4), "qkv": (1, 3, 2, 4)}
 
 
 def flip(value, bit):
@@ -625,7 +625,7 @@
         self.gots = tuple(flip(v, b) for v, b in zip(parts[1::2], HALVING[kind]))
 
     def step(self, outs):
-        extra = 0 if self.sums is None else 2 * SUM_ROWS
+        extra = 0 if self.sums is None else SUM_ROWS
         total = self.keeps[0].shape[0]
         width = self.keeps[0].shape[1]
         half = total // 2
@@ -889,7 +889,7 @@
         out_shape=(
             shape_of(rows, 3 * width),
             shape_of(rows, 2 * qkv_block),
-            shape_of(loc + 2 * SUM_ROWS, 2 * qkv_block),
+            shape_of(loc + SUM_ROWS, 2 * qkv_block),
             shape_of(rows - loc, 2 * qkv_block),
             shape_of(SUM_ROWS, width, dtype=F32),
         ),
@@ -912,7 +912,7 @@
             cost_estimate=cost(3),
             out_shape=(
                 shape_of(part_rows, width),
-                shape_of(part_rows + 2 * SUM_ROWS, width),
+                shape_of(part_rows + SUM_ROWS, width),
                 shape_of(part_rows, width),
                 shape_of(part_rows, width),
                 shape_of(SUM_ROWS, width, dtype=F32),
@@ -922,7 +922,7 @@
             + [pl.BlockSpec((rows, width), lambda i: (0, 0))] * 3
             + [acts_block(ctx_at)] * 2
             + [pl.BlockSpec((rows, 2 * qkv_block), lambda i: (0, 0))]
-            + [pl.BlockSpec((loc + 2 * SUM_ROWS, 2 * qkv_block), lambda i: (0, 0))]
+            + [pl.BlockSpec((loc + SUM_ROWS, 2 * qkv_block), lambda i: (0, 0))]
             + [pl.BlockSpec((rows - loc, 2 * qkv_block), lambda i: (0, 0))]
             + [pl.BlockSpec((rows, extra), lambda i: (0, out_at))] * 2
             + [pl.BlockSpec((SUM_ROWS, width), lambda i: (0, 0))],

time: 137 us -> 134 us (0.978)
  waiting for transfers between devices: 42.8 us -> 38.1 us
  starting transfers between devices: 35.5 us -> 37 us
    ppermute x22, waiting for transfers between devices: 42.8 us -> 38.1 us  [flip(): return lax.ppermute(value, BOTH, [(i, i ^ 1 << bit) for i in range(count)])]
    ppermute x22, starting transfers between devices: 27.3 us -> 28.8 us  [flip(): return lax.ppermute(value, BOTH, [(i, i ^ 1 << bit) for i in range(count)])]
  transfers between devices with their start and end apart: 26 -> 26, of which waited for: 9 -> 8; matrix products, arithmetic and copies ran while one was open for 5% -> 5% of each run, Pallas kernels for 22% -> 23%
where the time goes in v2:
time: 134 us; the launch traced here: 133 us
  Pallas kernels  45.5 us (34%)
  waiting for transfers between devices  38.1 us (28%)
  starting transfers between devices  37 us (28%)
  local copies, waits for them, and re-layouts  8.53 us (6%)
  other arithmetic  1.62 us (1%)
    ppermute x22, waiting for transfers between devices, flip(): return lax.ppermute(value, BOTH, [(i, i ^ 1 << bit) for i in range(count)])  38.1 us
    ppermute x22, starting transfers between devices, flip(): return lax.ppermute(value, BOTH, [(i, i ^ 1 << bit) for i in range(count)])  28.8 us
    pallas_call x1, Pallas kernels, local(): pl.pallas_call(functools.partial(forward_kernel, groups), name='layer_for...  13.8 us
    pallas_call x1, Pallas kernels, local(): pl.pallas_call(functools.partial(attend_back_kernel, groups), name='atten...  10.4 us
    ppermute x4, starting transfers between devices, around(): return (lax.ppermute(value, 'seq', up), lax.ppermute(value, 'seq', down))  8.22 us
    unnamed x64, local copies, waits for them, and re-layouts  6.56 us
    pallas_call x1, Pallas kernels, local(): pl.pallas_call(functools.partial(backward_kernel, groups), name='layer_ba...  5.37 us
    pallas_call x1, Pallas kernels, local(): pl.pallas_call(functools.partial(back_kernel, dp), name='grad_w_back', co...  3.34 us
  transfers between devices with their start and end apart: 26, of which 8 were waited for; matrix products, arithmetic and copies ran while one was open for 5% of the time, Pallas kernels for 23%

profile of v2, /device:TPU:0, one launch (start us, length us, event | category | flops | bytes accessed | tf_op | source)
XLA Modules:
  0.0 133.2 jit_solution(15700115009355168832)
XLA Ops:
  0.7 2.5 %collective-permute-start = (bf16[256,768]{1,0:T(8,128)(2,1)}, bf16[256,768]{1,0:T(8,128)(2,1)S(1)}, u32[]{:S(2)}, u32[]{:S(2)}) collective-permute-start(bf16[256,768]{1,0:T(8,128)(2,1)} %bitcast.10), channel_id=1, source_target_pairs={{0,1},{1,2},{2,3},{4,5},{5,6},{6,7},{8,9},{9,10},{10,11},{12,13},{... | collective-permute-start | bytes 1179656 | tf_op jit(solution)/shard_map/ppermute | solution.py:746
  3.2 1.3 collective-permute-start.1
  4.5 0.7 constant_dynamic-update-slice_fusion.3
  5.2 0.7 constant_dynamic-update-slice_fusion.2
  5.9 0.7 constant_dynamic-update-slice_fusion.1
  6.6 0.7 constant_dynamic-update-slice_fusion.vec_ref
  7.3 0.7 pad_add_fusion.ids_ref
  8.0 1.0 copy-done.2
  9.0 3.1 %own_projections.1 = (bf16[256,2304]{1,0:T(8,128)(2,1)S(1)}, f32[2,128,384]{2,1,0:T(8,128)S(1)}, f32[2,128,384]{2,1,0:T(8,128)S(1)}, bf16[768,2304]{1,0:T(8,128)(2,1)S(1)}) custom-call(s32[1]{0:T(128)} %bitcast.me_ref, s32[2,2,512]{2,1,0:T(2,128)S(1)} %pad_add_fusion.ids_ref, bf16[256,768]{1,0:T(8,128)(2,1)S(1)} %bitcast.12, ...), custom_call_target="tpu_custom_call" | custom-call | flops 4000000 | bytes 40000 | tf_op jit(solution)/shard_map/own_projections/pallas_call | solution.py:753
  12.2 13.8 %layer_forward.1 = (bf16[2,256,2304]{2,1,0:T(8,128)(2,1)S(1)}, bf16[256,4992]{1,0:T(8,128)(2,1)S(1)}, bf16[256,768]{1,0:T(8,128)(2,1)S(1)}, bf16[256,3072]{1,0:T...) custom-call(s32[1]{0:T(128)} %bitcast.me_ref, ...), custom_call_target="tpu_custom_call" | custom-call | flops 16000000 | bytes 160000 | tf_op jit(solution)/shard_map/layer_forward/pallas_call | solution.py:771
  26.1 3.3 %collective-permute-start.4 = (bf16[256,4992]{1,0:T(8,128)(2,1)S(1)}, bf16[256,4992]{1,0:T(8,128)(2,1)}, u32[]{:S(2)}, u32[]{:S(2)}) collective-permute-start(bf16[256,4992]{1,0:T(8,128)(2,1)S(1)} %get-tuple-element.122.acts_ref.hid.acts.ctx), channel_id=1, source_target_pairs={{0,1},{1,0},{2,3},{3,2},{4,5},{5,4},{6,7},{7,6},{8,9},{9,8},{10,11... | collective-permute-start | bytes 7667720 | tf_op jit(solution)/shard_map/ppermute | solution.py:618
  29.4 5.4 %layer_backward.1 = (bf16[256,1920]{1,0:T(8,128)(2,1)S(1)}, bf16[256,1920]{1,0:T(8,128)(2,1)}, bf16[256,896]{1,0:T(8,128)(2,1)}, f32[256,768]{1,0:T(8,128)S(1)}, f32[7,768]{1,0:T(8,128)S(1)}) custom-call(s32[1]{0:T(128)} %bitcast.me_ref, bf16[256,768]{1,0:T(8,128)(2,1)S(1)} %get-tuple-element.117.feed_ref, ...), custom_call_target="tpu_custom_call" | custom-call | flops 8000000 | bytes 80000 | tf_op jit(solution)/shard_map/layer_backward/pallas_call | solution.py:817
  34.8 1.0 copy-done.13
  35.8 0.6 copy-done.20
  36.4 3.1 %collective-permute-start.2 = (bf16[256,896]{1,0:T(8,128)(2,1)}, bf16[256,896]{1,0:T(8,128)(2,1)}, u32[]{:S(2)}, u32[]{:S(2)}) collective-permute-start(bf16[256,896]{1,0:T(8,128)(2,1)} %get-tuple-element.131.msg_own), channel_id=1, source_target_pairs={{0,1},{1,2},{2,3},{4,5},{5,6},{6,7},{8,9},{9,10},{10,11},{12,13},{... | collective-permute-start | bytes 1376264 | tf_op jit(solution)/shard_map/ppermute | solution.py:746
  39.5 1.3 collective-permute-start.3
  40.9 0.9 copy-done.19
  41.8 3.3 %grad_w_back.1 = (bf16[384,768]{1,0:T(8,128)(2,1)S(1)}, bf16[384,768]{1,0:T(8,128)(2,1)S(1)}, bf16[384,768]{1,0:T(8,128)(2,1)S(1)}, bf16[384,768]{1,0:T(8,128)(2,1)S(1)}) custom-call(s32[1]{0:T(128)} %bitcast.6.d_ref, bf16[256,4992]{1,0:T(8,128)(2,1)S(1)} %get-tuple-element.122.acts_ref.hid.acts.ctx, ...), custom_call_target="tpu_custom_call" | custom-call | flops 3000000 | bytes 30000 | tf_op jit(solution)/shard_map/grad_w_back/pallas_call | solution.py:849
  45.1 1.7 %collective-permute-start.10 = (bf16[384,768]{1,0:T(8,128)(2,1)S(1)}, bf16[384,768]{1,0:T(8,128)(2,1)S(1)}, u32[]{:S(2)}, u32[]{:S(2)}) collective-permute-start(bf16[384,768]{1,0:T(8,128)(2,1)S(1)} %get-tuple-element.153), channel_id=1, source_target_pairs={{0,8},{1,9},{2,10},{3,11},{4,12},{5,13},{6,14},{7,15},{8,0},{9,1},... | collective-permute-start | bytes 1769480 | tf_op jit(solution)/shard_map/ppermute | solution.py:618
  46.8 1.5 %collective-permute-start.9 = (bf16[384,768]{1,0:T(8,128)(2,1)S(1)}, bf16[384,768]{1,0:T(8,128)(2,1)S(1)}, u32[]{:S(2)}, u32[]{:S(2)}) collective-permute-start(bf16[384,768]{1,0:T(8,128)(2,1)S(1)} %get-tuple-element.151), channel_id=1, source_target_pairs={{0,4},{1,5},{2,6},{3,7},{4,0},{5,1},{6,2},{7,3},{8,12},{9,13},{10,... | collective-permute-start | bytes 1769480 | tf_op jit(solution)/shard_map/ppermute | solution.py:618
  48.4 3.1 %grad_w_in.1 = (bf16[384,768]{1,0:T(8,128)(2,1)S(1)}, bf16[384,768]{1,0:T(8,128)(2,1)S(1)}, bf16[384,768]{1,0:T(8,128)(2,1)S(1)}, bf16[384,768]{1,0:T(8,128)(2,1)S(1)}) custom-call(s32[1]{0:T(128)} %bitcast.6.d_ref, bf16[256,4992]{1,0:T(8,128)(2,1)S(1)} %get-tuple-element.122.acts_ref.hid.acts.ctx, ...), custom_call_target="tpu_custom_call" | custom-call | flops 4000000 | bytes 40000 | tf_op jit(solution)/shard_map/grad_w_in/pallas_call | solution.py:866
  51.5 3.3 %collective-permute-start.6 = (bf16[384,768]{1,0:T(8,128)(2,1)S(1)}, bf16[384,768]{1,0:T(8,128)(2,1)S(1)}, u32[]{:S(2)}, u32[]{:S(2)}) collective-permute-start(bf16[384,768]{1,0:T(8,128)(2,1)S(1)} %get-tuple-element.145), channel_id=1, source_target_pairs={{0,2},{1,3},{2,0},{3,1},{4,6},{5,7},{6,4},{7,5},{8,10},{9,11},{10,... | collective-permute-start | bytes 1769480 | tf_op jit(solution)/shard_map/ppermute | solution.py:618
  54.8 0.4 collective-permute-start.7
  55.3 10.4 %attend_backward.1 = (bf16[256,2304]{1,0:T(8,128)(2,1)S(1)}, bf16[256,1152]{1,0:T(8,128)(2,1)S(1)}, bf16[144,1152]{1,0:T(8,128)(2,1)S(1)}, bf16[128,1152]{1,0:T(8,128)(2,1)S(1)}, f32[16,768]{1,0:T(8,128)S(1)}) custom-call(s32[1]{0:T(128)} %bitcast.me_ref, f32[2,128,384]{2,1,0:T(8,128)S(1)} %copy-done.11, f32[2,128,384]{2,1,0:T(8,128)S(1)} %copy-done.16, ...), custom_call_target="tpu_custom_call" | custom-call | flops 11000000 | bytes 110000 | tf_op jit(solution)/shard_map/attend_backward/pallas_call | solution.py:885
  65.8 0.3 add_back_0.1
  66.0 0.3 collective-permute-start.14
  66.3 0.3 collective-permute-start.15
  66.6 0.1 pad_add_fusion.1.ids_ref
  66.7 1.5 %collective-permute-done.15.peer2 = bf16[128,1152]{1,0:T(8,128)(2,1)S(1)} collective-permute-done((bf16[128,1152]{1,0:T(8,128)(2,1)S(1)}, bf16[128,1152]{1,0:T(8,128)(2,1)S(1)}, u32[]{:S(2)}, u32[]{:S(2)}) %collective-permute-start.15) | collective-permute-done | bytes 294944 | tf_op jit(solution)/shard_map/ppermute | solution.py:618
  68.2 3.2 %grad_w_qkv_out.1 = (bf16[384,768]{1,0:T(8,128)(2,1)S(1)}, bf16[400,768]{1,0:T(8,128)(2,1)S(1)}, bf16[384,768]{1,0:T(8,128)(2,1)S(1)}, bf16[384,768]{1,0:T(8,128)(2,1)S(1)}, f32[16,768]{1,0:T(8,128)S(1)}) custom-call(s32[2]{0:T(128)S(1)} %pad_add_fusion.1.ids_ref, bf16[256,768]{1,0:T(8,128)(2,1)S(1)} %bitcast.14, bf16[256,768]{1,0:T(8,128)(2,1)S(1)} %copy-done.7, ...), custom_call_target="tpu_custom_call" | custom-call | flops 3000000 | bytes 30000 | tf_op jit(solution)/shard_map/grad_w_qkv_out/pallas_call | solution.py:909
  71.4 1.5 %collective-permute-start.19 = (bf16[400,768]{1,0:T(8,128)(2,1)S(1)}, bf16[400,768]{1,0:T(8,128)(2,1)S(1)}, u32[]{:S(2)}, u32[]{:S(2)}) collective-permute-start(bf16[400,768]{1,0:T(8,128)(2,1)S(1)} %get-tuple-element.177), channel_id=1, source_target_pairs={{0,2},{1,3},{2,0},{3,1},{4,6},{5,7},{6,4},{7,5},{8,10},{9,11},{10,... | collective-permute-start | bytes 1843208 | tf_op jit(solution)/shard_map/ppermute | solution.py:618
  72.9 0.5 collective-permute-start.11
  73.4 1.5 %collective-permute-start.12 = (bf16[192,768]{1,0:T(8,128)(2,1)S(1)}, bf16[192,768]{1,0:T(8,128)(2,1)S(1)}, u32[]{:S(2)}, u32[]{:S(2)}) collective-permute-start(bf16[192,768]{1,0:T(8,128)(2,1)S(1)} %get-tuple-element.158), channel_id=1, source_target_pairs={{0,4},{1,5},{2,6},{3,7},{4,0},{5,1},{6,2},{7,3},{8,12},{9,13},{10,... | collective-permute-start | bytes 884744 | tf_op jit(solution)/shard_map/ppermute | solution.py:618
  74.9 0.3 add_in_0.1
  75.2 1.6 %collective-permute-start.20 = (bf16[384,768]{1,0:T(8,128)(2,1)S(1)}, bf16[384,768]{1,0:T(8,128)(2,1)S(1)}, u32[]{:S(2)}, u32[]{:S(2)}) collective-permute-start(bf16[384,768]{1,0:T(8,128)(2,1)S(1)} %get-tuple-element.181), channel_id=1, source_target_pairs={{0,8},{1,9},{2,10},{3,11},{4,12},{5,13},{6,14},{7,15},{8,0},{9,1},... | collective-permute-start | bytes 1769480 | tf_op jit(solution)/shard_map/ppermute | solution.py:618
  76.8 0.5 collective-permute-start.8
  77.3 5.5 %collective-permute-done.11.got0 = bf16[192,768]{1,0:T(8,128)(2,1)S(1)} collective-permute-done((bf16[192,768]{1,0:T(8,128)(2,1)S(1)}, bf16[192,768]{1,0:T(8,128)(2,1)S(1)}, u32[]{:S(2)}, u32[]{:S(2)}) %collective-permute-start.11) | collective-permute-done | bytes 294944 | tf_op jit(solution)/shard_map/ppermute | solution.py:618
  82.8 0.6 collective-permute-start.16
  83.4 0.1 add_back_1.1
  83.5 1.5 %collective-permute-start.13 = (bf16[192,768]{1,0:T(8,128)(2,1)S(1)}, bf16[192,768]{1,0:T(8,128)(2,1)S(1)}, u32[]{:S(2)}, u32[]{:S(2)}) collective-permute-start(bf16[192,768]{1,0:T(8,128)(2,1)S(1)} %get-tuple-element.161), channel_id=1, source_target_pairs={{0,2},{1,3},{2,0},{3,1},{4,6},{5,7},{6,4},{7,5},{8,10},{9,11},{10,... | collective-permute-start | bytes 884744 | tf_op jit(solution)/shard_map/ppermute | solution.py:618
  85.0 15.9 %collective-permute-done.8.got0 = bf16[192,768]{1,0:T(8,128)(2,1)S(1)} collective-permute-done((bf16[192,768]{1,0:T(8,128)(2,1)S(1)}, bf16[192,768]{1,0:T(8,128)(2,1)S(1)}, u32[]{:S(2)}, u32[]{:S(2)}) %collective-permute-start.8) | collective-permute-done | bytes 294944 | tf_op jit(solution)/shard_map/ppermute | solution.py:618
  101.0 0.1 add_in_1.1
  101.2 0.3 add_qkv_0.1
  101.5 0.5 collective-permute-start.21
  102.0 1.5 %collective-permute-start.18 = (bf16[192,768]{1,0:T(8,128)(2,1)S(1)}, bf16[192,768]{1,0:T(8,128)(2,1)S(1)}, u32[]{:S(2)}, u32[]{:S(2)}) collective-permute-start(bf16[192,768]{1,0:T(8,128)(2,1)S(1)} %get-tuple-element.175), channel_id=1, source_target_pairs={{0,4},{1,5},{2,6},{3,7},{4,0},{5,1},{6,2},{7,3},{8,12},{9,13},{10,... | collective-permute-start | bytes 884744 | tf_op jit(solution)/shard_map/ppermute | solution.py:618
  103.5 1.4 %collective-permute-start.22 = (bf16[192,768]{1,0:T(8,128)(2,1)S(1)}, bf16[192,768]{1,0:T(8,128)(2,1)S(1)}, u32[]{:S(2)}, u32[]{:S(2)}) collective-permute-start(bf16[192,768]{1,0:T(8,128)(2,1)S(1)} %get-tuple-element.191), channel_id=1, source_target_pairs={{0,2},{1,3},{2,0},{3,1},{4,6},{5,7},{6,4},{7,5},{8,10},{9,11},{10,... | collective-permute-start | bytes 884744 | tf_op jit(solution)/shard_map/ppermute | solution.py:618
  104.9 2.6 %collective-permute-start.17 = (bf16[96,768]{1,0:T(8,128)(2,1)S(1)}, bf16[96,768]{1,0:T(8,128)(2,1)S(1)}, u32[]{:S(2)}, u32[]{:S(2)}) collective-permute-start(bf16[96,768]{1,0:T(8,128)(2,1)S(1)} %get-tuple-element.174), channel_id=1, source_target_pairs={{0,16},{1,17},{2,18},{3,19},{4,20},{5,21},{6,22},{7,23},{8,24},{9,... | collective-permute-start | bytes 442376 | tf_op jit(solution)/shard_map/ppermute | solution.py:618
  107.5 2.5 %collective-permute-done.18.got = bf16[192,768]{1,0:T(8,128)(2,1)S(1)} collective-permute-done((bf16[192,768]{1,0:T(8,128)(2,1)S(1)}, bf16[192,768]{1,0:T(8,128)(2,1)S(1)}, u32[]{:S(2)}, u32[]{:S(2)}) %collective-permute-start.18) | collective-permute-done | bytes 294944 | tf_op jit(solution)/shard_map/ppermute | solution.py:618
  110.0 2.6 %collective-permute-start.24 = (bf16[96,768]{1,0:T(8,128)(2,1)S(1)}, bf16[96,768]{1,0:T(8,128)(2,1)S(1)}, u32[]{:S(2)}, u32[]{:S(2)}) collective-permute-start(bf16[96,768]{1,0:T(8,128)(2,1)S(1)} %get-tuple-element.197), channel_id=1, source_target_pairs={{0,16},{1,17},{2,18},{3,19},{4,20},{5,21},{6,22},{7,23},{8,24},{9,... | collective-permute-start | bytes 442376 | tf_op jit(solution)/shard_map/ppermute | solution.py:618
  112.6 2.1 %collective-permute-done.21.got0 = bf16[208,768]{1,0:T(8,128)(2,1)S(1)} collective-permute-done((bf16[208,768]{1,0:T(8,128)(2,1)S(1)}, bf16[208,768]{1,0:T(8,128)(2,1)S(1)}, u32[]{:S(2)}, u32[]{:S(2)}) %collective-permute-start.21) | collective-permute-done | bytes 319520 | tf_op jit(solution)/shard_map/ppermute | solution.py:618
  114.8 0.1 add_qkv_1.1
  114.9 1.6 %collective-permute-start.23 = (bf16[208,768]{1,0:T(8,128)(2,1)S(1)}, bf16[208,768]{1,0:T(8,128)(2,1)S(1)}, u32[]{:S(2)}, u32[]{:S(2)}) collective-permute-start(bf16[208,768]{1,0:T(8,128)(2,1)S(1)} %get-tuple-element.195), channel_id=1, source_target_pairs={{0,4},{1,5},{2,6},{3,7},{4,0},{5,1},{6,2},{7,3},{8,12},{9,13},{10,... | collective-permute-start | bytes 958472 | tf_op jit(solution)/shard_map/ppermute | solution.py:618
  116.6 1.1 fusion
  117.7 0.3 add_back_3.1
  118.0 2.7 %collective-permute-done.24.got = bf16[96,768]{1,0:T(8,128)(2,1)S(1)} collective-permute-done((bf16[96,768]{1,0:T(8,128)(2,1)S(1)}, bf16[96,768]{1,0:T(8,128)(2,1)S(1)}, u32[]{:S(2)}, u32[]{:S(2)}) %collective-permute-start.24) | collective-permute-done | bytes 147488 | tf_op jit(solution)/shard_map/ppermute | solution.py:618
  120.6 0.7 add_in_3.1
  121.4 0.6 collective-permute-done.23.got
  122.0 0.1 add_qkv_2.1
  122.2 0.8 add_convert_fusion
  123.0 0.9 copy.32
  123.9 7.3 %collective-permute-done.25.got = bf16[112,768]{1,0:T(8,128)(2,1)S(1)} collective-permute-done((bf16[112,768]{1,0:T(8,128)(2,1)S(1)}, bf16[112,768]{1,0:T(8,128)(2,1)S(1)}, u32[]{:S(2)}, u32[]{:S(2)}) %collective-permute-start.25) | collective-permute-done | bytes 172064 | tf_op jit(solution)/shard_map/ppermute | solution.py:618
  131.2 0.8 add_qkv_3.1
  131.9 0.7 slice_reduce_fusion
  132.6 0.6 reshape.55
  (81 shorter events, 0.5 us)
Async XLA Ops:
  0.6 11.4 %copy-start.29 = (f32[768]{0:T(1024)S(1)}, f32[768]{0:T(1024)}, u32[]{:S(2)}) copy-start(f32[768]{0:T(1024)} %param.26) | copy-start | bytes 9220
  0.7 11.4 %copy-start.28 = (f32[768]{0:T(1024)S(1)}, f32[768]{0:T(1024)}, u32[]{:S(2)}) copy-start(f32[768]{0:T(1024)} %param.30) | copy-start | bytes 9220
  0.7 11.4 %copy-start.27 = (f32[768]{0:T(1024)S(1)}, f32[768]{0:T(1024)}, u32[]{:S(2)}) copy-start(f32[768]{0:T(1024)} %param.31) | copy-start | bytes 9220
  0.7 11.4 %copy-start.26 = (f32[768]{0:T(1024)S(1)}, f32[768]{0:T(1024)}, u32[]{:S(2)}) copy-start(f32[768]{0:T(1024)} %param.32) | copy-start | bytes 9220
  0.7 11.5 %copy-start.22 = (f32[3072]{0:T(1024)S(1)}, f32[3072]{0:T(1024)}, u32[]{:S(2)}) copy-start(f32[3072]{0:T(1024)} %b_in_ref.1) | copy-start | bytes 36868
  0.7 11.5 %collective-permute-start = (bf16[256,768]{1,0:T(8,128)(2,1)}, bf16[256,768]{1,0:T(8,128)(2,1)S(1)}, u32[]{:S(2)}, u32[]{:S(2)}) collective-permute-start(bf16[256,768]{1,0:T(8,128)(2,1)} %bitcast.10), channel_id=1, source_target_pairs={{0,1},{1,2},{2,3},{4,5},{5,6},{6,7},{8,9},{9,10},{10,11},{12,13},{... | collective-permute-start | bytes 1179656 | tf_op jit(solution)/shard_map/ppermute | solution.py:746
  3.2 9.0 %collective-permute-start.1 = (bf16[256,768]{1,0:T(8,128)(2,1)}, bf16[256,768]{1,0:T(8,128)(2,1)S(1)}, u32[]{:S(2)}, u32[]{:S(2)}) collective-permute-start(bf16[256,768]{1,0:T(8,128)(2,1)} %bitcast.11), channel_id=1, source_target_pairs={{1,0},{2,1},{3,2},{5,4},{6,5},{7,6},{9,8},{10,9},{11,10},{13,12},{... | collective-permute-start | bytes 1179656 | tf_op jit(solution)/shard_map/ppermute | solution.py:746
  8.0 1.0 copy-start.2
  9.0 3.2 %copy-start.12 = (bf16[768,768]{1,0:T(8,128)(2,1)S(1)}, bf16[768,768]{1,0:T(8,128)(2,1)}, u32[]{:S(2)}) copy-start(bf16[768,768]{1,0:T(8,128)(2,1)} %wout_hbm.1) | copy-start | bytes 3538948
  9.0 3.2 %copy-start.17 = (bf16[2,128,768]{2,1,0:T(8,128)(2,1)S(1)}, bf16[2,128,768]{2,1,0:T(8,128)(2,1)}, u32[]{:S(2)}) copy-start(bf16[2,128,768]{2,1,0:T(8,128)(2,1)} %param.33) | copy-start | bytes 1179652
  12.1 13.9 %copy-start = (bf16[256,2304]{1,0:T(8,128)(2,1)}, bf16[256,2304]{1,0:T(8,128)(2,1)S(1)}, u32[]{:S(2)}) copy-start(bf16[256,2304]{1,0:T(8,128)(2,1)S(1)} %get-tuple-element.113.own_ref) | copy-start | bytes 3538948
  12.1 13.9 %copy-start.10 = (f32[2,128,384]{2,1,0:T(8,128)}, f32[2,128,384]{2,1,0:T(8,128)S(1)}, u32[]{:S(2)}) copy-start(f32[2,128,384]{2,1,0:T(8,128)S(1)} %get-tuple-element.114.mask_ref) | copy-start | bytes 1179652
  12.2 13.9 %copy-start.15 = (f32[2,128,384]{2,1,0:T(8,128)}, f32[2,128,384]{2,1,0:T(8,128)S(1)}, u32[]{:S(2)}) copy-start(f32[2,128,384]{2,1,0:T(8,128)S(1)} %get-tuple-element.128.mask_t_ref) | copy-start | bytes 1179652
  12.2 13.9 %copy-start.6 = (bf16[256,768]{1,0:T(8,128)(2,1)}, bf16[256,768]{1,0:T(8,128)(2,1)S(1)}, u32[]{:S(2)}) copy-start(bf16[256,768]{1,0:T(8,128)(2,1)S(1)} %collective-permute-done.tok_prev) | copy-start | bytes 1179652
  12.2 13.9 %copy-start.8 = (bf16[256,768]{1,0:T(8,128)(2,1)}, bf16[256,768]{1,0:T(8,128)(2,1)S(1)}, u32[]{:S(2)}) copy-start(bf16[256,768]{1,0:T(8,128)(2,1)S(1)} %collective-permute-done.1.tok_next) | copy-start | bytes 1179652
  26.1 8.7 %copy-start.4 = (bf16[2,256,2304]{2,1,0:T(8,128)(2,1)}, bf16[2,256,2304]{2,1,0:T(8,128)(2,1)S(1)}, u32[]{:S(2)}) copy-start(bf16[2,256,2304]{2,1,0:T(8,128)(2,1)S(1)} %get-tuple-element.129.near_ref) | copy-start | bytes 7077892
  26.1 8.7 %copy-start.18 = (bf16[256,384]{1,0:T(8,128)(2,1)}, bf16[256,384]{1,0:T(8,128)(2,1)S(1)}, u32[]{:S(2)}) copy-start(bf16[256,384]{1,0:T(8,128)(2,1)S(1)} %get-tuple-element.134.feed) | copy-start | bytes 589828
  26.1 8.7 %copy-start.23 = (f32[3,768]{1,0:T(4,128)}, f32[3,768]{1,0:T(4,128)S(1)}, u32[]{:S(2)}) copy-start(f32[3,768]{1,0:T(4,128)S(1)} %get-tuple-element.141.small1_ref) | copy-start | bytes 27652
  26.1 14.7 %collective-permute-start.4 = (bf16[256,4992]{1,0:T(8,128)(2,1)S(1)}, bf16[256,4992]{1,0:T(8,128)(2,1)}, u32[]{:S(2)}, u32[]{:S(2)}) collective-permute-start(bf16[256,4992]{1,0:T(8,128)(2,1)S(1)} %get-tuple-element.122.acts_ref.hid.acts.ctx), channel_id=1, source_target_pairs={{0,1},{1,0},{2,3},{3,2},{4,5},{5,4},{6,7},{7,6},{8,9},{9,8},{10,11... | collective-permute-start | bytes 7667720 | tf_op jit(solution)/shard_map/ppermute | solution.py:618
  34.8 1.0 copy-start.13
  35.8 0.6 copy-start.20
  36.4 12.0 %collective-permute-start.5 = (bf16[256,1920]{1,0:T(8,128)(2,1)}, bf16[256,1920]{1,0:T(8,128)(2,1)}, u32[]{:S(2)}, u32[]{:S(2)}) collective-permute-start(bf16[256,1920]{1,0:T(8,128)(2,1)} %get-tuple-element.137), channel_id=1, source_target_pairs={{0,1},{1,0},{2,3},{3,2},{4,5},{5,4},{6,7},{7,6},{8,9},{9,8},{10,11... | collective-permute-start | bytes 2949128 | tf_op jit(solution)/shard_map/ppermute | solution.py:618
  36.4 11.9 %collective-permute-start.2 = (bf16[256,896]{1,0:T(8,128)(2,1)}, bf16[256,896]{1,0:T(8,128)(2,1)}, u32[]{:S(2)}, u32[]{:S(2)}) collective-permute-start(bf16[256,896]{1,0:T(8,128)(2,1)} %get-tuple-element.131.msg_own), channel_id=1, source_target_pairs={{0,1},{1,2},{2,3},{4,5},{5,6},{6,7},{8,9},{9,10},{10,11},{12,13},{... | collective-permute-start | bytes 1376264 | tf_op jit(solution)/shard_map/ppermute | solution.py:746
  39.5 8.8 %collective-permute-start.3 = (bf16[256,896]{1,0:T(8,128)(2,1)}, bf16[256,896]{1,0:T(8,128)(2,1)}, u32[]{:S(2)}, u32[]{:S(2)}) collective-permute-start(bf16[256,896]{1,0:T(8,128)(2,1)} %get-tuple-element.131.msg_own), channel_id=1, source_target_pairs={{1,0},{2,1},{3,2},{5,4},{6,5},{7,6},{9,8},{10,9},{11,10},{13,12},{... | collective-permute-start | bytes 1376264 | tf_op jit(solution)/shard_map/ppermute | solution.py:746
  40.8 0.9 copy-start.19
  45.1 20.6 %collective-permute-start.10 = (bf16[384,768]{1,0:T(8,128)(2,1)S(1)}, bf16[384,768]{1,0:T(8,128)(2,1)S(1)}, u32[]{:S(2)}, u32[]{:S(2)}) collective-permute-start(bf16[384,768]{1,0:T(8,128)(2,1)S(1)} %get-tuple-element.153), channel_id=1, source_target_pairs={{0,8},{1,9},{2,10},{3,11},{4,12},{5,13},{6,14},{7,15},{8,0},{9,1},... | collective-permute-start | bytes 1769480 | tf_op jit(solution)/shard_map/ppermute | solution.py:618
  46.8 19.0 %collective-permute-start.9 = (bf16[384,768]{1,0:T(8,128)(2,1)S(1)}, bf16[384,768]{1,0:T(8,128)(2,1)S(1)}, u32[]{:S(2)}, u32[]{:S(2)}) collective-permute-start(bf16[384,768]{1,0:T(8,128)(2,1)S(1)} %get-tuple-element.151), channel_id=1, source_target_pairs={{0,4},{1,5},{2,6},{3,7},{4,0},{5,1},{6,2},{7,3},{8,12},{9,13},{10,... | collective-permute-start | bytes 1769480 | tf_op jit(solution)/shard_map/ppermute | solution.py:618
  48.3 6.9 %copy-start.1 = (bf16[256,2304]{1,0:T(8,128)(2,1)S(1)}, bf16[256,2304]{1,0:T(8,128)(2,1)}, u32[]{:S(2)}) copy-start(bf16[256,2304]{1,0:T(8,128)(2,1)} %copy-done) | copy-start | bytes 3538948
  48.3 6.9 %copy-start.5 = (bf16[2,256,2304]{2,1,0:T(8,128)(2,1)S(1)}, bf16[2,256,2304]{2,1,0:T(8,128)(2,1)}, u32[]{:S(2)}) copy-start(bf16[2,256,2304]{2,1,0:T(8,128)(2,1)} %copy-done.4) | copy-start | bytes 7077892
  48.3 6.9 %copy-start.11 = (f32[2,128,384]{2,1,0:T(8,128)S(1)}, f32[2,128,384]{2,1,0:T(8,128)}, u32[]{:S(2)}) copy-start(f32[2,128,384]{2,1,0:T(8,128)} %copy-done.10) | copy-start | bytes 1179652
  48.3 6.9 %copy-start.16 = (f32[2,128,384]{2,1,0:T(8,128)S(1)}, f32[2,128,384]{2,1,0:T(8,128)}, u32[]{:S(2)}) copy-start(f32[2,128,384]{2,1,0:T(8,128)} %copy-done.15) | copy-start | bytes 1179652
  48.3 6.9 %copy-start.21 = (f32[7,768]{1,0:T(8,128)S(1)}, f32[7,768]{1,0:T(8,128)}, u32[]{:S(2)}) copy-start(f32[7,768]{1,0:T(8,128)} %copy-done.20) | copy-start | bytes 64516
  48.3 6.9 %copy-start.24 = (f32[3,768]{1,0:T(4,128)S(1)}, f32[3,768]{1,0:T(4,128)}, u32[]{:S(2)}) copy-start(f32[3,768]{1,0:T(4,128)} %copy-done.23) | copy-start | bytes 27652
  51.5 23.5 %collective-permute-start.6 = (bf16[384,768]{1,0:T(8,128)(2,1)S(1)}, bf16[384,768]{1,0:T(8,128)(2,1)S(1)}, u32[]{:S(2)}, u32[]{:S(2)}) collective-permute-start(bf16[384,768]{1,0:T(8,128)(2,1)S(1)} %get-tuple-element.145), channel_id=1, source_target_pairs={{0,2},{1,3},{2,0},{3,1},{4,6},{5,7},{6,4},{7,5},{8,10},{9,11},{10,... | collective-permute-start | bytes 1769480 | tf_op jit(solution)/shard_map/ppermute | solution.py:618
  54.8 20.1 %collective-permute-start.7 = (bf16[384,768]{1,0:T(8,128)(2,1)S(1)}, bf16[384,768]{1,0:T(8,128)(2,1)S(1)}, u32[]{:S(2)}, u32[]{:S(2)}) collective-permute-start(bf16[384,768]{1,0:T(8,128)(2,1)S(1)} %get-tuple-element.147), channel_id=1, source_target_pairs={{0,8},{1,9},{2,10},{3,11},{4,12},{5,13},{6,14},{7,15},{8,0},{9,1},... | collective-permute-start | bytes 1769480 | tf_op jit(solution)/shard_map/ppermute | solution.py:618
  65.7 2.5 %copy-start.3 = (bf16[2,128,768]{2,1,0:T(8,128)(2,1)S(1)}, bf16[2,128,768]{2,1,0:T(8,128)(2,1)}, u32[]{:S(2)}) copy-start(bf16[2,128,768]{2,1,0:T(8,128)(2,1)} %param.17) | copy-start | bytes 1179652
  65.7 2.5 %copy-start.7 = (bf16[256,768]{1,0:T(8,128)(2,1)S(1)}, bf16[256,768]{1,0:T(8,128)(2,1)}, u32[]{:S(2)}) copy-start(bf16[256,768]{1,0:T(8,128)(2,1)} %copy-done.6) | copy-start | bytes 1179652
  65.7 2.4 %copy-start.9 = (bf16[256,768]{1,0:T(8,128)(2,1)S(1)}, bf16[256,768]{1,0:T(8,128)(2,1)}, u32[]{:S(2)}) copy-start(bf16[256,768]{1,0:T(8,128)(2,1)} %copy-done.8) | copy-start | bytes 1179652
  66.0 2.1 %collective-permute-start.14 = (bf16[144,1152]{1,0:T(8,128)(2,1)S(1)}, bf16[144,1152]{1,0:T(8,128)(2,1)S(1)}, u32[]{:S(2)}, u32[]{:S(2)}) collective-permute-start(bf16[144,1152]{1,0:T(8,128)(2,1)S(1)} %get-tuple-element.163), channel_id=1, source_target_pairs={{0,1},{1,0},{2,3},{3,2},{4,5},{5,4},{6,7},{7,6},{8,9},{9,8},{10,11... | collective-permute-start | bytes 995336 | tf_op jit(solution)/shard_map/ppermute | solution.py:618
  66.3 1.9 %collective-permute-start.15 = (bf16[128,1152]{1,0:T(8,128)(2,1)S(1)}, bf16[128,1152]{1,0:T(8,128)(2,1)S(1)}, u32[]{:S(2)}, u32[]{:S(2)}) collective-permute-start(bf16[128,1152]{1,0:T(8,128)(2,1)S(1)} %get-tuple-element.164), channel_id=1, source_target_pairs={{0,1},{1,0},{2,3},{3,2},{4,5},{5,4},{6,7},{7,6},{8,9},{9,8},{10,11... | collective-permute-start | bytes 884744 | tf_op jit(solution)/shard_map/ppermute | solution.py:618
  71.4 29.8 %collective-permute-start.19 = (bf16[400,768]{1,0:T(8,128)(2,1)S(1)}, bf16[400,768]{1,0:T(8,128)(2,1)S(1)}, u32[]{:S(2)}, u32[]{:S(2)}) collective-permute-start(bf16[400,768]{1,0:T(8,128)(2,1)S(1)} %get-tuple-element.177), channel_id=1, source_target_pairs={{0,2},{1,3},{2,0},{3,1},{4,6},{5,7},{6,4},{7,5},{8,10},{9,11},{10,... | collective-permute-start | bytes 1843208 | tf_op jit(solution)/shard_map/ppermute | solution.py:618
  72.9 9.9 %collective-permute-start.11 = (bf16[192,768]{1,0:T(8,128)(2,1)S(1)}, bf16[192,768]{1,0:T(8,128)(2,1)S(1)}, u32[]{:S(2)}, u32[]{:S(2)}) collective-permute-start(bf16[192,768]{1,0:T(8,128)(2,1)S(1)} %get-tuple-element.156), channel_id=1, source_target_pairs={{0,8},{1,9},{2,10},{3,11},{4,12},{5,13},{6,14},{7,15},{8,0},{9,1},... | collective-permute-start | bytes 884744 | tf_op jit(solution)/shard_map/ppermute | solution.py:618
  73.4 10.0 %collective-permute-start.12 = (bf16[192,768]{1,0:T(8,128)(2,1)S(1)}, bf16[192,768]{1,0:T(8,128)(2,1)S(1)}, u32[]{:S(2)}, u32[]{:S(2)}) collective-permute-start(bf16[192,768]{1,0:T(8,128)(2,1)S(1)} %get-tuple-element.158), channel_id=1, source_target_pairs={{0,4},{1,5},{2,6},{3,7},{4,0},{5,1},{6,2},{7,3},{8,12},{9,13},{10,... | collective-permute-start | bytes 884744 | tf_op jit(solution)/shard_map/ppermute | solution.py:618
  75.2 26.0 %collective-permute-start.20 = (bf16[384,768]{1,0:T(8,128)(2,1)S(1)}, bf16[384,768]{1,0:T(8,128)(2,1)S(1)}, u32[]{:S(2)}, u32[]{:S(2)}) collective-permute-start(bf16[384,768]{1,0:T(8,128)(2,1)S(1)} %get-tuple-element.181), channel_id=1, source_target_pairs={{0,8},{1,9},{2,10},{3,11},{4,12},{5,13},{6,14},{7,15},{8,0},{9,1},... | collective-permute-start | bytes 1769480 | tf_op jit(solution)/shard_map/ppermute | solution.py:618
  76.8 24.1 %collective-permute-start.8 = (bf16[192,768]{1,0:T(8,128)(2,1)S(1)}, bf16[192,768]{1,0:T(8,128)(2,1)S(1)}, u32[]{:S(2)}, u32[]{:S(2)}) collective-permute-start(bf16[192,768]{1,0:T(8,128)(2,1)S(1)} %get-tuple-element.148), channel_id=1, source_target_pairs={{0,8},{1,9},{2,10},{3,11},{4,12},{5,13},{6,14},{7,15},{8,0},{9,1},... | collective-permute-start | bytes 884744 | tf_op jit(solution)/shard_map/ppermute | solution.py:618
  82.8 18.2 %collective-permute-start.16 = (bf16[192,768]{1,0:T(8,128)(2,1)S(1)}, bf16[192,768]{1,0:T(8,128)(2,1)S(1)}, u32[]{:S(2)}, u32[]{:S(2)}) collective-permute-start(bf16[192,768]{1,0:T(8,128)(2,1)S(1)} %get-tuple-element.171), channel_id=1, source_target_pairs={{0,2},{1,3},{2,0},{3,1},{4,6},{5,7},{6,4},{7,5},{8,10},{9,11},{10,... | collective-permute-start | bytes 884744 | tf_op jit(solution)/shard_map/ppermute | solution.py:618
  83.5 17.6 %collective-permute-start.13 = (bf16[192,768]{1,0:T(8,128)(2,1)S(1)}, bf16[192,768]{1,0:T(8,128)(2,1)S(1)}, u32[]{:S(2)}, u32[]{:S(2)}) collective-permute-start(bf16[192,768]{1,0:T(8,128)(2,1)S(1)} %get-tuple-element.161), channel_id=1, source_target_pairs={{0,2},{1,3},{2,0},{3,1},{4,6},{5,7},{6,4},{7,5},{8,10},{9,11},{10,... | collective-permute-start | bytes 884744 | tf_op jit(solution)/shard_map/ppermute | solution.py:618
  101.1 15.5 %copy-start.25 = (bf16[768,2304]{1,0:T(8,128)(2,1)S(1)}, bf16[768,2304]{1,0:T(8,128)(2,1)}, u32[]{:S(2)}) copy-start(bf16[768,2304]{1,0:T(8,128)(2,1)} %wqkv_hbm.1) | copy-start | bytes 10616836
  101.5 13.3 %collective-permute-start.21 = (bf16[208,768]{1,0:T(8,128)(2,1)S(1)}, bf16[208,768]{1,0:T(8,128)(2,1)S(1)}, u32[]{:S(2)}, u32[]{:S(2)}) collective-permute-start(bf16[208,768]{1,0:T(8,128)(2,1)S(1)} %get-tuple-element.185), channel_id=1, source_target_pairs={{0,8},{1,9},{2,10},{3,11},{4,12},{5,13},{6,14},{7,15},{8,0},{9,1},... | collective-permute-start | bytes 958472 | tf_op jit(solution)/shard_map/ppermute | solution.py:618
  102.0 7.9 %collective-permute-start.18 = (bf16[192,768]{1,0:T(8,128)(2,1)S(1)}, bf16[192,768]{1,0:T(8,128)(2,1)S(1)}, u32[]{:S(2)}, u32[]{:S(2)}) collective-permute-start(bf16[192,768]{1,0:T(8,128)(2,1)S(1)} %get-tuple-element.175), channel_id=1, source_target_pairs={{0,4},{1,5},{2,6},{3,7},{4,0},{5,1},{6,2},{7,3},{8,12},{9,13},{10,... | collective-permute-start | bytes 884744 | tf_op jit(solution)/shard_map/ppermute | solution.py:618
  103.5 11.3 %collective-permute-start.22 = (bf16[192,768]{1,0:T(8,128)(2,1)S(1)}, bf16[192,768]{1,0:T(8,128)(2,1)S(1)}, u32[]{:S(2)}, u32[]{:S(2)}) collective-permute-start(bf16[192,768]{1,0:T(8,128)(2,1)S(1)} %get-tuple-element.191), channel_id=1, source_target_pairs={{0,2},{1,3},{2,0},{3,1},{4,6},{5,7},{6,4},{7,5},{8,10},{9,11},{10,... | collective-permute-start | bytes 884744 | tf_op jit(solution)/shard_map/ppermute | solution.py:618
  104.9 12.8 %collective-permute-start.17 = (bf16[96,768]{1,0:T(8,128)(2,1)S(1)}, bf16[96,768]{1,0:T(8,128)(2,1)S(1)}, u32[]{:S(2)}, u32[]{:S(2)}) collective-permute-start(bf16[96,768]{1,0:T(8,128)(2,1)S(1)} %get-tuple-element.174), channel_id=1, source_target_pairs={{0,16},{1,17},{2,18},{3,19},{4,20},{5,21},{6,22},{7,23},{8,24},{9,... | collective-permute-start | bytes 442376 | tf_op jit(solution)/shard_map/ppermute | solution.py:618
  110.0 10.6 %collective-permute-start.24 = (bf16[96,768]{1,0:T(8,128)(2,1)S(1)}, bf16[96,768]{1,0:T(8,128)(2,1)S(1)}, u32[]{:S(2)}, u32[]{:S(2)}) collective-permute-start(bf16[96,768]{1,0:T(8,128)(2,1)S(1)} %get-tuple-element.197), channel_id=1, source_target_pairs={{0,16},{1,17},{2,18},{3,19},{4,20},{5,21},{6,22},{7,23},{8,24},{9,... | collective-permute-start | bytes 442376 | tf_op jit(solution)/shard_map/ppermute | solution.py:618
  114.9 7.1 %collective-permute-start.23 = (bf16[208,768]{1,0:T(8,128)(2,1)S(1)}, bf16[208,768]{1,0:T(8,128)(2,1)S(1)}, u32[]{:S(2)}, u32[]{:S(2)}) collective-permute-start(bf16[208,768]{1,0:T(8,128)(2,1)S(1)} %get-tuple-element.195), channel_id=1, source_target_pairs={{0,4},{1,5},{2,6},{3,7},{4,0},{5,1},{6,2},{7,3},{8,12},{9,13},{10,... | collective-permute-start | bytes 958472 | tf_op jit(solution)/shard_map/ppermute | solution.py:618
  116.6 5.6 %copy-start.14 = (f32[256,768]{1,0:T(8,128)S(1)}, f32[256,768]{1,0:T(8,128)}, u32[]{:S(2)}) copy-start(f32[256,768]{1,0:T(8,128)} %copy-done.13) | copy-start | bytes 2359300
  122.1 9.1 %collective-permute-start.25 = (bf16[112,768]{1,0:T(8,128)(2,1)S(1)}, bf16[112,768]{1,0:T(8,128)(2,1)S(1)}, u32[]{:S(2)}, u32[]{:S(2)}) collective-permute-start(bf16[112,768]{1,0:T(8,128)(2,1)S(1)} %get-tuple-element.204), channel_id=1, source_target_pairs={{0,16},{1,17},{2,18},{3,19},{4,20},{5,21},{6,22},{7,23},{8,24},{9,... | collective-permute-start | bytes 516104 | tf_op jit(solution)/shard_map/ppermute | solution.py:618

commit v3 on v2

--- a/solution.py
+++ b/solution.py
@@ -604,10 +604,15 @@
     elif kind == "in":
         refs[0][...] = total
     else:
-        sums_ref, qkv_ref, out_ref, total_ref = refs
+        sums_ref, qkv_ref, out_ref, inner_ref, *vectors = refs
         qkv_ref[...] = total[:, : qkv_ref.shape[1]]
         out_ref[...] = total[:, qkv_ref.shape[1] :]
-        step_sums(sums_ref, got, keep.shape[0], total_ref, None, 0)
+        width = sums_ref.shape[1]
+        sums = sums_ref[...] + read_sums(got, keep.shape[0], width)
+        for i in range(4):
+            inner_ref[i * width : (i + 1) * width] = sums[3 + i]
+        for row, ref in zip((0, 1, 2, 7, 8, 9, 10, 11), vectors):
+            ref[...] = sums[row]
 
 
 HALVING = {"back": (2, 3, 1, 4), "in": (1, 3, 2, 4), "qkv": (1, 3, 2, 4)}
@@ -643,7 +648,7 @@
         last = self.at > 1 and "last" in outs
         if last:
             kernel = functools.partial(last_step, self.kind)
-            shapes = tuple(shape_of(*dims, dtype=F32) for dims in outs["last"]) + sums
+            shapes = tuple(shape_of(*dims, dtype=F32) for dims in outs["last"])
         if self.sums is not None:
             operands.append(self.sums)
         result = pl.pallas_call(
@@ -655,12 +660,12 @@
             out_specs=(VMEM,) * len(shapes),
             compiler_params=params(12),
         )(*operands)
-        if self.sums is not None:
-            self.sums = result[-1]
         self.at += 1
         if last:
             self.result = result
             return
+        if self.sums is not None:
+            self.sums = result[-1]
         self.keeps = result[0 : len(shapes) - len(sums) : 2]
         sends = result[1 : len(shapes) - len(sums) : 2]
         bits = HALVING[self.kind]
@@ -950,7 +955,7 @@
         last = (
             ((ff // dp, small),),
             ((block_rows, wide),),
-            ((block_rows, qkv_block), (block_rows, small)),
+            ((block_rows, qkv_block), (block_rows, small), (ff,)) + ((width,),) * 8,
         )
         done = None
         for k in EVENTS if dp_bits == 3 else [0, 1, 2] * (dp_bits + 1):
@@ -965,7 +970,7 @@
             done = units[k]
         g_back = red_back.result[0]
         g_in = red_in.result[0]
-        g_qkv, g_out, sums = red_qkv.result
+        g_qkv, g_out, b_in_g, *vectors = red_qkv.result
     else:
 
         def by_x(v, w):
@@ -984,9 +989,9 @@
         grads = by_x(pile(qkv_keep, pile(qkv_peer[:loc], qkv_peer2)), qkv_block)
         g_qkv = plain_reduce(pile(flat, other), grads)
         sums = plain_sum(sums, 0)
-    b_back_g, gain2, shift2 = sums[0], sums[1], sums[2]
-    b_in_g = sums[3:7].reshape(-1)
-    b_out_g, gain1, shift1, b_q_g, b_v_g = sums[7], sums[8], sums[9], sums[10], sums[11]
+        b_in_g = sums[3:7].reshape(-1)
+        vectors = [sums[i] for i in (0, 1, 2, 7, 8, 9, 10, 11)]
+    b_back_g, gain2, shift2, b_out_g, gain1, shift1, b_q_g, b_v_g = vectors
     shape = (seqs, loc, width)
     return (
         result.reshape(shape),

time: 134 us -> 132 us (0.985)
  local copies, waits for them, and re-layouts: 8.53 us -> 7.15 us
where the time goes in v3:
time: 132 us
  Pallas kernels  45.5 us (34%)
  waiting for transfers between devices  38.2 us (29%)
  starting transfers between devices  37 us (28%)
  local copies, waits for them, and re-layouts  7.15 us (5%)
  other arithmetic  1.62 us (1%)
    ppermute x22, waiting for transfers between devices, flip(): return lax.ppermute(value, BOTH, [(i, i ^ 1 << bit) for i in range(count)])  38.2 us
    ppermute x22, starting transfers between devices, flip(): return lax.ppermute(value, BOTH, [(i, i ^ 1 << bit) for i in range(count)])  28.7 us
    pallas_call x1, Pallas kernels, local(): pl.pallas_call(functools.partial(forward_kernel, groups), name='layer_for...  13.8 us
    pallas_call x1, Pallas kernels, local(): pl.pallas_call(functools.partial(attend_back_kernel, groups), name='atten...  10.4 us
    ppermute x4, starting transfers between devices, around(): return (lax.ppermute(value, 'seq', up), lax.ppermute(value, 'seq', down))  8.25 us
    unnamed x64, local copies, waits for them, and re-layouts  6.46 us
    pallas_call x1, Pallas kernels, local(): pl.pallas_call(functools.partial(backward_kernel, groups), name='layer_ba...  5.31 us
    pallas_call x1, Pallas kernels, local(): pl.pallas_call(functools.partial(back_kernel, dp), name='grad_w_back', co...  3.34 us
  transfers between devices with their start and end apart: 26, of which 8 were waited for; matrix products, arithmetic and copies ran while one was open for 5% of the time, Pallas kernels for 23%

profile of v3, /device:TPU:0, one launch (start us, length us, event | category | flops | bytes accessed | tf_op | source)
XLA Modules:
  0.0 131.8 jit_solution(13570640968265923083)
XLA Ops:
  0.7 2.5 %collective-permute-start = (bf16[256,768]{1,0:T(8,128)(2,1)}, bf16[256,768]{1,0:T(8,128)(2,1)S(1)}, u32[]{:S(2)}, u32[]{:S(2)}) collective-permute-start(bf16[256,768]{1,0:T(8,128)(2,1)} %bitcast.10), channel_id=1, source_target_pairs={{0,1},{1,2},{2,3},{4,5},{5,6},{6,7},{8,9},{9,10},{10,11},{12,13},{... | collective-permute-start | bytes 1179656 | tf_op jit(solution)/shard_map/ppermute | solution.py:751
  3.2 1.3 collective-permute-start.1
  4.5 0.7 constant_dynamic-update-slice_fusion.3
  5.2 0.7 constant_dynamic-update-slice_fusion.2
  5.9 0.7 constant_dynamic-update-slice_fusion.1
  6.6 0.7 constant_dynamic-update-slice_fusion.vec_ref
  7.3 0.7 pad_add_fusion.ids_ref
  8.0 1.0 copy-done.2
  9.0 3.1 %own_projections.1 = (bf16[256,2304]{1,0:T(8,128)(2,1)S(1)}, f32[2,128,384]{2,1,0:T(8,128)S(1)}, f32[2,128,384]{2,1,0:T(8,128)S(1)}, bf16[768,2304]{1,0:T(8,128)(2,1)S(1)}) custom-call(s32[1]{0:T(128)} %bitcast.me_ref, s32[2,2,512]{2,1,0:T(2,128)S(1)} %pad_add_fusion.ids_ref, bf16[256,768]{1,0:T(8,128)(2,1)S(1)} %bitcast.12, ...), custom_call_target="tpu_custom_call" | custom-call | flops 4000000 | bytes 40000 | tf_op jit(solution)/shard_map/own_projections/pallas_call | solution.py:758
  12.2 13.8 %layer_forward.1 = (bf16[2,256,2304]{2,1,0:T(8,128)(2,1)S(1)}, bf16[256,4992]{1,0:T(8,128)(2,1)S(1)}, bf16[256,768]{1,0:T(8,128)(2,1)S(1)}, bf16[256,3072]{1,0:T...) custom-call(s32[1]{0:T(128)} %bitcast.me_ref, ...), custom_call_target="tpu_custom_call" | custom-call | flops 16000000 | bytes 160000 | tf_op jit(solution)/shard_map/layer_forward/pallas_call | solution.py:776
  26.1 3.3 %collective-permute-start.4 = (bf16[256,4992]{1,0:T(8,128)(2,1)S(1)}, bf16[256,4992]{1,0:T(8,128)(2,1)}, u32[]{:S(2)}, u32[]{:S(2)}) collective-permute-start(bf16[256,4992]{1,0:T(8,128)(2,1)S(1)} %get-tuple-element.130.acts_ref.hid.acts.ctx), channel_id=1, source_target_pairs={{0,1},{1,0},{2,3},{3,2},{4,5},{5,4},{6,7},{7,6},{8,9},{9,8},{10,11... | collective-permute-start | bytes 7667720 | tf_op jit(solution)/shard_map/ppermute | solution.py:623
  29.4 5.3 %layer_backward.1 = (bf16[256,1920]{1,0:T(8,128)(2,1)S(1)}, bf16[256,1920]{1,0:T(8,128)(2,1)}, bf16[256,896]{1,0:T(8,128)(2,1)}, f32[256,768]{1,0:T(8,128)S(1)}, f32[7,768]{1,0:T(8,128)S(1)}) custom-call(s32[1]{0:T(128)} %bitcast.me_ref, bf16[256,768]{1,0:T(8,128)(2,1)S(1)} %get-tuple-element.125.feed_ref, ...), custom_call_target="tpu_custom_call" | custom-call | flops 8000000 | bytes 80000 | tf_op jit(solution)/shard_map/layer_backward/pallas_call | solution.py:822
  34.8 0.9 copy-done.13
  35.6 0.6 copy-done.20
  36.3 3.2 %collective-permute-start.2 = (bf16[256,896]{1,0:T(8,128)(2,1)}, bf16[256,896]{1,0:T(8,128)(2,1)}, u32[]{:S(2)}, u32[]{:S(2)}) collective-permute-start(bf16[256,896]{1,0:T(8,128)(2,1)} %get-tuple-element.139.msg_own), channel_id=1, source_target_pairs={{0,1},{1,2},{2,3},{4,5},{5,6},{6,7},{8,9},{9,10},{10,11},{12,13},{... | collective-permute-start | bytes 1376264 | tf_op jit(solution)/shard_map/ppermute | solution.py:751
  39.4 1.3 collective-permute-start.3
  40.8 0.9 copy-done.19
  41.7 3.3 %grad_w_back.1 = (bf16[384,768]{1,0:T(8,128)(2,1)S(1)}, bf16[384,768]{1,0:T(8,128)(2,1)S(1)}, bf16[384,768]{1,0:T(8,128)(2,1)S(1)}, bf16[384,768]{1,0:T(8,128)(2,1)S(1)}) custom-call(s32[1]{0:T(128)} %bitcast.6.d_ref, bf16[256,4992]{1,0:T(8,128)(2,1)S(1)} %get-tuple-element.130.acts_ref.hid.acts.ctx, ...), custom_call_target="tpu_custom_call" | custom-call | flops 3000000 | bytes 30000 | tf_op jit(solution)/shard_map/grad_w_back/pallas_call | solution.py:854
  45.0 1.6 %collective-permute-start.10 = (bf16[384,768]{1,0:T(8,128)(2,1)S(1)}, bf16[384,768]{1,0:T(8,128)(2,1)S(1)}, u32[]{:S(2)}, u32[]{:S(2)}) collective-permute-start(bf16[384,768]{1,0:T(8,128)(2,1)S(1)} %get-tuple-element.161), channel_id=1, source_target_pairs={{0,8},{1,9},{2,10},{3,11},{4,12},{5,13},{6,14},{7,15},{8,0},{9,1},... | collective-permute-start | bytes 1769480 | tf_op jit(solution)/shard_map/ppermute | solution.py:623
  46.6 1.5 %collective-permute-start.9 = (bf16[384,768]{1,0:T(8,128)(2,1)S(1)}, bf16[384,768]{1,0:T(8,128)(2,1)S(1)}, u32[]{:S(2)}, u32[]{:S(2)}) collective-permute-start(bf16[384,768]{1,0:T(8,128)(2,1)S(1)} %get-tuple-element.159), channel_id=1, source_target_pairs={{0,4},{1,5},{2,6},{3,7},{4,0},{5,1},{6,2},{7,3},{8,12},{9,13},{10,... | collective-permute-start | bytes 1769480 | tf_op jit(solution)/shard_map/ppermute | solution.py:623
  48.3 3.1 %grad_w_in.1 = (bf16[384,768]{1,0:T(8,128)(2,1)S(1)}, bf16[384,768]{1,0:T(8,128)(2,1)S(1)}, bf16[384,768]{1,0:T(8,128)(2,1)S(1)}, bf16[384,768]{1,0:T(8,128)(2,1)S(1)}) custom-call(s32[1]{0:T(128)} %bitcast.6.d_ref, bf16[256,4992]{1,0:T(8,128)(2,1)S(1)} %get-tuple-element.130.acts_ref.hid.acts.ctx, ...), custom_call_target="tpu_custom_call" | custom-call | flops 4000000 | bytes 40000 | tf_op jit(solution)/shard_map/grad_w_in/pallas_call | solution.py:871
  51.4 3.3 %collective-permute-start.6 = (bf16[384,768]{1,0:T(8,128)(2,1)S(1)}, bf16[384,768]{1,0:T(8,128)(2,1)S(1)}, u32[]{:S(2)}, u32[]{:S(2)}) collective-permute-start(bf16[384,768]{1,0:T(8,128)(2,1)S(1)} %get-tuple-element.153), channel_id=1, source_target_pairs={{0,2},{1,3},{2,0},{3,1},{4,6},{5,7},{6,4},{7,5},{8,10},{9,11},{10,... | collective-permute-start | bytes 1769480 | tf_op jit(solution)/shard_map/ppermute | solution.py:623
  54.6 0.4 collective-permute-start.7
  55.1 10.4 %attend_backward.1 = (bf16[256,2304]{1,0:T(8,128)(2,1)S(1)}, bf16[256,1152]{1,0:T(8,128)(2,1)S(1)}, bf16[144,1152]{1,0:T(8,128)(2,1)S(1)}, bf16[128,1152]{1,0:T(8,128)(2,1)S(1)}, f32[16,768]{1,0:T(8,128)S(1)}) custom-call(s32[1]{0:T(128)} %bitcast.me_ref, f32[2,128,384]{2,1,0:T(8,128)S(1)} %copy-done.11, f32[2,128,384]{2,1,0:T(8,128)S(1)} %copy-done.16, ...), custom_call_target="tpu_custom_call" | custom-call | flops 11000000 | bytes 110000 | tf_op jit(solution)/shard_map/attend_backward/pallas_call | solution.py:890
  65.6 0.3 add_back_0.1
  65.9 0.2 collective-permute-start.14
  66.1 0.3 collective-permute-start.15
  66.5 0.1 pad_add_fusion.1.ids_ref
  66.5 1.5 %collective-permute-done.15.peer2 = bf16[128,1152]{1,0:T(8,128)(2,1)S(1)} collective-permute-done((bf16[128,1152]{1,0:T(8,128)(2,1)S(1)}, bf16[128,1152]{1,0:T(8,128)(2,1)S(1)}, u32[]{:S(2)}, u32[]{:S(2)}) %collective-permute-start.15) | collective-permute-done | bytes 294944 | tf_op jit(solution)/shard_map/ppermute | solution.py:623
  68.0 3.2 %grad_w_qkv_out.1 = (bf16[384,768]{1,0:T(8,128)(2,1)S(1)}, bf16[400,768]{1,0:T(8,128)(2,1)S(1)}, bf16[384,768]{1,0:T(8,128)(2,1)S(1)}, bf16[384,768]{1,0:T(8,128)(2,1)S(1)}, f32[16,768]{1,0:T(8,128)S(1)}) custom-call(s32[2]{0:T(128)S(1)} %pad_add_fusion.1.ids_ref, bf16[256,768]{1,0:T(8,128)(2,1)S(1)} %bitcast.14, bf16[256,768]{1,0:T(8,128)(2,1)S(1)} %copy-done.7, ...), custom_call_target="tpu_custom_call" | custom-call | flops 3000000 | bytes 30000 | tf_op jit(solution)/shard_map/grad_w_qkv_out/pallas_call | solution.py:914
  71.2 1.5 %collective-permute-start.19 = (bf16[400,768]{1,0:T(8,128)(2,1)S(1)}, bf16[400,768]{1,0:T(8,128)(2,1)S(1)}, u32[]{:S(2)}, u32[]{:S(2)}) collective-permute-start(bf16[400,768]{1,0:T(8,128)(2,1)S(1)} %get-tuple-element.185), channel_id=1, source_target_pairs={{0,2},{1,3},{2,0},{3,1},{4,6},{5,7},{6,4},{7,5},{8,10},{9,11},{10,... | collective-permute-start | bytes 1843208 | tf_op jit(solution)/shard_map/ppermute | solution.py:623
  72.8 0.5 collective-permute-start.11
  73.2 1.5 %collective-permute-start.12 = (bf16[192,768]{1,0:T(8,128)(2,1)S(1)}, bf16[192,768]{1,0:T(8,128)(2,1)S(1)}, u32[]{:S(2)}, u32[]{:S(2)}) collective-permute-start(bf16[192,768]{1,0:T(8,128)(2,1)S(1)} %get-tuple-element.166), channel_id=1, source_target_pairs={{0,4},{1,5},{2,6},{3,7},{4,0},{5,1},{6,2},{7,3},{8,12},{9,13},{10,... | collective-permute-start | bytes 884744 | tf_op jit(solution)/shard_map/ppermute | solution.py:623
  74.8 0.3 add_in_0.1
  75.1 1.7 %collective-permute-start.20 = (bf16[384,768]{1,0:T(8,128)(2,1)S(1)}, bf16[384,768]{1,0:T(8,128)(2,1)S(1)}, u32[]{:S(2)}, u32[]{:S(2)}) collective-permute-start(bf16[384,768]{1,0:T(8,128)(2,1)S(1)} %get-tuple-element.189), channel_id=1, source_target_pairs={{0,8},{1,9},{2,10},{3,11},{4,12},{5,13},{6,14},{7,15},{8,0},{9,1},... | collective-permute-start | bytes 1769480 | tf_op jit(solution)/shard_map/ppermute | solution.py:623
  76.7 0.4 collective-permute-start.8
  77.1 5.5 %collective-permute-done.11.got0 = bf16[192,768]{1,0:T(8,128)(2,1)S(1)} collective-permute-done((bf16[192,768]{1,0:T(8,128)(2,1)S(1)}, bf16[192,768]{1,0:T(8,128)(2,1)S(1)}, u32[]{:S(2)}, u32[]{:S(2)}) %collective-permute-start.11) | collective-permute-done | bytes 294944 | tf_op jit(solution)/shard_map/ppermute | solution.py:623
  82.6 0.6 collective-permute-start.16
  83.2 0.1 add_back_1.1
  83.4 1.5 %collective-permute-start.13 = (bf16[192,768]{1,0:T(8,128)(2,1)S(1)}, bf16[192,768]{1,0:T(8,128)(2,1)S(1)}, u32[]{:S(2)}, u32[]{:S(2)}) collective-permute-start(bf16[192,768]{1,0:T(8,128)(2,1)S(1)} %get-tuple-element.169), channel_id=1, source_target_pairs={{0,2},{1,3},{2,0},{3,1},{4,6},{5,7},{6,4},{7,5},{8,10},{9,11},{10,... | collective-permute-start | bytes 884744 | tf_op jit(solution)/shard_map/ppermute | solution.py:623
  84.9 15.9 %collective-permute-done.8.got0 = bf16[192,768]{1,0:T(8,128)(2,1)S(1)} collective-permute-done((bf16[192,768]{1,0:T(8,128)(2,1)S(1)}, bf16[192,768]{1,0:T(8,128)(2,1)S(1)}, u32[]{:S(2)}, u32[]{:S(2)}) %collective-permute-start.8) | collective-permute-done | bytes 294944 | tf_op jit(solution)/shard_map/ppermute | solution.py:623
  100.8 0.1 add_in_1.1
  101.0 0.1 add_back_2.1
  101.1 0.3 add_qkv_0.1
  101.3 0.5 collective-permute-start.21
  101.9 1.5 %collective-permute-start.18 = (bf16[192,768]{1,0:T(8,128)(2,1)S(1)}, bf16[192,768]{1,0:T(8,128)(2,1)S(1)}, u32[]{:S(2)}, u32[]{:S(2)}) collective-permute-start(bf16[192,768]{1,0:T(8,128)(2,1)S(1)} %get-tuple-element.183), channel_id=1, source_target_pairs={{0,4},{1,5},{2,6},{3,7},{4,0},{5,1},{6,2},{7,3},{8,12},{9,13},{10,... | collective-permute-start | bytes 884744 | tf_op jit(solution)/shard_map/ppermute | solution.py:623
  103.4 1.3 %collective-permute-start.22 = (bf16[192,768]{1,0:T(8,128)(2,1)S(1)}, bf16[192,768]{1,0:T(8,128)(2,1)S(1)}, u32[]{:S(2)}, u32[]{:S(2)}) collective-permute-start(bf16[192,768]{1,0:T(8,128)(2,1)S(1)} %get-tuple-element.199), channel_id=1, source_target_pairs={{0,2},{1,3},{2,0},{3,1},{4,6},{5,7},{6,4},{7,5},{8,10},{9,11},{10,... | collective-permute-start | bytes 884744 | tf_op jit(solution)/shard_map/ppermute | solution.py:623
  104.7 2.6 %collective-permute-start.17 = (bf16[96,768]{1,0:T(8,128)(2,1)S(1)}, bf16[96,768]{1,0:T(8,128)(2,1)S(1)}, u32[]{:S(2)}, u32[]{:S(2)}) collective-permute-start(bf16[96,768]{1,0:T(8,128)(2,1)S(1)} %get-tuple-element.182), channel_id=1, source_target_pairs={{0,16},{1,17},{2,18},{3,19},{4,20},{5,21},{6,22},{7,23},{8,24},{9,... | collective-permute-start | bytes 442376 | tf_op jit(solution)/shard_map/ppermute | solution.py:623
  107.3 2.5 %collective-permute-done.18.got = bf16[192,768]{1,0:T(8,128)(2,1)S(1)} collective-permute-done((bf16[192,768]{1,0:T(8,128)(2,1)S(1)}, bf16[192,768]{1,0:T(8,128)(2,1)S(1)}, u32[]{:S(2)}, u32[]{:S(2)}) %collective-permute-start.18) | collective-permute-done | bytes 294944 | tf_op jit(solution)/shard_map/ppermute | solution.py:623
  109.9 2.6 %collective-permute-start.24 = (bf16[96,768]{1,0:T(8,128)(2,1)S(1)}, bf16[96,768]{1,0:T(8,128)(2,1)S(1)}, u32[]{:S(2)}, u32[]{:S(2)}) collective-permute-start(bf16[96,768]{1,0:T(8,128)(2,1)S(1)} %get-tuple-element.205), channel_id=1, source_target_pairs={{0,16},{1,17},{2,18},{3,19},{4,20},{5,21},{6,22},{7,23},{8,24},{9,... | collective-permute-start | bytes 442376 | tf_op jit(solution)/shard_map/ppermute | solution.py:623
  112.5 2.1 %collective-permute-done.21.got0 = bf16[208,768]{1,0:T(8,128)(2,1)S(1)} collective-permute-done((bf16[208,768]{1,0:T(8,128)(2,1)S(1)}, bf16[208,768]{1,0:T(8,128)(2,1)S(1)}, u32[]{:S(2)}, u32[]{:S(2)}) %collective-permute-start.21) | collective-permute-done | bytes 319520 | tf_op jit(solution)/shard_map/ppermute | solution.py:623
  114.6 0.1 add_qkv_1.1
  114.7 1.6 %collective-permute-start.23 = (bf16[208,768]{1,0:T(8,128)(2,1)S(1)}, bf16[208,768]{1,0:T(8,128)(2,1)S(1)}, u32[]{:S(2)}, u32[]{:S(2)}) collective-permute-start(bf16[208,768]{1,0:T(8,128)(2,1)S(1)} %get-tuple-element.203), channel_id=1, source_target_pairs={{0,4},{1,5},{2,6},{3,7},{4,0},{5,1},{6,2},{7,3},{8,12},{9,13},{10,... | collective-permute-start | bytes 958472 | tf_op jit(solution)/shard_map/ppermute | solution.py:623
  116.4 1.1 fusion
  117.5 0.3 add_back_3.1
  117.8 2.8 %collective-permute-done.24.got = bf16[96,768]{1,0:T(8,128)(2,1)S(1)} collective-permute-done((bf16[96,768]{1,0:T(8,128)(2,1)S(1)}, bf16[96,768]{1,0:T(8,128)(2,1)S(1)}, u32[]{:S(2)}, u32[]{:S(2)}) %collective-permute-start.24) | collective-permute-done | bytes 147488 | tf_op jit(solution)/shard_map/ppermute | solution.py:623
  120.5 0.7 add_in_3.1
  121.3 0.5 collective-permute-done.23.got
  121.8 0.1 add_qkv_2.1
  121.9 0.1 collective-permute-start.25
  122.0 0.8 add_convert_fusion
  122.8 0.9 copy.32
  123.7 7.4 %collective-permute-done.25.got = bf16[112,768]{1,0:T(8,128)(2,1)S(1)} collective-permute-done((bf16[112,768]{1,0:T(8,128)(2,1)S(1)}, bf16[112,768]{1,0:T(8,128)(2,1)S(1)}, u32[]{:S(2)}, u32[]{:S(2)}) %collective-permute-start.25) | collective-permute-done | bytes 172064 | tf_op jit(solution)/shard_map/ppermute | solution.py:623
  131.1 0.8 add_qkv_3.1
  (78 shorter events, 0.3 us)
Async XLA Ops:
  0.6 11.4 %copy-start.29 = (f32[768]{0:T(1024)S(1)}, f32[768]{0:T(1024)}, u32[]{:S(2)}) copy-start(f32[768]{0:T(1024)} %param.26) | copy-start | bytes 9220
  0.7 11.4 %copy-start.28 = (f32[768]{0:T(1024)S(1)}, f32[768]{0:T(1024)}, u32[]{:S(2)}) copy-start(f32[768]{0:T(1024)} %param.30) | copy-start | bytes 9220
  0.7 11.4 %copy-start.27 = (f32[768]{0:T(1024)S(1)}, f32[768]{0:T(1024)}, u32[]{:S(2)}) copy-start(f32[768]{0:T(1024)} %param.31) | copy-start | bytes 9220
  0.7 11.4 %copy-start.26 = (f32[768]{0:T(1024)S(1)}, f32[768]{0:T(1024)}, u32[]{:S(2)}) copy-start(f32[768]{0:T(1024)} %param.32) | copy-start | bytes 9220
  0.7 11.5 %copy-start.22 = (f32[3072]{0:T(1024)S(1)}, f32[3072]{0:T(1024)}, u32[]{:S(2)}) copy-start(f32[3072]{0:T(1024)} %b_in_ref.1) | copy-start | bytes 36868
  0.7 11.5 %collective-permute-start = (bf16[256,768]{1,0:T(8,128)(2,1)}, bf16[256,768]{1,0:T(8,128)(2,1)S(1)}, u32[]{:S(2)}, u32[]{:S(2)}) collective-permute-start(bf16[256,768]{1,0:T(8,128)(2,1)} %bitcast.10), channel_id=1, source_target_pairs={{0,1},{1,2},{2,3},{4,5},{5,6},{6,7},{8,9},{9,10},{10,11},{12,13},{... | collective-permute-start | bytes 1179656 | tf_op jit(solution)/shard_map/ppermute | solution.py:751
  3.2 9.0 %collective-permute-start.1 = (bf16[256,768]{1,0:T(8,128)(2,1)}, bf16[256,768]{1,0:T(8,128)(2,1)S(1)}, u32[]{:S(2)}, u32[]{:S(2)}) collective-permute-start(bf16[256,768]{1,0:T(8,128)(2,1)} %bitcast.11), channel_id=1, source_target_pairs={{1,0},{2,1},{3,2},{5,4},{6,5},{7,6},{9,8},{10,9},{11,10},{13,12},{... | collective-permute-start | bytes 1179656 | tf_op jit(solution)/shard_map/ppermute | solution.py:751
  8.0 1.0 copy-start.2
  9.0 3.2 %copy-start.12 = (bf16[768,768]{1,0:T(8,128)(2,1)S(1)}, bf16[768,768]{1,0:T(8,128)(2,1)}, u32[]{:S(2)}) copy-start(bf16[768,768]{1,0:T(8,128)(2,1)} %wout_hbm.1) | copy-start | bytes 3538948
  9.0 3.2 %copy-start.17 = (bf16[2,128,768]{2,1,0:T(8,128)(2,1)S(1)}, bf16[2,128,768]{2,1,0:T(8,128)(2,1)}, u32[]{:S(2)}) copy-start(bf16[2,128,768]{2,1,0:T(8,128)(2,1)} %param.33) | copy-start | bytes 1179652
  12.1 13.9 %copy-start = (bf16[256,2304]{1,0:T(8,128)(2,1)}, bf16[256,2304]{1,0:T(8,128)(2,1)S(1)}, u32[]{:S(2)}) copy-start(bf16[256,2304]{1,0:T(8,128)(2,1)S(1)} %get-tuple-element.121.own_ref) | copy-start | bytes 3538948
  12.1 13.9 %copy-start.10 = (f32[2,128,384]{2,1,0:T(8,128)}, f32[2,128,384]{2,1,0:T(8,128)S(1)}, u32[]{:S(2)}) copy-start(f32[2,128,384]{2,1,0:T(8,128)S(1)} %get-tuple-element.122.mask_ref) | copy-start | bytes 1179652
  12.2 13.9 %copy-start.15 = (f32[2,128,384]{2,1,0:T(8,128)}, f32[2,128,384]{2,1,0:T(8,128)S(1)}, u32[]{:S(2)}) copy-start(f32[2,128,384]{2,1,0:T(8,128)S(1)} %get-tuple-element.136.mask_t_ref) | copy-start | bytes 1179652
  12.2 13.9 %copy-start.6 = (bf16[256,768]{1,0:T(8,128)(2,1)}, bf16[256,768]{1,0:T(8,128)(2,1)S(1)}, u32[]{:S(2)}) copy-start(bf16[256,768]{1,0:T(8,128)(2,1)S(1)} %collective-permute-done.tok_prev) | copy-start | bytes 1179652
  12.2 13.9 %copy-start.8 = (bf16[256,768]{1,0:T(8,128)(2,1)}, bf16[256,768]{1,0:T(8,128)(2,1)S(1)}, u32[]{:S(2)}) copy-start(bf16[256,768]{1,0:T(8,128)(2,1)S(1)} %collective-permute-done.1.tok_next) | copy-start | bytes 1179652
  26.1 8.7 %copy-start.4 = (bf16[2,256,2304]{2,1,0:T(8,128)(2,1)}, bf16[2,256,2304]{2,1,0:T(8,128)(2,1)S(1)}, u32[]{:S(2)}) copy-start(bf16[2,256,2304]{2,1,0:T(8,128)(2,1)S(1)} %get-tuple-element.137.near_ref) | copy-start | bytes 7077892
  26.1 8.6 %copy-start.18 = (bf16[256,384]{1,0:T(8,128)(2,1)}, bf16[256,384]{1,0:T(8,128)(2,1)S(1)}, u32[]{:S(2)}) copy-start(bf16[256,384]{1,0:T(8,128)(2,1)S(1)} %get-tuple-element.142.feed) | copy-start | bytes 589828
  26.1 8.6 %copy-start.23 = (f32[3,768]{1,0:T(4,128)}, f32[3,768]{1,0:T(4,128)S(1)}, u32[]{:S(2)}) copy-start(f32[3,768]{1,0:T(4,128)S(1)} %get-tuple-element.149.small1_ref) | copy-start | bytes 27652
  26.1 14.6 %collective-permute-start.4 = (bf16[256,4992]{1,0:T(8,128)(2,1)S(1)}, bf16[256,4992]{1,0:T(8,128)(2,1)}, u32[]{:S(2)}, u32[]{:S(2)}) collective-permute-start(bf16[256,4992]{1,0:T(8,128)(2,1)S(1)} %get-tuple-element.130.acts_ref.hid.acts.ctx), channel_id=1, source_target_pairs={{0,1},{1,0},{2,3},{3,2},{4,5},{5,4},{6,7},{7,6},{8,9},{9,8},{10,11... | collective-permute-start | bytes 7667720 | tf_op jit(solution)/shard_map/ppermute | solution.py:623
  34.8 0.9 copy-start.13
  35.6 0.6 copy-start.20
  36.2 12.0 %collective-permute-start.5 = (bf16[256,1920]{1,0:T(8,128)(2,1)}, bf16[256,1920]{1,0:T(8,128)(2,1)}, u32[]{:S(2)}, u32[]{:S(2)}) collective-permute-start(bf16[256,1920]{1,0:T(8,128)(2,1)} %get-tuple-element.145), channel_id=1, source_target_pairs={{0,1},{1,0},{2,3},{3,2},{4,5},{5,4},{6,7},{7,6},{8,9},{9,8},{10,11... | collective-permute-start | bytes 2949128 | tf_op jit(solution)/shard_map/ppermute | solution.py:623
  36.3 11.9 %collective-permute-start.2 = (bf16[256,896]{1,0:T(8,128)(2,1)}, bf16[256,896]{1,0:T(8,128)(2,1)}, u32[]{:S(2)}, u32[]{:S(2)}) collective-permute-start(bf16[256,896]{1,0:T(8,128)(2,1)} %get-tuple-element.139.msg_own), channel_id=1, source_target_pairs={{0,1},{1,2},{2,3},{4,5},{5,6},{6,7},{8,9},{9,10},{10,11},{12,13},{... | collective-permute-start | bytes 1376264 | tf_op jit(solution)/shard_map/ppermute | solution.py:751
  39.4 8.8 %collective-permute-start.3 = (bf16[256,896]{1,0:T(8,128)(2,1)}, bf16[256,896]{1,0:T(8,128)(2,1)}, u32[]{:S(2)}, u32[]{:S(2)}) collective-permute-start(bf16[256,896]{1,0:T(8,128)(2,1)} %get-tuple-element.139.msg_own), channel_id=1, source_target_pairs={{1,0},{2,1},{3,2},{5,4},{6,5},{7,6},{9,8},{10,9},{11,10},{13,12},{... | collective-permute-start | bytes 1376264 | tf_op jit(solution)/shard_map/ppermute | solution.py:751
  40.7 0.9 copy-start.19
  45.0 20.6 %collective-permute-start.10 = (bf16[384,768]{1,0:T(8,128)(2,1)S(1)}, bf16[384,768]{1,0:T(8,128)(2,1)S(1)}, u32[]{:S(2)}, u32[]{:S(2)}) collective-permute-start(bf16[384,768]{1,0:T(8,128)(2,1)S(1)} %get-tuple-element.161), channel_id=1, source_target_pairs={{0,8},{1,9},{2,10},{3,11},{4,12},{5,13},{6,14},{7,15},{8,0},{9,1},... | collective-permute-start | bytes 1769480 | tf_op jit(solution)/shard_map/ppermute | solution.py:623
  46.6 19.0 %collective-permute-start.9 = (bf16[384,768]{1,0:T(8,128)(2,1)S(1)}, bf16[384,768]{1,0:T(8,128)(2,1)S(1)}, u32[]{:S(2)}, u32[]{:S(2)}) collective-permute-start(bf16[384,768]{1,0:T(8,128)(2,1)S(1)} %get-tuple-element.159), channel_id=1, source_target_pairs={{0,4},{1,5},{2,6},{3,7},{4,0},{5,1},{6,2},{7,3},{8,12},{9,13},{10,... | collective-permute-start | bytes 1769480 | tf_op jit(solution)/shard_map/ppermute | solution.py:623
  48.2 6.9 %copy-start.1 = (bf16[256,2304]{1,0:T(8,128)(2,1)S(1)}, bf16[256,2304]{1,0:T(8,128)(2,1)}, u32[]{:S(2)}) copy-start(bf16[256,2304]{1,0:T(8,128)(2,1)} %copy-done) | copy-start | bytes 3538948
  48.2 6.9 %copy-start.5 = (bf16[2,256,2304]{2,1,0:T(8,128)(2,1)S(1)}, bf16[2,256,2304]{2,1,0:T(8,128)(2,1)}, u32[]{:S(2)}) copy-start(bf16[2,256,2304]{2,1,0:T(8,128)(2,1)} %copy-done.4) | copy-start | bytes 7077892
  48.2 6.9 %copy-start.11 = (f32[2,128,384]{2,1,0:T(8,128)S(1)}, f32[2,128,384]{2,1,0:T(8,128)}, u32[]{:S(2)}) copy-start(f32[2,128,384]{2,1,0:T(8,128)} %copy-done.10) | copy-start | bytes 1179652
  48.2 6.9 %copy-start.16 = (f32[2,128,384]{2,1,0:T(8,128)S(1)}, f32[2,128,384]{2,1,0:T(8,128)}, u32[]{:S(2)}) copy-start(f32[2,128,384]{2,1,0:T(8,128)} %copy-done.15) | copy-start | bytes 1179652
  48.2 6.9 %copy-start.21 = (f32[7,768]{1,0:T(8,128)S(1)}, f32[7,768]{1,0:T(8,128)}, u32[]{:S(2)}) copy-start(f32[7,768]{1,0:T(8,128)} %copy-done.20) | copy-start | bytes 64516
  48.2 6.9 %copy-start.24 = (f32[3,768]{1,0:T(4,128)S(1)}, f32[3,768]{1,0:T(4,128)}, u32[]{:S(2)}) copy-start(f32[3,768]{1,0:T(4,128)} %copy-done.23) | copy-start | bytes 27652
  51.4 23.4 %collective-permute-start.6 = (bf16[384,768]{1,0:T(8,128)(2,1)S(1)}, bf16[384,768]{1,0:T(8,128)(2,1)S(1)}, u32[]{:S(2)}, u32[]{:S(2)}) collective-permute-start(bf16[384,768]{1,0:T(8,128)(2,1)S(1)} %get-tuple-element.153), channel_id=1, source_target_pairs={{0,2},{1,3},{2,0},{3,1},{4,6},{5,7},{6,4},{7,5},{8,10},{9,11},{10,... | collective-permute-start | bytes 1769480 | tf_op jit(solution)/shard_map/ppermute | solution.py:623
  54.6 20.1 %collective-permute-start.7 = (bf16[384,768]{1,0:T(8,128)(2,1)S(1)}, bf16[384,768]{1,0:T(8,128)(2,1)S(1)}, u32[]{:S(2)}, u32[]{:S(2)}) collective-permute-start(bf16[384,768]{1,0:T(8,128)(2,1)S(1)} %get-tuple-element.155), channel_id=1, source_target_pairs={{0,8},{1,9},{2,10},{3,11},{4,12},{5,13},{6,14},{7,15},{8,0},{9,1},... | collective-permute-start | bytes 1769480 | tf_op jit(solution)/shard_map/ppermute | solution.py:623
  65.6 2.5 %copy-start.3 = (bf16[2,128,768]{2,1,0:T(8,128)(2,1)S(1)}, bf16[2,128,768]{2,1,0:T(8,128)(2,1)}, u32[]{:S(2)}) copy-start(bf16[2,128,768]{2,1,0:T(8,128)(2,1)} %param.17) | copy-start | bytes 1179652
  65.6 2.5 %copy-start.7 = (bf16[256,768]{1,0:T(8,128)(2,1)S(1)}, bf16[256,768]{1,0:T(8,128)(2,1)}, u32[]{:S(2)}) copy-start(bf16[256,768]{1,0:T(8,128)(2,1)} %copy-done.6) | copy-start | bytes 1179652
  65.6 2.4 %copy-start.9 = (bf16[256,768]{1,0:T(8,128)(2,1)S(1)}, bf16[256,768]{1,0:T(8,128)(2,1)}, u32[]{:S(2)}) copy-start(bf16[256,768]{1,0:T(8,128)(2,1)} %copy-done.8) | copy-start | bytes 1179652
  65.9 2.1 %collective-permute-start.14 = (bf16[144,1152]{1,0:T(8,128)(2,1)S(1)}, bf16[144,1152]{1,0:T(8,128)(2,1)S(1)}, u32[]{:S(2)}, u32[]{:S(2)}) collective-permute-start(bf16[144,1152]{1,0:T(8,128)(2,1)S(1)} %get-tuple-element.171), channel_id=1, source_target_pairs={{0,1},{1,0},{2,3},{3,2},{4,5},{5,4},{6,7},{7,6},{8,9},{9,8},{10,11... | collective-permute-start | bytes 995336 | tf_op jit(solution)/shard_map/ppermute | solution.py:623
  66.1 1.9 %collective-permute-start.15 = (bf16[128,1152]{1,0:T(8,128)(2,1)S(1)}, bf16[128,1152]{1,0:T(8,128)(2,1)S(1)}, u32[]{:S(2)}, u32[]{:S(2)}) collective-permute-start(bf16[128,1152]{1,0:T(8,128)(2,1)S(1)} %get-tuple-element.172), channel_id=1, source_target_pairs={{0,1},{1,0},{2,3},{3,2},{4,5},{5,4},{6,7},{7,6},{8,9},{9,8},{10,11... | collective-permute-start | bytes 884744 | tf_op jit(solution)/shard_map/ppermute | solution.py:623
  71.2 29.8 %collective-permute-start.19 = (bf16[400,768]{1,0:T(8,128)(2,1)S(1)}, bf16[400,768]{1,0:T(8,128)(2,1)S(1)}, u32[]{:S(2)}, u32[]{:S(2)}) collective-permute-start(bf16[400,768]{1,0:T(8,128)(2,1)S(1)} %get-tuple-element.185), channel_id=1, source_target_pairs={{0,2},{1,3},{2,0},{3,1},{4,6},{5,7},{6,4},{7,5},{8,10},{9,11},{10,... | collective-permute-start | bytes 1843208 | tf_op jit(solution)/shard_map/ppermute | solution.py:623
  72.8 9.9 %collective-permute-start.11 = (bf16[192,768]{1,0:T(8,128)(2,1)S(1)}, bf16[192,768]{1,0:T(8,128)(2,1)S(1)}, u32[]{:S(2)}, u32[]{:S(2)}) collective-permute-start(bf16[192,768]{1,0:T(8,128)(2,1)S(1)} %get-tuple-element.164), channel_id=1, source_target_pairs={{0,8},{1,9},{2,10},{3,11},{4,12},{5,13},{6,14},{7,15},{8,0},{9,1},... | collective-permute-start | bytes 884744 | tf_op jit(solution)/shard_map/ppermute | solution.py:623
  73.2 10.0 %collective-permute-start.12 = (bf16[192,768]{1,0:T(8,128)(2,1)S(1)}, bf16[192,768]{1,0:T(8,128)(2,1)S(1)}, u32[]{:S(2)}, u32[]{:S(2)}) collective-permute-start(bf16[192,768]{1,0:T(8,128)(2,1)S(1)} %get-tuple-element.166), channel_id=1, source_target_pairs={{0,4},{1,5},{2,6},{3,7},{4,0},{5,1},{6,2},{7,3},{8,12},{9,13},{10,... | collective-permute-start | bytes 884744 | tf_op jit(solution)/shard_map/ppermute | solution.py:623
  75.1 26.0 %collective-permute-start.20 = (bf16[384,768]{1,0:T(8,128)(2,1)S(1)}, bf16[384,768]{1,0:T(8,128)(2,1)S(1)}, u32[]{:S(2)}, u32[]{:S(2)}) collective-permute-start(bf16[384,768]{1,0:T(8,128)(2,1)S(1)} %get-tuple-element.189), channel_id=1, source_target_pairs={{0,8},{1,9},{2,10},{3,11},{4,12},{5,13},{6,14},{7,15},{8,0},{9,1},... | collective-permute-start | bytes 1769480 | tf_op jit(solution)/shard_map/ppermute | solution.py:623
  76.7 24.1 %collective-permute-start.8 = (bf16[192,768]{1,0:T(8,128)(2,1)S(1)}, bf16[192,768]{1,0:T(8,128)(2,1)S(1)}, u32[]{:S(2)}, u32[]{:S(2)}) collective-permute-start(bf16[192,768]{1,0:T(8,128)(2,1)S(1)} %get-tuple-element.156), channel_id=1, source_target_pairs={{0,8},{1,9},{2,10},{3,11},{4,12},{5,13},{6,14},{7,15},{8,0},{9,1},... | collective-permute-start | bytes 884744 | tf_op jit(solution)/shard_map/ppermute | solution.py:623
  82.6 18.2 %collective-permute-start.16 = (bf16[192,768]{1,0:T(8,128)(2,1)S(1)}, bf16[192,768]{1,0:T(8,128)(2,1)S(1)}, u32[]{:S(2)}, u32[]{:S(2)}) collective-permute-start(bf16[192,768]{1,0:T(8,128)(2,1)S(1)} %get-tuple-element.179), channel_id=1, source_target_pairs={{0,2},{1,3},{2,0},{3,1},{4,6},{5,7},{6,4},{7,5},{8,10},{9,11},{10,... | collective-permute-start | bytes 884744 | tf_op jit(solution)/shard_map/ppermute | solution.py:623
  83.4 17.6 %collective-permute-start.13 = (bf16[192,768]{1,0:T(8,128)(2,1)S(1)}, bf16[192,768]{1,0:T(8,128)(2,1)S(1)}, u32[]{:S(2)}, u32[]{:S(2)}) collective-permute-start(bf16[192,768]{1,0:T(8,128)(2,1)S(1)} %get-tuple-element.169), channel_id=1, source_target_pairs={{0,2},{1,3},{2,0},{3,1},{4,6},{5,7},{6,4},{7,5},{8,10},{9,11},{10,... | collective-permute-start | bytes 884744 | tf_op jit(solution)/shard_map/ppermute | solution.py:623
  100.9 15.4 %copy-start.25 = (bf16[768,2304]{1,0:T(8,128)(2,1)S(1)}, bf16[768,2304]{1,0:T(8,128)(2,1)}, u32[]{:S(2)}) copy-start(bf16[768,2304]{1,0:T(8,128)(2,1)} %wqkv_hbm.1) | copy-start | bytes 10616836
  101.3 13.3 %collective-permute-start.21 = (bf16[208,768]{1,0:T(8,128)(2,1)S(1)}, bf16[208,768]{1,0:T(8,128)(2,1)S(1)}, u32[]{:S(2)}, u32[]{:S(2)}) collective-permute-start(bf16[208,768]{1,0:T(8,128)(2,1)S(1)} %get-tuple-element.193), channel_id=1, source_target_pairs={{0,8},{1,9},{2,10},{3,11},{4,12},{5,13},{6,14},{7,15},{8,0},{9,1},... | collective-permute-start | bytes 958472 | tf_op jit(solution)/shard_map/ppermute | solution.py:623
  101.9 8.0 %collective-permute-start.18 = (bf16[192,768]{1,0:T(8,128)(2,1)S(1)}, bf16[192,768]{1,0:T(8,128)(2,1)S(1)}, u32[]{:S(2)}, u32[]{:S(2)}) collective-permute-start(bf16[192,768]{1,0:T(8,128)(2,1)S(1)} %get-tuple-element.183), channel_id=1, source_target_pairs={{0,4},{1,5},{2,6},{3,7},{4,0},{5,1},{6,2},{7,3},{8,12},{9,13},{10,... | collective-permute-start | bytes 884744 | tf_op jit(solution)/shard_map/ppermute | solution.py:623
  103.4 11.2 %collective-permute-start.22 = (bf16[192,768]{1,0:T(8,128)(2,1)S(1)}, bf16[192,768]{1,0:T(8,128)(2,1)S(1)}, u32[]{:S(2)}, u32[]{:S(2)}) collective-permute-start(bf16[192,768]{1,0:T(8,128)(2,1)S(1)} %get-tuple-element.199), channel_id=1, source_target_pairs={{0,2},{1,3},{2,0},{3,1},{4,6},{5,7},{6,4},{7,5},{8,10},{9,11},{10,... | collective-permute-start | bytes 884744 | tf_op jit(solution)/shard_map/ppermute | solution.py:623
  104.7 12.8 %collective-permute-start.17 = (bf16[96,768]{1,0:T(8,128)(2,1)S(1)}, bf16[96,768]{1,0:T(8,128)(2,1)S(1)}, u32[]{:S(2)}, u32[]{:S(2)}) collective-permute-start(bf16[96,768]{1,0:T(8,128)(2,1)S(1)} %get-tuple-element.182), channel_id=1, source_target_pairs={{0,16},{1,17},{2,18},{3,19},{4,20},{5,21},{6,22},{7,23},{8,24},{9,... | collective-permute-start | bytes 442376 | tf_op jit(solution)/shard_map/ppermute | solution.py:623
  109.9 10.6 %collective-permute-start.24 = (bf16[96,768]{1,0:T(8,128)(2,1)S(1)}, bf16[96,768]{1,0:T(8,128)(2,1)S(1)}, u32[]{:S(2)}, u32[]{:S(2)}) collective-permute-start(bf16[96,768]{1,0:T(8,128)(2,1)S(1)} %get-tuple-element.205), channel_id=1, source_target_pairs={{0,16},{1,17},{2,18},{3,19},{4,20},{5,21},{6,22},{7,23},{8,24},{9,... | collective-permute-start | bytes 442376 | tf_op jit(solution)/shard_map/ppermute | solution.py:623
  114.7 7.1 %collective-permute-start.23 = (bf16[208,768]{1,0:T(8,128)(2,1)S(1)}, bf16[208,768]{1,0:T(8,128)(2,1)S(1)}, u32[]{:S(2)}, u32[]{:S(2)}) collective-permute-start(bf16[208,768]{1,0:T(8,128)(2,1)S(1)} %get-tuple-element.203), channel_id=1, source_target_pairs={{0,4},{1,5},{2,6},{3,7},{4,0},{5,1},{6,2},{7,3},{8,12},{9,13},{10,... | collective-permute-start | bytes 958472 | tf_op jit(solution)/shard_map/ppermute | solution.py:623
  116.4 5.6 %copy-start.14 = (f32[256,768]{1,0:T(8,128)S(1)}, f32[256,768]{1,0:T(8,128)}, u32[]{:S(2)}) copy-start(f32[256,768]{1,0:T(8,128)} %copy-done.13) | copy-start | bytes 2359300
  121.9 9.2 %collective-permute-start.25 = (bf16[112,768]{1,0:T(8,128)(2,1)S(1)}, bf16[112,768]{1,0:T(8,128)(2,1)S(1)}, u32[]{:S(2)}, u32[]{:S(2)}) collective-permute-start(bf16[112,768]{1,0:T(8,128)(2,1)S(1)} %get-tuple-element.212), channel_id=1, source_target_pairs={{0,16},{1,17},{2,18},{3,19},{4,20},{5,21},{6,22},{7,23},{8,24},{9,... | collective-permute-start | bytes 516104 | tf_op jit(solution)/shard_map/ppermute | solution.py:623

commit v4 on v3

--- a/solution.py
+++ b/solution.py
@@ -179,7 +179,7 @@
         return tuple(result)
 
     zero = jnp.zeros((loc, 128), F32)
-    totals = lax.fori_loop(0, HEADS // 2, attend, (zero, zero), unroll=3)
+    totals = lax.fori_loop(0, HEADS // 2, attend, (zero, zero), unroll=6)
     lse_ref[:loc, :] = totals[0]
     lse_ref[loc:, :] = totals[1]
     context = ctx_ref[...]
@@ -390,7 +390,7 @@
             all_ref[at, spans[2]] = value_grad.astype(BF)
         return carry
 
-    lax.fori_loop(0, HEADS // 2, heads, 0, unroll=3)
+    lax.fori_loop(0, HEADS // 2, heads, 0, unroll=6)
     value_at = 2 * width
     sums_ref[...] = jnp.concatenate(
         [

time: 132 us -> 132 us (level)
  transfers between devices with their start and end apart: 26 -> 26, of which waited for: 8 -> 7; matrix products, arithmetic and copies ran while one was open for 5% -> 5% of each run, Pallas kernels for 23% -> 23%
where the time goes in v4:
time: 132 us
  Pallas kernels  44.8 us (34%)
  starting transfers between devices  38 us (29%)
  waiting for transfers between devices  37.6 us (28%)
  local copies, waits for them, and re-layouts  7.15 us (5%)
  other arithmetic  1.62 us (1%)
    ppermute x22, waiting for transfers between devices, flip(): return lax.ppermute(value, BOTH, [(i, i ^ 1 << bit) for i in range(count)])  37.6 us
    ppermute x22, starting transfers between devices, flip(): return lax.ppermute(value, BOTH, [(i, i ^ 1 << bit) for i in range(count)])  29.8 us
    pallas_call x1, Pallas kernels, local(): pl.pallas_call(functools.partial(forward_kernel, groups), name='layer_for...  13.7 us
    pallas_call x1, Pallas kernels, local(): pl.pallas_call(functools.partial(attend_back_kernel, groups), name='atten...  9.82 us
    ppermute x4, starting transfers between devices, around(): return (lax.ppermute(value, 'seq', up), lax.ppermute(value, 'seq', down))  8.24 us
    unnamed x64, local copies, waits for them, and re-layouts  6.46 us
    pallas_call x1, Pallas kernels, local(): pl.pallas_call(functools.partial(backward_kernel, groups), name='layer_ba...  5.32 us
    pallas_call x1, Pallas kernels, local(): pl.pallas_call(functools.partial(back_kernel, dp), name='grad_w_back', co...  3.34 us
  transfers between devices with their start and end apart: 26, of which 7 were waited for; matrix products, arithmetic and copies ran while one was open for 5% of the time, Pallas kernels for 23%

profile of v4, /device:TPU:0, one launch (start us, length us, event | category | flops | bytes accessed | tf_op | source)
XLA Modules:
  0.0 131.6 jit_solution(10346003317365982865)
XLA Ops:
  0.7 2.5 %collective-permute-start = (bf16[256,768]{1,0:T(8,128)(2,1)}, bf16[256,768]{1,0:T(8,128)(2,1)S(1)}, u32[]{:S(2)}, u32[]{:S(2)}) collective-permute-start(bf16[256,768]{1,0:T(8,128)(2,1)} %bitcast.10), channel_id=1, source_target_pairs={{0,1},{1,2},{2,3},{4,5},{5,6},{6,7},{8,9},{9,10},{10,11},{12,13},{... | collective-permute-start | bytes 1179656 | tf_op jit(solution)/shard_map/ppermute | solution.py:751
  3.2 1.3 collective-permute-start.1
  4.5 0.7 constant_dynamic-update-slice_fusion.3
  5.2 0.7 constant_dynamic-update-slice_fusion.2
  5.9 0.7 constant_dynamic-update-slice_fusion.1
  6.6 0.7 constant_dynamic-update-slice_fusion.vec_ref
  7.3 0.7 pad_add_fusion.ids_ref
  8.0 1.0 copy-done.2
  9.0 3.1 %own_projections.1 = (bf16[256,2304]{1,0:T(8,128)(2,1)S(1)}, f32[2,128,384]{2,1,0:T(8,128)S(1)}, f32[2,128,384]{2,1,0:T(8,128)S(1)}, bf16[768,2304]{1,0:T(8,128)(2,1)S(1)}) custom-call(s32[1]{0:T(128)} %bitcast.me_ref, s32[2,2,512]{2,1,0:T(2,128)S(1)} %pad_add_fusion.ids_ref, bf16[256,768]{1,0:T(8,128)(2,1)S(1)} %bitcast.12, ...), custom_call_target="tpu_custom_call" | custom-call | flops 4000000 | bytes 40000 | tf_op jit(solution)/shard_map/own_projections/pallas_call | solution.py:758
  12.2 13.7 %layer_forward.1 = (bf16[2,256,2304]{2,1,0:T(8,128)(2,1)S(1)}, bf16[256,4992]{1,0:T(8,128)(2,1)S(1)}, bf16[256,768]{1,0:T(8,128)(2,1)S(1)}, bf16[256,3072]{1,0:T...) custom-call(s32[1]{0:T(128)} %bitcast.me_ref, ...), custom_call_target="tpu_custom_call" | custom-call | flops 16000000 | bytes 160000 | tf_op jit(solution)/shard_map/layer_forward/pallas_call | solution.py:776
  26.0 3.3 %collective-permute-start.4 = (bf16[256,4992]{1,0:T(8,128)(2,1)S(1)}, bf16[256,4992]{1,0:T(8,128)(2,1)}, u32[]{:S(2)}, u32[]{:S(2)}) collective-permute-start(bf16[256,4992]{1,0:T(8,128)(2,1)S(1)} %get-tuple-element.130.acts_ref.hid.acts.ctx), channel_id=1, source_target_pairs={{0,1},{1,0},{2,3},{3,2},{4,5},{5,4},{6,7},{7,6},{8,9},{9,8},{10,11... | collective-permute-start | bytes 7667720 | tf_op jit(solution)/shard_map/ppermute | solution.py:623
  29.3 5.3 %layer_backward.1 = (bf16[256,1920]{1,0:T(8,128)(2,1)S(1)}, bf16[256,1920]{1,0:T(8,128)(2,1)}, bf16[256,896]{1,0:T(8,128)(2,1)}, f32[256,768]{1,0:T(8,128)S(1)}, f32[7,768]{1,0:T(8,128)S(1)}) custom-call(s32[1]{0:T(128)} %bitcast.me_ref, bf16[256,768]{1,0:T(8,128)(2,1)S(1)} %get-tuple-element.125.feed_ref, ...), custom_call_target="tpu_custom_call" | custom-call | flops 8000000 | bytes 80000 | tf_op jit(solution)/shard_map/layer_backward/pallas_call | solution.py:822
  34.7 0.9 copy-done.13
  35.5 0.6 copy-done.20
  36.2 3.2 %collective-permute-start.2 = (bf16[256,896]{1,0:T(8,128)(2,1)}, bf16[256,896]{1,0:T(8,128)(2,1)}, u32[]{:S(2)}, u32[]{:S(2)}) collective-permute-start(bf16[256,896]{1,0:T(8,128)(2,1)} %get-tuple-element.139.msg_own), channel_id=1, source_target_pairs={{0,1},{1,2},{2,3},{4,5},{5,6},{6,7},{8,9},{9,10},{10,11},{12,13},{... | collective-permute-start | bytes 1376264 | tf_op jit(solution)/shard_map/ppermute | solution.py:751
  39.3 1.3 collective-permute-start.3
  40.6 0.9 copy-done.19
  41.6 3.3 %grad_w_back.1 = (bf16[384,768]{1,0:T(8,128)(2,1)S(1)}, bf16[384,768]{1,0:T(8,128)(2,1)S(1)}, bf16[384,768]{1,0:T(8,128)(2,1)S(1)}, bf16[384,768]{1,0:T(8,128)(2,1)S(1)}) custom-call(s32[1]{0:T(128)} %bitcast.6.d_ref, bf16[256,4992]{1,0:T(8,128)(2,1)S(1)} %get-tuple-element.130.acts_ref.hid.acts.ctx, ...), custom_call_target="tpu_custom_call" | custom-call | flops 3000000 | bytes 30000 | tf_op jit(solution)/shard_map/grad_w_back/pallas_call | solution.py:854
  44.9 1.7 %collective-permute-start.10 = (bf16[384,768]{1,0:T(8,128)(2,1)S(1)}, bf16[384,768]{1,0:T(8,128)(2,1)S(1)}, u32[]{:S(2)}, u32[]{:S(2)}) collective-permute-start(bf16[384,768]{1,0:T(8,128)(2,1)S(1)} %get-tuple-element.161), channel_id=1, source_target_pairs={{0,8},{1,9},{2,10},{3,11},{4,12},{5,13},{6,14},{7,15},{8,0},{9,1},... | collective-permute-start | bytes 1769480 | tf_op jit(solution)/shard_map/ppermute | solution.py:623
  46.6 1.5 %collective-permute-start.9 = (bf16[384,768]{1,0:T(8,128)(2,1)S(1)}, bf16[384,768]{1,0:T(8,128)(2,1)S(1)}, u32[]{:S(2)}, u32[]{:S(2)}) collective-permute-start(bf16[384,768]{1,0:T(8,128)(2,1)S(1)} %get-tuple-element.159), channel_id=1, source_target_pairs={{0,4},{1,5},{2,6},{3,7},{4,0},{5,1},{6,2},{7,3},{8,12},{9,13},{10,... | collective-permute-start | bytes 1769480 | tf_op jit(solution)/shard_map/ppermute | solution.py:623
  48.2 3.1 %grad_w_in.1 = (bf16[384,768]{1,0:T(8,128)(2,1)S(1)}, bf16[384,768]{1,0:T(8,128)(2,1)S(1)}, bf16[384,768]{1,0:T(8,128)(2,1)S(1)}, bf16[384,768]{1,0:T(8,128)(2,1)S(1)}) custom-call(s32[1]{0:T(128)} %bitcast.6.d_ref, bf16[256,4992]{1,0:T(8,128)(2,1)S(1)} %get-tuple-element.130.acts_ref.hid.acts.ctx, ...), custom_call_target="tpu_custom_call" | custom-call | flops 4000000 | bytes 40000 | tf_op jit(solution)/shard_map/grad_w_in/pallas_call | solution.py:871
  51.3 3.3 %collective-permute-start.6 = (bf16[384,768]{1,0:T(8,128)(2,1)S(1)}, bf16[384,768]{1,0:T(8,128)(2,1)S(1)}, u32[]{:S(2)}, u32[]{:S(2)}) collective-permute-start(bf16[384,768]{1,0:T(8,128)(2,1)S(1)} %get-tuple-element.153), channel_id=1, source_target_pairs={{0,2},{1,3},{2,0},{3,1},{4,6},{5,7},{6,4},{7,5},{8,10},{9,11},{10,... | collective-permute-start | bytes 1769480 | tf_op jit(solution)/shard_map/ppermute | solution.py:623
  54.5 0.4 collective-permute-start.7
  55.0 9.8 %attend_backward.1 = (bf16[256,2304]{1,0:T(8,128)(2,1)S(1)}, bf16[256,1152]{1,0:T(8,128)(2,1)S(1)}, bf16[144,1152]{1,0:T(8,128)(2,1)S(1)}, bf16[128,1152]{1,0:T(8,128)(2,1)S(1)}, f32[16,768]{1,0:T(8,128)S(1)}) custom-call(s32[1]{0:T(128)} %bitcast.me_ref, f32[2,128,384]{2,1,0:T(8,128)S(1)} %copy-done.11, f32[2,128,384]{2,1,0:T(8,128)S(1)} %copy-done.16, ...), custom_call_target="tpu_custom_call" | custom-call | flops 11000000 | bytes 110000 | tf_op jit(solution)/shard_map/attend_backward/pallas_call | solution.py:890
  64.9 0.3 add_back_0.1
  65.2 0.3 collective-permute-start.14
  65.4 0.3 collective-permute-start.15
  65.7 0.1 pad_add_fusion.1.ids_ref
  65.8 1.5 %collective-permute-done.15.peer2 = bf16[128,1152]{1,0:T(8,128)(2,1)S(1)} collective-permute-done((bf16[128,1152]{1,0:T(8,128)(2,1)S(1)}, bf16[128,1152]{1,0:T(8,128)(2,1)S(1)}, u32[]{:S(2)}, u32[]{:S(2)}) %collective-permute-start.15) | collective-permute-done | bytes 294944 | tf_op jit(solution)/shard_map/ppermute | solution.py:623
  67.3 3.2 %grad_w_qkv_out.1 = (bf16[384,768]{1,0:T(8,128)(2,1)S(1)}, bf16[400,768]{1,0:T(8,128)(2,1)S(1)}, bf16[384,768]{1,0:T(8,128)(2,1)S(1)}, bf16[384,768]{1,0:T(8,128)(2,1)S(1)}, f32[16,768]{1,0:T(8,128)S(1)}) custom-call(s32[2]{0:T(128)S(1)} %pad_add_fusion.1.ids_ref, bf16[256,768]{1,0:T(8,128)(2,1)S(1)} %bitcast.14, bf16[256,768]{1,0:T(8,128)(2,1)S(1)} %copy-done.7, ...), custom_call_target="tpu_custom_call" | custom-call | flops 3000000 | bytes 30000 | tf_op jit(solution)/shard_map/grad_w_qkv_out/pallas_call | solution.py:914
  70.5 1.6 %collective-permute-start.19 = (bf16[400,768]{1,0:T(8,128)(2,1)S(1)}, bf16[400,768]{1,0:T(8,128)(2,1)S(1)}, u32[]{:S(2)}, u32[]{:S(2)}) collective-permute-start(bf16[400,768]{1,0:T(8,128)(2,1)S(1)} %get-tuple-element.185), channel_id=1, source_target_pairs={{0,2},{1,3},{2,0},{3,1},{4,6},{5,7},{6,4},{7,5},{8,10},{9,11},{10,... | collective-permute-start | bytes 1843208 | tf_op jit(solution)/shard_map/ppermute | solution.py:623
  72.1 0.5 collective-permute-start.11
  72.5 1.5 %collective-permute-start.12 = (bf16[192,768]{1,0:T(8,128)(2,1)S(1)}, bf16[192,768]{1,0:T(8,128)(2,1)S(1)}, u32[]{:S(2)}, u32[]{:S(2)}) collective-permute-start(bf16[192,768]{1,0:T(8,128)(2,1)S(1)} %get-tuple-element.166), channel_id=1, source_target_pairs={{0,4},{1,5},{2,6},{3,7},{4,0},{5,1},{6,2},{7,3},{8,12},{9,13},{10,... | collective-permute-start | bytes 884744 | tf_op jit(solution)/shard_map/ppermute | solution.py:623
  74.1 0.3 add_in_0.1
  74.4 1.6 %collective-permute-start.20 = (bf16[384,768]{1,0:T(8,128)(2,1)S(1)}, bf16[384,768]{1,0:T(8,128)(2,1)S(1)}, u32[]{:S(2)}, u32[]{:S(2)}) collective-permute-start(bf16[384,768]{1,0:T(8,128)(2,1)S(1)} %get-tuple-element.189), channel_id=1, source_target_pairs={{0,8},{1,9},{2,10},{3,11},{4,12},{5,13},{6,14},{7,15},{8,0},{9,1},... | collective-permute-start | bytes 1769480 | tf_op jit(solution)/shard_map/ppermute | solution.py:623
  76.0 0.5 collective-permute-start.8
  76.5 5.5 %collective-permute-done.11.got0 = bf16[192,768]{1,0:T(8,128)(2,1)S(1)} collective-permute-done((bf16[192,768]{1,0:T(8,128)(2,1)S(1)}, bf16[192,768]{1,0:T(8,128)(2,1)S(1)}, u32[]{:S(2)}, u32[]{:S(2)}) %collective-permute-start.11) | collective-permute-done | bytes 294944 | tf_op jit(solution)/shard_map/ppermute | solution.py:623
  82.0 0.6 collective-permute-start.16
  82.5 0.1 add_back_1.1
  82.7 1.5 %collective-permute-start.13 = (bf16[192,768]{1,0:T(8,128)(2,1)S(1)}, bf16[192,768]{1,0:T(8,128)(2,1)S(1)}, u32[]{:S(2)}, u32[]{:S(2)}) collective-permute-start(bf16[192,768]{1,0:T(8,128)(2,1)S(1)} %get-tuple-element.169), channel_id=1, source_target_pairs={{0,2},{1,3},{2,0},{3,1},{4,6},{5,7},{6,4},{7,5},{8,10},{9,11},{10,... | collective-permute-start | bytes 884744 | tf_op jit(solution)/shard_map/ppermute | solution.py:623
  84.2 15.9 %collective-permute-done.8.got0 = bf16[192,768]{1,0:T(8,128)(2,1)S(1)} collective-permute-done((bf16[192,768]{1,0:T(8,128)(2,1)S(1)}, bf16[192,768]{1,0:T(8,128)(2,1)S(1)}, u32[]{:S(2)}, u32[]{:S(2)}) %collective-permute-start.8) | collective-permute-done | bytes 294944 | tf_op jit(solution)/shard_map/ppermute | solution.py:623
  100.1 0.1 add_in_1.1
  100.2 0.1 add_back_2.1
  100.3 0.3 add_qkv_0.1
  100.6 0.7 collective-permute-start.21
  101.3 1.5 %collective-permute-start.18 = (bf16[192,768]{1,0:T(8,128)(2,1)S(1)}, bf16[192,768]{1,0:T(8,128)(2,1)S(1)}, u32[]{:S(2)}, u32[]{:S(2)}) collective-permute-start(bf16[192,768]{1,0:T(8,128)(2,1)S(1)} %get-tuple-element.183), channel_id=1, source_target_pairs={{0,4},{1,5},{2,6},{3,7},{4,0},{5,1},{6,2},{7,3},{8,12},{9,13},{10,... | collective-permute-start | bytes 884744 | tf_op jit(solution)/shard_map/ppermute | solution.py:623
  102.8 1.8 %collective-permute-start.22 = (bf16[192,768]{1,0:T(8,128)(2,1)S(1)}, bf16[192,768]{1,0:T(8,128)(2,1)S(1)}, u32[]{:S(2)}, u32[]{:S(2)}) collective-permute-start(bf16[192,768]{1,0:T(8,128)(2,1)S(1)} %get-tuple-element.199), channel_id=1, source_target_pairs={{0,2},{1,3},{2,0},{3,1},{4,6},{5,7},{6,4},{7,5},{8,10},{9,11},{10,... | collective-permute-start | bytes 884744 | tf_op jit(solution)/shard_map/ppermute | solution.py:623
  104.6 2.6 %collective-permute-start.17 = (bf16[96,768]{1,0:T(8,128)(2,1)S(1)}, bf16[96,768]{1,0:T(8,128)(2,1)S(1)}, u32[]{:S(2)}, u32[]{:S(2)}) collective-permute-start(bf16[96,768]{1,0:T(8,128)(2,1)S(1)} %get-tuple-element.182), channel_id=1, source_target_pairs={{0,16},{1,17},{2,18},{3,19},{4,20},{5,21},{6,22},{7,23},{8,24},{9,... | collective-permute-start | bytes 442376 | tf_op jit(solution)/shard_map/ppermute | solution.py:623
  107.2 2.1 %collective-permute-done.18.got = bf16[192,768]{1,0:T(8,128)(2,1)S(1)} collective-permute-done((bf16[192,768]{1,0:T(8,128)(2,1)S(1)}, bf16[192,768]{1,0:T(8,128)(2,1)S(1)}, u32[]{:S(2)}, u32[]{:S(2)}) %collective-permute-start.18) | collective-permute-done | bytes 294944 | tf_op jit(solution)/shard_map/ppermute | solution.py:623
  109.3 0.1 add_in_2.1
  109.3 2.6 %collective-permute-start.24 = (bf16[96,768]{1,0:T(8,128)(2,1)S(1)}, bf16[96,768]{1,0:T(8,128)(2,1)S(1)}, u32[]{:S(2)}, u32[]{:S(2)}) collective-permute-start(bf16[96,768]{1,0:T(8,128)(2,1)S(1)} %get-tuple-element.205), channel_id=1, source_target_pairs={{0,16},{1,17},{2,18},{3,19},{4,20},{5,21},{6,22},{7,23},{8,24},{9,... | collective-permute-start | bytes 442376 | tf_op jit(solution)/shard_map/ppermute | solution.py:623
  112.0 1.3 %collective-permute-done.21.got0 = bf16[208,768]{1,0:T(8,128)(2,1)S(1)} collective-permute-done((bf16[208,768]{1,0:T(8,128)(2,1)S(1)}, bf16[208,768]{1,0:T(8,128)(2,1)S(1)}, u32[]{:S(2)}, u32[]{:S(2)}) %collective-permute-start.21) | collective-permute-done | bytes 319520 | tf_op jit(solution)/shard_map/ppermute | solution.py:623
  113.3 0.1 add_qkv_1.1
  113.5 1.9 %collective-permute-start.23 = (bf16[208,768]{1,0:T(8,128)(2,1)S(1)}, bf16[208,768]{1,0:T(8,128)(2,1)S(1)}, u32[]{:S(2)}, u32[]{:S(2)}) collective-permute-start(bf16[208,768]{1,0:T(8,128)(2,1)S(1)} %get-tuple-element.203), channel_id=1, source_target_pairs={{0,4},{1,5},{2,6},{3,7},{4,0},{5,1},{6,2},{7,3},{8,12},{9,13},{10,... | collective-permute-start | bytes 958472 | tf_op jit(solution)/shard_map/ppermute | solution.py:623
  115.4 1.1 fusion
  116.5 0.3 add_back_3.1
  116.8 3.3 %collective-permute-done.24.got = bf16[96,768]{1,0:T(8,128)(2,1)S(1)} collective-permute-done((bf16[96,768]{1,0:T(8,128)(2,1)S(1)}, bf16[96,768]{1,0:T(8,128)(2,1)S(1)}, u32[]{:S(2)}, u32[]{:S(2)}) %collective-permute-start.24) | collective-permute-done | bytes 147488 | tf_op jit(solution)/shard_map/ppermute | solution.py:623
  120.1 0.7 add_in_3.1
  120.9 0.1 add_qkv_2.1
  121.0 0.1 collective-permute-start.25
  121.1 0.8 add_convert_fusion
  121.9 0.9 copy.32
  122.8 8.0 %collective-permute-done.25.got = bf16[112,768]{1,0:T(8,128)(2,1)S(1)} collective-permute-done((bf16[112,768]{1,0:T(8,128)(2,1)S(1)}, bf16[112,768]{1,0:T(8,128)(2,1)S(1)}, u32[]{:S(2)}, u32[]{:S(2)}) %collective-permute-start.25) | collective-permute-done | bytes 172064 | tf_op jit(solution)/shard_map/ppermute | solution.py:623
  130.8 0.8 add_qkv_3.1
  (78 shorter events, 0.2 us)
Async XLA Ops:
  0.6 11.4 %copy-start.29 = (f32[768]{0:T(1024)S(1)}, f32[768]{0:T(1024)}, u32[]{:S(2)}) copy-start(f32[768]{0:T(1024)} %param.26) | copy-start | bytes 9220
  0.7 11.4 %copy-start.28 = (f32[768]{0:T(1024)S(1)}, f32[768]{0:T(1024)}, u32[]{:S(2)}) copy-start(f32[768]{0:T(1024)} %param.30) | copy-start | bytes 9220
  0.7 11.4 %copy-start.27 = (f32[768]{0:T(1024)S(1)}, f32[768]{0:T(1024)}, u32[]{:S(2)}) copy-start(f32[768]{0:T(1024)} %param.31) | copy-start | bytes 9220
  0.7 11.4 %copy-start.26 = (f32[768]{0:T(1024)S(1)}, f32[768]{0:T(1024)}, u32[]{:S(2)}) copy-start(f32[768]{0:T(1024)} %param.32) | copy-start | bytes 9220
  0.7 11.5 %copy-start.22 = (f32[3072]{0:T(1024)S(1)}, f32[3072]{0:T(1024)}, u32[]{:S(2)}) copy-start(f32[3072]{0:T(1024)} %b_in_ref.1) | copy-start | bytes 36868
  0.7 11.5 %collective-permute-start = (bf16[256,768]{1,0:T(8,128)(2,1)}, bf16[256,768]{1,0:T(8,128)(2,1)S(1)}, u32[]{:S(2)}, u32[]{:S(2)}) collective-permute-start(bf16[256,768]{1,0:T(8,128)(2,1)} %bitcast.10), channel_id=1, source_target_pairs={{0,1},{1,2},{2,3},{4,5},{5,6},{6,7},{8,9},{9,10},{10,11},{12,13},{... | collective-permute-start | bytes 1179656 | tf_op jit(solution)/shard_map/ppermute | solution.py:751
  3.2 9.0 %collective-permute-start.1 = (bf16[256,768]{1,0:T(8,128)(2,1)}, bf16[256,768]{1,0:T(8,128)(2,1)S(1)}, u32[]{:S(2)}, u32[]{:S(2)}) collective-permute-start(bf16[256,768]{1,0:T(8,128)(2,1)} %bitcast.11), channel_id=1, source_target_pairs={{1,0},{2,1},{3,2},{5,4},{6,5},{7,6},{9,8},{10,9},{11,10},{13,12},{... | collective-permute-start | bytes 1179656 | tf_op jit(solution)/shard_map/ppermute | solution.py:751
  8.0 1.0 copy-start.2
  9.0 3.2 %copy-start.12 = (bf16[768,768]{1,0:T(8,128)(2,1)S(1)}, bf16[768,768]{1,0:T(8,128)(2,1)}, u32[]{:S(2)}) copy-start(bf16[768,768]{1,0:T(8,128)(2,1)} %wout_hbm.1) | copy-start | bytes 3538948
  9.0 3.2 %copy-start.17 = (bf16[2,128,768]{2,1,0:T(8,128)(2,1)S(1)}, bf16[2,128,768]{2,1,0:T(8,128)(2,1)}, u32[]{:S(2)}) copy-start(bf16[2,128,768]{2,1,0:T(8,128)(2,1)} %param.33) | copy-start | bytes 1179652
  12.1 13.8 %copy-start = (bf16[256,2304]{1,0:T(8,128)(2,1)}, bf16[256,2304]{1,0:T(8,128)(2,1)S(1)}, u32[]{:S(2)}) copy-start(bf16[256,2304]{1,0:T(8,128)(2,1)S(1)} %get-tuple-element.121.own_ref) | copy-start | bytes 3538948
  12.1 13.8 %copy-start.10 = (f32[2,128,384]{2,1,0:T(8,128)}, f32[2,128,384]{2,1,0:T(8,128)S(1)}, u32[]{:S(2)}) copy-start(f32[2,128,384]{2,1,0:T(8,128)S(1)} %get-tuple-element.122.mask_ref) | copy-start | bytes 1179652
  12.2 13.8 %copy-start.15 = (f32[2,128,384]{2,1,0:T(8,128)}, f32[2,128,384]{2,1,0:T(8,128)S(1)}, u32[]{:S(2)}) copy-start(f32[2,128,384]{2,1,0:T(8,128)S(1)} %get-tuple-element.136.mask_t_ref) | copy-start | bytes 1179652
  12.2 13.8 %copy-start.6 = (bf16[256,768]{1,0:T(8,128)(2,1)}, bf16[256,768]{1,0:T(8,128)(2,1)S(1)}, u32[]{:S(2)}) copy-start(bf16[256,768]{1,0:T(8,128)(2,1)S(1)} %collective-permute-done.tok_prev) | copy-start | bytes 1179652
  12.2 13.8 %copy-start.8 = (bf16[256,768]{1,0:T(8,128)(2,1)}, bf16[256,768]{1,0:T(8,128)(2,1)S(1)}, u32[]{:S(2)}) copy-start(bf16[256,768]{1,0:T(8,128)(2,1)S(1)} %collective-permute-done.1.tok_next) | copy-start | bytes 1179652
  26.0 8.6 %copy-start.4 = (bf16[2,256,2304]{2,1,0:T(8,128)(2,1)}, bf16[2,256,2304]{2,1,0:T(8,128)(2,1)S(1)}, u32[]{:S(2)}) copy-start(bf16[2,256,2304]{2,1,0:T(8,128)(2,1)S(1)} %get-tuple-element.137.near_ref) | copy-start | bytes 7077892
  26.0 8.6 %copy-start.18 = (bf16[256,384]{1,0:T(8,128)(2,1)}, bf16[256,384]{1,0:T(8,128)(2,1)S(1)}, u32[]{:S(2)}) copy-start(bf16[256,384]{1,0:T(8,128)(2,1)S(1)} %get-tuple-element.142.feed) | copy-start | bytes 589828
  26.0 8.6 %copy-start.23 = (f32[3,768]{1,0:T(4,128)}, f32[3,768]{1,0:T(4,128)S(1)}, u32[]{:S(2)}) copy-start(f32[3,768]{1,0:T(4,128)S(1)} %get-tuple-element.149.small1_ref) | copy-start | bytes 27652
  26.0 14.6 %collective-permute-start.4 = (bf16[256,4992]{1,0:T(8,128)(2,1)S(1)}, bf16[256,4992]{1,0:T(8,128)(2,1)}, u32[]{:S(2)}, u32[]{:S(2)}) collective-permute-start(bf16[256,4992]{1,0:T(8,128)(2,1)S(1)} %get-tuple-element.130.acts_ref.hid.acts.ctx), channel_id=1, source_target_pairs={{0,1},{1,0},{2,3},{3,2},{4,5},{5,4},{6,7},{7,6},{8,9},{9,8},{10,11... | collective-permute-start | bytes 7667720 | tf_op jit(solution)/shard_map/ppermute | solution.py:623
  34.6 0.9 copy-start.13
  35.5 0.6 copy-start.20
  36.1 12.0 %collective-permute-start.5 = (bf16[256,1920]{1,0:T(8,128)(2,1)}, bf16[256,1920]{1,0:T(8,128)(2,1)}, u32[]{:S(2)}, u32[]{:S(2)}) collective-permute-start(bf16[256,1920]{1,0:T(8,128)(2,1)} %get-tuple-element.145), channel_id=1, source_target_pairs={{0,1},{1,0},{2,3},{3,2},{4,5},{5,4},{6,7},{7,6},{8,9},{9,8},{10,11... | collective-permute-start | bytes 2949128 | tf_op jit(solution)/shard_map/ppermute | solution.py:623
  36.2 11.9 %collective-permute-start.2 = (bf16[256,896]{1,0:T(8,128)(2,1)}, bf16[256,896]{1,0:T(8,128)(2,1)}, u32[]{:S(2)}, u32[]{:S(2)}) collective-permute-start(bf16[256,896]{1,0:T(8,128)(2,1)} %get-tuple-element.139.msg_own), channel_id=1, source_target_pairs={{0,1},{1,2},{2,3},{4,5},{5,6},{6,7},{8,9},{9,10},{10,11},{12,13},{... | collective-permute-start | bytes 1376264 | tf_op jit(solution)/shard_map/ppermute | solution.py:751
  39.3 8.8 %collective-permute-start.3 = (bf16[256,896]{1,0:T(8,128)(2,1)}, bf16[256,896]{1,0:T(8,128)(2,1)}, u32[]{:S(2)}, u32[]{:S(2)}) collective-permute-start(bf16[256,896]{1,0:T(8,128)(2,1)} %get-tuple-element.139.msg_own), channel_id=1, source_target_pairs={{1,0},{2,1},{3,2},{5,4},{6,5},{7,6},{9,8},{10,9},{11,10},{13,12},{... | collective-permute-start | bytes 1376264 | tf_op jit(solution)/shard_map/ppermute | solution.py:751
  40.6 0.9 copy-start.19
  44.9 20.0 %collective-permute-start.10 = (bf16[384,768]{1,0:T(8,128)(2,1)S(1)}, bf16[384,768]{1,0:T(8,128)(2,1)S(1)}, u32[]{:S(2)}, u32[]{:S(2)}) collective-permute-start(bf16[384,768]{1,0:T(8,128)(2,1)S(1)} %get-tuple-element.161), channel_id=1, source_target_pairs={{0,8},{1,9},{2,10},{3,11},{4,12},{5,13},{6,14},{7,15},{8,0},{9,1},... | collective-permute-start | bytes 1769480 | tf_op jit(solution)/shard_map/ppermute | solution.py:623
  46.6 18.3 %collective-permute-start.9 = (bf16[384,768]{1,0:T(8,128)(2,1)S(1)}, bf16[384,768]{1,0:T(8,128)(2,1)S(1)}, u32[]{:S(2)}, u32[]{:S(2)}) collective-permute-start(bf16[384,768]{1,0:T(8,128)(2,1)S(1)} %get-tuple-element.159), channel_id=1, source_target_pairs={{0,4},{1,5},{2,6},{3,7},{4,0},{5,1},{6,2},{7,3},{8,12},{9,13},{10,... | collective-permute-start | bytes 1769480 | tf_op jit(solution)/shard_map/ppermute | solution.py:623
  48.1 6.9 %copy-start.1 = (bf16[256,2304]{1,0:T(8,128)(2,1)S(1)}, bf16[256,2304]{1,0:T(8,128)(2,1)}, u32[]{:S(2)}) copy-start(bf16[256,2304]{1,0:T(8,128)(2,1)} %copy-done) | copy-start | bytes 3538948
  48.1 6.9 %copy-start.5 = (bf16[2,256,2304]{2,1,0:T(8,128)(2,1)S(1)}, bf16[2,256,2304]{2,1,0:T(8,128)(2,1)}, u32[]{:S(2)}) copy-start(bf16[2,256,2304]{2,1,0:T(8,128)(2,1)} %copy-done.4) | copy-start | bytes 7077892
  48.1 6.9 %copy-start.11 = (f32[2,128,384]{2,1,0:T(8,128)S(1)}, f32[2,128,384]{2,1,0:T(8,128)}, u32[]{:S(2)}) copy-start(f32[2,128,384]{2,1,0:T(8,128)} %copy-done.10) | copy-start | bytes 1179652
  48.1 6.9 %copy-start.16 = (f32[2,128,384]{2,1,0:T(8,128)S(1)}, f32[2,128,384]{2,1,0:T(8,128)}, u32[]{:S(2)}) copy-start(f32[2,128,384]{2,1,0:T(8,128)} %copy-done.15) | copy-start | bytes 1179652
  48.1 6.9 %copy-start.21 = (f32[7,768]{1,0:T(8,128)S(1)}, f32[7,768]{1,0:T(8,128)}, u32[]{:S(2)}) copy-start(f32[7,768]{1,0:T(8,128)} %copy-done.20) | copy-start | bytes 64516
  48.1 6.9 %copy-start.24 = (f32[3,768]{1,0:T(4,128)S(1)}, f32[3,768]{1,0:T(4,128)}, u32[]{:S(2)}) copy-start(f32[3,768]{1,0:T(4,128)} %copy-done.23) | copy-start | bytes 27652
  51.3 22.8 %collective-permute-start.6 = (bf16[384,768]{1,0:T(8,128)(2,1)S(1)}, bf16[384,768]{1,0:T(8,128)(2,1)S(1)}, u32[]{:S(2)}, u32[]{:S(2)}) collective-permute-start(bf16[384,768]{1,0:T(8,128)(2,1)S(1)} %get-tuple-element.153), channel_id=1, source_target_pairs={{0,2},{1,3},{2,0},{3,1},{4,6},{5,7},{6,4},{7,5},{8,10},{9,11},{10,... | collective-permute-start | bytes 1769480 | tf_op jit(solution)/shard_map/ppermute | solution.py:623
  54.5 19.5 %collective-permute-start.7 = (bf16[384,768]{1,0:T(8,128)(2,1)S(1)}, bf16[384,768]{1,0:T(8,128)(2,1)S(1)}, u32[]{:S(2)}, u32[]{:S(2)}) collective-permute-start(bf16[384,768]{1,0:T(8,128)(2,1)S(1)} %get-tuple-element.155), channel_id=1, source_target_pairs={{0,8},{1,9},{2,10},{3,11},{4,12},{5,13},{6,14},{7,15},{8,0},{9,1},... | collective-permute-start | bytes 1769480 | tf_op jit(solution)/shard_map/ppermute | solution.py:623
  64.8 2.5 %copy-start.3 = (bf16[2,128,768]{2,1,0:T(8,128)(2,1)S(1)}, bf16[2,128,768]{2,1,0:T(8,128)(2,1)}, u32[]{:S(2)}) copy-start(bf16[2,128,768]{2,1,0:T(8,128)(2,1)} %param.17) | copy-start | bytes 1179652
  64.9 2.5 %copy-start.7 = (bf16[256,768]{1,0:T(8,128)(2,1)S(1)}, bf16[256,768]{1,0:T(8,128)(2,1)}, u32[]{:S(2)}) copy-start(bf16[256,768]{1,0:T(8,128)(2,1)} %copy-done.6) | copy-start | bytes 1179652
  64.9 2.4 %copy-start.9 = (bf16[256,768]{1,0:T(8,128)(2,1)S(1)}, bf16[256,768]{1,0:T(8,128)(2,1)}, u32[]{:S(2)}) copy-start(bf16[256,768]{1,0:T(8,128)(2,1)} %copy-done.8) | copy-start | bytes 1179652
  65.2 2.1 %collective-permute-start.14 = (bf16[144,1152]{1,0:T(8,128)(2,1)S(1)}, bf16[144,1152]{1,0:T(8,128)(2,1)S(1)}, u32[]{:S(2)}, u32[]{:S(2)}) collective-permute-start(bf16[144,1152]{1,0:T(8,128)(2,1)S(1)} %get-tuple-element.171), channel_id=1, source_target_pairs={{0,1},{1,0},{2,3},{3,2},{4,5},{5,4},{6,7},{7,6},{8,9},{9,8},{10,11... | collective-permute-start | bytes 995336 | tf_op jit(solution)/shard_map/ppermute | solution.py:623
  65.4 1.9 %collective-permute-start.15 = (bf16[128,1152]{1,0:T(8,128)(2,1)S(1)}, bf16[128,1152]{1,0:T(8,128)(2,1)S(1)}, u32[]{:S(2)}, u32[]{:S(2)}) collective-permute-start(bf16[128,1152]{1,0:T(8,128)(2,1)S(1)} %get-tuple-element.172), channel_id=1, source_target_pairs={{0,1},{1,0},{2,3},{3,2},{4,5},{5,4},{6,7},{7,6},{8,9},{9,8},{10,11... | collective-permute-start | bytes 884744 | tf_op jit(solution)/shard_map/ppermute | solution.py:623
  70.5 29.8 %collective-permute-start.19 = (bf16[400,768]{1,0:T(8,128)(2,1)S(1)}, bf16[400,768]{1,0:T(8,128)(2,1)S(1)}, u32[]{:S(2)}, u32[]{:S(2)}) collective-permute-start(bf16[400,768]{1,0:T(8,128)(2,1)S(1)} %get-tuple-element.185), channel_id=1, source_target_pairs={{0,2},{1,3},{2,0},{3,1},{4,6},{5,7},{6,4},{7,5},{8,10},{9,11},{10,... | collective-permute-start | bytes 1843208 | tf_op jit(solution)/shard_map/ppermute | solution.py:623
  72.1 9.9 %collective-permute-start.11 = (bf16[192,768]{1,0:T(8,128)(2,1)S(1)}, bf16[192,768]{1,0:T(8,128)(2,1)S(1)}, u32[]{:S(2)}, u32[]{:S(2)}) collective-permute-start(bf16[192,768]{1,0:T(8,128)(2,1)S(1)} %get-tuple-element.164), channel_id=1, source_target_pairs={{0,8},{1,9},{2,10},{3,11},{4,12},{5,13},{6,14},{7,15},{8,0},{9,1},... | collective-permute-start | bytes 884744 | tf_op jit(solution)/shard_map/ppermute | solution.py:623
  72.5 10.0 %collective-permute-start.12 = (bf16[192,768]{1,0:T(8,128)(2,1)S(1)}, bf16[192,768]{1,0:T(8,128)(2,1)S(1)}, u32[]{:S(2)}, u32[]{:S(2)}) collective-permute-start(bf16[192,768]{1,0:T(8,128)(2,1)S(1)} %get-tuple-element.166), channel_id=1, source_target_pairs={{0,4},{1,5},{2,6},{3,7},{4,0},{5,1},{6,2},{7,3},{8,12},{9,13},{10,... | collective-permute-start | bytes 884744 | tf_op jit(solution)/shard_map/ppermute | solution.py:623
  74.4 25.9 %collective-permute-start.20 = (bf16[384,768]{1,0:T(8,128)(2,1)S(1)}, bf16[384,768]{1,0:T(8,128)(2,1)S(1)}, u32[]{:S(2)}, u32[]{:S(2)}) collective-permute-start(bf16[384,768]{1,0:T(8,128)(2,1)S(1)} %get-tuple-element.189), channel_id=1, source_target_pairs={{0,8},{1,9},{2,10},{3,11},{4,12},{5,13},{6,14},{7,15},{8,0},{9,1},... | collective-permute-start | bytes 1769480 | tf_op jit(solution)/shard_map/ppermute | solution.py:623
  76.0 24.0 %collective-permute-start.8 = (bf16[192,768]{1,0:T(8,128)(2,1)S(1)}, bf16[192,768]{1,0:T(8,128)(2,1)S(1)}, u32[]{:S(2)}, u32[]{:S(2)}) collective-permute-start(bf16[192,768]{1,0:T(8,128)(2,1)S(1)} %get-tuple-element.156), channel_id=1, source_target_pairs={{0,8},{1,9},{2,10},{3,11},{4,12},{5,13},{6,14},{7,15},{8,0},{9,1},... | collective-permute-start | bytes 884744 | tf_op jit(solution)/shard_map/ppermute | solution.py:623
  82.0 18.1 %collective-permute-start.16 = (bf16[192,768]{1,0:T(8,128)(2,1)S(1)}, bf16[192,768]{1,0:T(8,128)(2,1)S(1)}, u32[]{:S(2)}, u32[]{:S(2)}) collective-permute-start(bf16[192,768]{1,0:T(8,128)(2,1)S(1)} %get-tuple-element.179), channel_id=1, source_target_pairs={{0,2},{1,3},{2,0},{3,1},{4,6},{5,7},{6,4},{7,5},{8,10},{9,11},{10,... | collective-permute-start | bytes 884744 | tf_op jit(solution)/shard_map/ppermute | solution.py:623
  82.7 17.5 %collective-permute-start.13 = (bf16[192,768]{1,0:T(8,128)(2,1)S(1)}, bf16[192,768]{1,0:T(8,128)(2,1)S(1)}, u32[]{:S(2)}, u32[]{:S(2)}) collective-permute-start(bf16[192,768]{1,0:T(8,128)(2,1)S(1)} %get-tuple-element.169), channel_id=1, source_target_pairs={{0,2},{1,3},{2,0},{3,1},{4,6},{5,7},{6,4},{7,5},{8,10},{9,11},{10,... | collective-permute-start | bytes 884744 | tf_op jit(solution)/shard_map/ppermute | solution.py:623
  100.2 15.2 %copy-start.25 = (bf16[768,2304]{1,0:T(8,128)(2,1)S(1)}, bf16[768,2304]{1,0:T(8,128)(2,1)}, u32[]{:S(2)}) copy-start(bf16[768,2304]{1,0:T(8,128)(2,1)} %wqkv_hbm.1) | copy-start | bytes 10616836
  100.6 12.7 %collective-permute-start.21 = (bf16[208,768]{1,0:T(8,128)(2,1)S(1)}, bf16[208,768]{1,0:T(8,128)(2,1)S(1)}, u32[]{:S(2)}, u32[]{:S(2)}) collective-permute-start(bf16[208,768]{1,0:T(8,128)(2,1)S(1)} %get-tuple-element.193), channel_id=1, source_target_pairs={{0,8},{1,9},{2,10},{3,11},{4,12},{5,13},{6,14},{7,15},{8,0},{9,1},... | collective-permute-start | bytes 958472 | tf_op jit(solution)/shard_map/ppermute | solution.py:623
  101.3 8.0 %collective-permute-start.18 = (bf16[192,768]{1,0:T(8,128)(2,1)S(1)}, bf16[192,768]{1,0:T(8,128)(2,1)S(1)}, u32[]{:S(2)}, u32[]{:S(2)}) collective-permute-start(bf16[192,768]{1,0:T(8,128)(2,1)S(1)} %get-tuple-element.183), channel_id=1, source_target_pairs={{0,4},{1,5},{2,6},{3,7},{4,0},{5,1},{6,2},{7,3},{8,12},{9,13},{10,... | collective-permute-start | bytes 884744 | tf_op jit(solution)/shard_map/ppermute | solution.py:623
  102.8 10.5 %collective-permute-start.22 = (bf16[192,768]{1,0:T(8,128)(2,1)S(1)}, bf16[192,768]{1,0:T(8,128)(2,1)S(1)}, u32[]{:S(2)}, u32[]{:S(2)}) collective-permute-start(bf16[192,768]{1,0:T(8,128)(2,1)S(1)} %get-tuple-element.199), channel_id=1, source_target_pairs={{0,2},{1,3},{2,0},{3,1},{4,6},{5,7},{6,4},{7,5},{8,10},{9,11},{10,... | collective-permute-start | bytes 884744 | tf_op jit(solution)/shard_map/ppermute | solution.py:623
  104.6 11.9 %collective-permute-start.17 = (bf16[96,768]{1,0:T(8,128)(2,1)S(1)}, bf16[96,768]{1,0:T(8,128)(2,1)S(1)}, u32[]{:S(2)}, u32[]{:S(2)}) collective-permute-start(bf16[96,768]{1,0:T(8,128)(2,1)S(1)} %get-tuple-element.182), channel_id=1, source_target_pairs={{0,16},{1,17},{2,18},{3,19},{4,20},{5,21},{6,22},{7,23},{8,24},{9,... | collective-permute-start | bytes 442376 | tf_op jit(solution)/shard_map/ppermute | solution.py:623
  109.3 10.8 %collective-permute-start.24 = (bf16[96,768]{1,0:T(8,128)(2,1)S(1)}, bf16[96,768]{1,0:T(8,128)(2,1)S(1)}, u32[]{:S(2)}, u32[]{:S(2)}) collective-permute-start(bf16[96,768]{1,0:T(8,128)(2,1)S(1)} %get-tuple-element.205), channel_id=1, source_target_pairs={{0,16},{1,17},{2,18},{3,19},{4,20},{5,21},{6,22},{7,23},{8,24},{9,... | collective-permute-start | bytes 442376 | tf_op jit(solution)/shard_map/ppermute | solution.py:623
  113.5 7.4 %collective-permute-start.23 = (bf16[208,768]{1,0:T(8,128)(2,1)S(1)}, bf16[208,768]{1,0:T(8,128)(2,1)S(1)}, u32[]{:S(2)}, u32[]{:S(2)}) collective-permute-start(bf16[208,768]{1,0:T(8,128)(2,1)S(1)} %get-tuple-element.203), channel_id=1, source_target_pairs={{0,4},{1,5},{2,6},{3,7},{4,0},{5,1},{6,2},{7,3},{8,12},{9,13},{10,... | collective-permute-start | bytes 958472 | tf_op jit(solution)/shard_map/ppermute | solution.py:623
  115.4 5.7 %copy-start.14 = (f32[256,768]{1,0:T(8,128)S(1)}, f32[256,768]{1,0:T(8,128)}, u32[]{:S(2)}) copy-start(f32[256,768]{1,0:T(8,128)} %copy-done.13) | copy-start | bytes 2359300
  121.0 9.8 %collective-permute-start.25 = (bf16[112,768]{1,0:T(8,128)(2,1)S(1)}, bf16[112,768]{1,0:T(8,128)(2,1)S(1)}, u32[]{:S(2)}, u32[]{:S(2)}) collective-permute-start(bf16[112,768]{1,0:T(8,128)(2,1)S(1)} %get-tuple-element.212), channel_id=1, source_target_pairs={{0,16},{1,17},{2,18},{3,19},{4,20},{5,21},{6,22},{7,23},{8,24},{9,... | collective-permute-start | bytes 516104 | tf_op jit(solution)/shard_map/ppermute | solution.py:623

commit v5 on v3

--- a/solution.py
+++ b/solution.py
@@ -1012,7 +1012,7 @@
     )
 
 
-EVENTS = [0, 1, 0, 2, 1, 2, 0, 1, 2, 2]
+EVENTS = [0, 1, 0, 2, 1, 2, 0, 2, 1, 2]
 
 
 def solution(mesh):

time: 132 us -> 133 us (level)
  no operation moved by 1% of the time
where the time goes in v5:
time: 133 us; the launch traced here: 132 us
  Pallas kernels  45.5 us (34%)
  waiting for transfers between devices  38.5 us (29%)
  starting transfers between devices  37.3 us (28%)
  local copies, waits for them, and re-layouts  7.15 us (5%)
  other arithmetic  1.61 us (1%)
    ppermute x22, waiting for transfers between devices, flip(): return lax.ppermute(value, BOTH, [(i, i ^ 1 << bit) for i in range(count)])  38.4 us
    ppermute x22, starting transfers between devices, flip(): return lax.ppermute(value, BOTH, [(i, i ^ 1 << bit) for i in range(count)])  29.1 us
    pallas_call x1, Pallas kernels, local(): pl.pallas_call(functools.partial(forward_kernel, groups), name='layer_for...  13.8 us
    pallas_call x1, Pallas kernels, local(): pl.pallas_call(functools.partial(attend_back_kernel, groups), name='atten...  10.4 us
    ppermute x4, starting transfers between devices, around(): return (lax.ppermute(value, 'seq', up), lax.ppermute(value, 'seq', down))  8.25 us
    unnamed x64, local copies, waits for them, and re-layouts  6.46 us
    pallas_call x1, Pallas kernels, local(): pl.pallas_call(functools.partial(backward_kernel, groups), name='layer_ba...  5.31 us
    pallas_call x1, Pallas kernels, local(): pl.pallas_call(functools.partial(back_kernel, dp), name='grad_w_back', co...  3.34 us
  transfers between devices with their start and end apart: 26, of which 8 were waited for; matrix products, arithmetic and copies ran while one was open for 5% of the time, Pallas kernels for 23%

profile of v5, /device:TPU:0, one launch (start us, length us, event | category | flops | bytes accessed | tf_op | source)
XLA Modules:
  0.0 132.4 jit_solution(8195059216897750154)
XLA Ops:
  0.7 2.5 %collective-permute-start = (bf16[256,768]{1,0:T(8,128)(2,1)}, bf16[256,768]{1,0:T(8,128)(2,1)S(1)}, u32[]{:S(2)}, u32[]{:S(2)}) collective-permute-start(bf16[256,768]{1,0:T(8,128)(2,1)} %bitcast.10), channel_id=1, source_target_pairs={{0,1},{1,2},{2,3},{4,5},{5,6},{6,7},{8,9},{9,10},{10,11},{12,13},{... | collective-permute-start | bytes 1179656 | tf_op jit(solution)/shard_map/ppermute | solution.py:751
  3.2 1.3 collective-permute-start.1
  4.5 0.7 constant_dynamic-update-slice_fusion.3
  5.2 0.7 constant_dynamic-update-slice_fusion.2
  5.9 0.7 constant_dynamic-update-slice_fusion.1
  6.6 0.7 constant_dynamic-update-slice_fusion.vec_ref
  7.3 0.7 pad_add_fusion.ids_ref
  8.0 1.0 copy-done.2
  9.0 3.1 %own_projections.1 = (bf16[256,2304]{1,0:T(8,128)(2,1)S(1)}, f32[2,128,384]{2,1,0:T(8,128)S(1)}, f32[2,128,384]{2,1,0:T(8,128)S(1)}, bf16[768,2304]{1,0:T(8,128)(2,1)S(1)}) custom-call(s32[1]{0:T(128)} %bitcast.me_ref, s32[2,2,512]{2,1,0:T(2,128)S(1)} %pad_add_fusion.ids_ref, bf16[256,768]{1,0:T(8,128)(2,1)S(1)} %bitcast.12, ...), custom_call_target="tpu_custom_call" | custom-call | flops 4000000 | bytes 40000 | tf_op jit(solution)/shard_map/own_projections/pallas_call | solution.py:758
  12.2 13.8 %layer_forward.1 = (bf16[2,256,2304]{2,1,0:T(8,128)(2,1)S(1)}, bf16[256,4992]{1,0:T(8,128)(2,1)S(1)}, bf16[256,768]{1,0:T(8,128)(2,1)S(1)}, bf16[256,3072]{1,0:T...) custom-call(s32[1]{0:T(128)} %bitcast.me_ref, ...), custom_call_target="tpu_custom_call" | custom-call | flops 16000000 | bytes 160000 | tf_op jit(solution)/shard_map/layer_forward/pallas_call | solution.py:776
  26.1 3.3 %collective-permute-start.4 = (bf16[256,4992]{1,0:T(8,128)(2,1)S(1)}, bf16[256,4992]{1,0:T(8,128)(2,1)}, u32[]{:S(2)}, u32[]{:S(2)}) collective-permute-start(bf16[256,4992]{1,0:T(8,128)(2,1)S(1)} %get-tuple-element.132.acts_ref.hid.acts.ctx), channel_id=1, source_target_pairs={{0,1},{1,0},{2,3},{3,2},{4,5},{5,4},{6,7},{7,6},{8,9},{9,8},{10,11... | collective-permute-start | bytes 7667720 | tf_op jit(solution)/shard_map/ppermute | solution.py:623
  29.4 5.3 %layer_backward.1 = (bf16[256,1920]{1,0:T(8,128)(2,1)S(1)}, bf16[256,1920]{1,0:T(8,128)(2,1)}, bf16[256,896]{1,0:T(8,128)(2,1)}, f32[256,768]{1,0:T(8,128)S(1)}, f32[7,768]{1,0:T(8,128)S(1)}) custom-call(s32[1]{0:T(128)} %bitcast.me_ref, bf16[256,768]{1,0:T(8,128)(2,1)S(1)} %get-tuple-element.127.feed_ref, ...), custom_call_target="tpu_custom_call" | custom-call | flops 8000000 | bytes 80000 | tf_op jit(solution)/shard_map/layer_backward/pallas_call | solution.py:822
  34.8 0.9 copy-done.13
  35.6 0.6 copy-done.20
  36.3 3.2 %collective-permute-start.2 = (bf16[256,896]{1,0:T(8,128)(2,1)}, bf16[256,896]{1,0:T(8,128)(2,1)}, u32[]{:S(2)}, u32[]{:S(2)}) collective-permute-start(bf16[256,896]{1,0:T(8,128)(2,1)} %get-tuple-element.141.msg_own), channel_id=1, source_target_pairs={{0,1},{1,2},{2,3},{4,5},{5,6},{6,7},{8,9},{9,10},{10,11},{12,13},{... | collective-permute-start | bytes 1376264 | tf_op jit(solution)/shard_map/ppermute | solution.py:751
  39.4 1.3 collective-permute-start.3
  40.8 0.9 copy-done.19
  41.7 3.3 %grad_w_back.1 = (bf16[384,768]{1,0:T(8,128)(2,1)S(1)}, bf16[384,768]{1,0:T(8,128)(2,1)S(1)}, bf16[384,768]{1,0:T(8,128)(2,1)S(1)}, bf16[384,768]{1,0:T(8,128)(2,1)S(1)}) custom-call(s32[1]{0:T(128)} %bitcast.6.d_ref, bf16[256,4992]{1,0:T(8,128)(2,1)S(1)} %get-tuple-element.132.acts_ref.hid.acts.ctx, ...), custom_call_target="tpu_custom_call" | custom-call | flops 3000000 | bytes 30000 | tf_op jit(solution)/shard_map/grad_w_back/pallas_call | solution.py:854
  45.0 1.6 %collective-permute-start.6 = (bf16[384,768]{1,0:T(8,128)(2,1)S(1)}, bf16[384,768]{1,0:T(8,128)(2,1)S(1)}, u32[]{:S(2)}, u32[]{:S(2)}) collective-permute-start(bf16[384,768]{1,0:T(8,128)(2,1)S(1)} %get-tuple-element.156), channel_id=1, source_target_pairs={{0,4},{1,5},{2,6},{3,7},{4,0},{5,1},{6,2},{7,3},{8,12},{9,13},{10,... | collective-permute-start | bytes 1769480 | tf_op jit(solution)/shard_map/ppermute | solution.py:623
  46.6 1.6 %collective-permute-start.7 = (bf16[384,768]{1,0:T(8,128)(2,1)S(1)}, bf16[384,768]{1,0:T(8,128)(2,1)S(1)}, u32[]{:S(2)}, u32[]{:S(2)}) collective-permute-start(bf16[384,768]{1,0:T(8,128)(2,1)S(1)} %get-tuple-element.158), channel_id=1, source_target_pairs={{0,8},{1,9},{2,10},{3,11},{4,12},{5,13},{6,14},{7,15},{8,0},{9,1},... | collective-permute-start | bytes 1769480 | tf_op jit(solution)/shard_map/ppermute | solution.py:623
  48.3 3.1 %grad_w_in.1 = (bf16[384,768]{1,0:T(8,128)(2,1)S(1)}, bf16[384,768]{1,0:T(8,128)(2,1)S(1)}, bf16[384,768]{1,0:T(8,128)(2,1)S(1)}, bf16[384,768]{1,0:T(8,128)(2,1)S(1)}) custom-call(s32[1]{0:T(128)} %bitcast.6.d_ref, bf16[256,4992]{1,0:T(8,128)(2,1)S(1)} %get-tuple-element.132.acts_ref.hid.acts.ctx, ...), custom_call_target="tpu_custom_call" | custom-call | flops 4000000 | bytes 40000 | tf_op jit(solution)/shard_map/grad_w_in/pallas_call | solution.py:871
  51.4 3.3 %collective-permute-start.13 = (bf16[384,768]{1,0:T(8,128)(2,1)S(1)}, bf16[384,768]{1,0:T(8,128)(2,1)S(1)}, u32[]{:S(2)}, u32[]{:S(2)}) collective-permute-start(bf16[384,768]{1,0:T(8,128)(2,1)S(1)} %get-tuple-element.171), channel_id=1, source_target_pairs={{0,2},{1,3},{2,0},{3,1},{4,6},{5,7},{6,4},{7,5},{8,10},{9,11},{10,... | collective-permute-start | bytes 1769480 | tf_op jit(solution)/shard_map/ppermute | solution.py:623
  54.6 0.4 collective-permute-start.14
  55.1 10.4 %attend_backward.1 = (bf16[256,2304]{1,0:T(8,128)(2,1)S(1)}, bf16[256,1152]{1,0:T(8,128)(2,1)S(1)}, bf16[144,1152]{1,0:T(8,128)(2,1)S(1)}, bf16[128,1152]{1,0:T(8,128)(2,1)S(1)}, f32[16,768]{1,0:T(8,128)S(1)}) custom-call(s32[1]{0:T(128)} %bitcast.me_ref, f32[2,128,384]{2,1,0:T(8,128)S(1)} %copy-done.11, f32[2,128,384]{2,1,0:T(8,128)S(1)} %copy-done.16, ...), custom_call_target="tpu_custom_call" | custom-call | flops 11000000 | bytes 110000 | tf_op jit(solution)/shard_map/attend_backward/pallas_call | solution.py:890
  65.6 0.3 add_back_0.1
  65.9 0.2 collective-permute-start.11
  66.1 0.3 collective-permute-start.12
  66.5 0.1 pad_add_fusion.1.ids_ref
  66.5 1.5 %collective-permute-done.12.peer2 = bf16[128,1152]{1,0:T(8,128)(2,1)S(1)} collective-permute-done((bf16[128,1152]{1,0:T(8,128)(2,1)S(1)}, bf16[128,1152]{1,0:T(8,128)(2,1)S(1)}, u32[]{:S(2)}, u32[]{:S(2)}) %collective-permute-start.12) | collective-permute-done | bytes 294944 | tf_op jit(solution)/shard_map/ppermute | solution.py:623
  68.0 3.2 %grad_w_qkv_out.1 = (bf16[384,768]{1,0:T(8,128)(2,1)S(1)}, bf16[400,768]{1,0:T(8,128)(2,1)S(1)}, bf16[384,768]{1,0:T(8,128)(2,1)S(1)}, bf16[384,768]{1,0:T(8,128)(2,1)S(1)}, f32[16,768]{1,0:T(8,128)S(1)}) custom-call(s32[2]{0:T(128)S(1)} %pad_add_fusion.1.ids_ref, bf16[256,768]{1,0:T(8,128)(2,1)S(1)} %bitcast.14, bf16[256,768]{1,0:T(8,128)(2,1)S(1)} %copy-done.7, ...), custom_call_target="tpu_custom_call" | custom-call | flops 3000000 | bytes 30000 | tf_op jit(solution)/shard_map/grad_w_qkv_out/pallas_call | solution.py:914
  71.2 1.5 %collective-permute-start.18 = (bf16[400,768]{1,0:T(8,128)(2,1)S(1)}, bf16[400,768]{1,0:T(8,128)(2,1)S(1)}, u32[]{:S(2)}, u32[]{:S(2)}) collective-permute-start(bf16[400,768]{1,0:T(8,128)(2,1)S(1)} %get-tuple-element.185), channel_id=1, source_target_pairs={{0,2},{1,3},{2,0},{3,1},{4,6},{5,7},{6,4},{7,5},{8,10},{9,11},{10,... | collective-permute-start | bytes 1843208 | tf_op jit(solution)/shard_map/ppermute | solution.py:623
  72.8 0.6 collective-permute-start.8
  73.4 1.4 %collective-permute-start.9 = (bf16[192,768]{1,0:T(8,128)(2,1)S(1)}, bf16[192,768]{1,0:T(8,128)(2,1)S(1)}, u32[]{:S(2)}, u32[]{:S(2)}) collective-permute-start(bf16[192,768]{1,0:T(8,128)(2,1)S(1)} %get-tuple-element.163), channel_id=1, source_target_pairs={{0,4},{1,5},{2,6},{3,7},{4,0},{5,1},{6,2},{7,3},{8,12},{9,13},{10,... | collective-permute-start | bytes 884744 | tf_op jit(solution)/shard_map/ppermute | solution.py:623
  74.8 0.3 collective-permute-done.14.got1
  75.1 0.3 add_in_0.1
  75.4 1.7 %collective-permute-start.19 = (bf16[384,768]{1,0:T(8,128)(2,1)S(1)}, bf16[384,768]{1,0:T(8,128)(2,1)S(1)}, u32[]{:S(2)}, u32[]{:S(2)}) collective-permute-start(bf16[384,768]{1,0:T(8,128)(2,1)S(1)} %get-tuple-element.191), channel_id=1, source_target_pairs={{0,8},{1,9},{2,10},{3,11},{4,12},{5,13},{6,14},{7,15},{8,0},{9,1},... | collective-permute-start | bytes 1769480 | tf_op jit(solution)/shard_map/ppermute | solution.py:623
  77.0 0.4 collective-permute-start.15
  77.5 5.1 %collective-permute-done.8.got0 = bf16[192,768]{1,0:T(8,128)(2,1)S(1)} collective-permute-done((bf16[192,768]{1,0:T(8,128)(2,1)S(1)}, bf16[192,768]{1,0:T(8,128)(2,1)S(1)}, u32[]{:S(2)}, u32[]{:S(2)}) %collective-permute-start.8) | collective-permute-done | bytes 294944 | tf_op jit(solution)/shard_map/ppermute | solution.py:623
  82.6 1.7 %collective-permute-start.16 = (bf16[192,768]{1,0:T(8,128)(2,1)S(1)}, bf16[192,768]{1,0:T(8,128)(2,1)S(1)}, u32[]{:S(2)}, u32[]{:S(2)}) collective-permute-start(bf16[192,768]{1,0:T(8,128)(2,1)S(1)} %get-tuple-element.180), channel_id=1, source_target_pairs={{0,2},{1,3},{2,0},{3,1},{4,6},{5,7},{6,4},{7,5},{8,10},{9,11},{10,... | collective-permute-start | bytes 884744 | tf_op jit(solution)/shard_map/ppermute | solution.py:623
  84.3 0.1 add_back_1.1
  84.5 0.4 collective-permute-start.10
  84.9 15.9 %collective-permute-done.15.got0 = bf16[192,768]{1,0:T(8,128)(2,1)S(1)} collective-permute-done((bf16[192,768]{1,0:T(8,128)(2,1)S(1)}, bf16[192,768]{1,0:T(8,128)(2,1)S(1)}, u32[]{:S(2)}, u32[]{:S(2)}) %collective-permute-start.15) | collective-permute-done | bytes 294944 | tf_op jit(solution)/shard_map/ppermute | solution.py:623
  100.8 0.1 add_in_1.1
  101.0 0.1 add_back_2.1
  101.1 0.3 add_qkv_0.1
  101.3 1.5 %collective-permute-start.22 = (bf16[208,768]{1,0:T(8,128)(2,1)S(1)}, bf16[208,768]{1,0:T(8,128)(2,1)S(1)}, u32[]{:S(2)}, u32[]{:S(2)}) collective-permute-start(bf16[208,768]{1,0:T(8,128)(2,1)S(1)} %get-tuple-element.198), channel_id=1, source_target_pairs={{0,8},{1,9},{2,10},{3,11},{4,12},{5,13},{6,14},{7,15},{8,0},{9,1},... | collective-permute-start | bytes 958472 | tf_op jit(solution)/shard_map/ppermute | solution.py:623
  102.9 0.5 collective-permute-start.17
  103.4 1.5 %collective-permute-start.23 = (bf16[192,768]{1,0:T(8,128)(2,1)S(1)}, bf16[192,768]{1,0:T(8,128)(2,1)S(1)}, u32[]{:S(2)}, u32[]{:S(2)}) collective-permute-start(bf16[192,768]{1,0:T(8,128)(2,1)S(1)} %get-tuple-element.202), channel_id=1, source_target_pairs={{0,2},{1,3},{2,0},{3,1},{4,6},{5,7},{6,4},{7,5},{8,10},{9,11},{10,... | collective-permute-start | bytes 884744 | tf_op jit(solution)/shard_map/ppermute | solution.py:623
  104.9 2.6 %collective-permute-start.21 = (bf16[96,768]{1,0:T(8,128)(2,1)S(1)}, bf16[96,768]{1,0:T(8,128)(2,1)S(1)}, u32[]{:S(2)}, u32[]{:S(2)}) collective-permute-start(bf16[96,768]{1,0:T(8,128)(2,1)S(1)} %get-tuple-element.196), channel_id=1, source_target_pairs={{0,16},{1,17},{2,18},{3,19},{4,20},{5,21},{6,22},{7,23},{8,24},{9,... | collective-permute-start | bytes 442376 | tf_op jit(solution)/shard_map/ppermute | solution.py:623
  107.5 4.1 %collective-permute-done.17.got = bf16[192,768]{1,0:T(8,128)(2,1)S(1)} collective-permute-done((bf16[192,768]{1,0:T(8,128)(2,1)S(1)}, bf16[192,768]{1,0:T(8,128)(2,1)S(1)}, u32[]{:S(2)}, u32[]{:S(2)}) %collective-permute-start.17) | collective-permute-done | bytes 294944 | tf_op jit(solution)/shard_map/ppermute | solution.py:623
  111.7 2.2 %collective-permute-done.22.got0 = bf16[208,768]{1,0:T(8,128)(2,1)S(1)} collective-permute-done((bf16[208,768]{1,0:T(8,128)(2,1)S(1)}, bf16[208,768]{1,0:T(8,128)(2,1)S(1)}, u32[]{:S(2)}, u32[]{:S(2)}) %collective-permute-start.22) | collective-permute-done | bytes 319520 | tf_op jit(solution)/shard_map/ppermute | solution.py:623
  113.9 0.1 add_qkv_1.1
  114.0 1.1 collective-permute-start.24
  115.1 1.1 fusion
  116.2 1.1 collective-permute-start.20
  117.3 0.3 add_back_3.1
  117.6 4.9 %collective-permute-done.24.got = bf16[208,768]{1,0:T(8,128)(2,1)S(1)} collective-permute-done((bf16[208,768]{1,0:T(8,128)(2,1)S(1)}, bf16[208,768]{1,0:T(8,128)(2,1)S(1)}, u32[]{:S(2)}, u32[]{:S(2)}) %collective-permute-start.24) | collective-permute-done | bytes 319520 | tf_op jit(solution)/shard_map/ppermute | solution.py:623
  122.5 0.1 add_qkv_2.1
  122.6 2.2 %collective-permute-start.25 = (bf16[112,768]{1,0:T(8,128)(2,1)S(1)}, bf16[112,768]{1,0:T(8,128)(2,1)S(1)}, u32[]{:S(2)}, u32[]{:S(2)}) collective-permute-start(bf16[112,768]{1,0:T(8,128)(2,1)S(1)} %get-tuple-element.213), channel_id=1, source_target_pairs={{0,16},{1,17},{2,18},{3,19},{4,20},{5,21},{6,22},{7,23},{8,24},{9,... | collective-permute-start | bytes 516104 | tf_op jit(solution)/shard_map/ppermute | solution.py:623
  124.8 0.8 add_convert_fusion
  125.6 0.9 copy.32
  126.5 0.7 add_in_3.1
  127.2 4.4 %collective-permute-done.25.got = bf16[112,768]{1,0:T(8,128)(2,1)S(1)} collective-permute-done((bf16[112,768]{1,0:T(8,128)(2,1)S(1)}, bf16[112,768]{1,0:T(8,128)(2,1)S(1)}, u32[]{:S(2)}, u32[]{:S(2)}) %collective-permute-start.25) | collective-permute-done | bytes 172064 | tf_op jit(solution)/shard_map/ppermute | solution.py:623
  131.6 0.8 add_qkv_3.1
  (78 shorter events, 0.3 us)
Async XLA Ops:
  0.6 11.4 %copy-start.29 = (f32[768]{0:T(1024)S(1)}, f32[768]{0:T(1024)}, u32[]{:S(2)}) copy-start(f32[768]{0:T(1024)} %param.26) | copy-start | bytes 9220
  0.7 11.4 %copy-start.28 = (f32[768]{0:T(1024)S(1)}, f32[768]{0:T(1024)}, u32[]{:S(2)}) copy-start(f32[768]{0:T(1024)} %param.30) | copy-start | bytes 9220
  0.7 11.4 %copy-start.27 = (f32[768]{0:T(1024)S(1)}, f32[768]{0:T(1024)}, u32[]{:S(2)}) copy-start(f32[768]{0:T(1024)} %param.31) | copy-start | bytes 9220
  0.7 11.4 %copy-start.26 = (f32[768]{0:T(1024)S(1)}, f32[768]{0:T(1024)}, u32[]{:S(2)}) copy-start(f32[768]{0:T(1024)} %param.32) | copy-start | bytes 9220
  0.7 11.5 %copy-start.22 = (f32[3072]{0:T(1024)S(1)}, f32[3072]{0:T(1024)}, u32[]{:S(2)}) copy-start(f32[3072]{0:T(1024)} %b_in_ref.1) | copy-start | bytes 36868
  0.7 11.5 %collective-permute-start = (bf16[256,768]{1,0:T(8,128)(2,1)}, bf16[256,768]{1,0:T(8,128)(2,1)S(1)}, u32[]{:S(2)}, u32[]{:S(2)}) collective-permute-start(bf16[256,768]{1,0:T(8,128)(2,1)} %bitcast.10), channel_id=1, source_target_pairs={{0,1},{1,2},{2,3},{4,5},{5,6},{6,7},{8,9},{9,10},{10,11},{12,13},{... | collective-permute-start | bytes 1179656 | tf_op jit(solution)/shard_map/ppermute | solution.py:751
  3.2 9.0 %collective-permute-start.1 = (bf16[256,768]{1,0:T(8,128)(2,1)}, bf16[256,768]{1,0:T(8,128)(2,1)S(1)}, u32[]{:S(2)}, u32[]{:S(2)}) collective-permute-start(bf16[256,768]{1,0:T(8,128)(2,1)} %bitcast.11), channel_id=1, source_target_pairs={{1,0},{2,1},{3,2},{5,4},{6,5},{7,6},{9,8},{10,9},{11,10},{13,12},{... | collective-permute-start | bytes 1179656 | tf_op jit(solution)/shard_map/ppermute | solution.py:751
  8.0 1.0 copy-start.2
  9.0 3.2 %copy-start.12 = (bf16[768,768]{1,0:T(8,128)(2,1)S(1)}, bf16[768,768]{1,0:T(8,128)(2,1)}, u32[]{:S(2)}) copy-start(bf16[768,768]{1,0:T(8,128)(2,1)} %wout_hbm.1) | copy-start | bytes 3538948
  9.0 3.2 %copy-start.17 = (bf16[2,128,768]{2,1,0:T(8,128)(2,1)S(1)}, bf16[2,128,768]{2,1,0:T(8,128)(2,1)}, u32[]{:S(2)}) copy-start(bf16[2,128,768]{2,1,0:T(8,128)(2,1)} %param.33) | copy-start | bytes 1179652
  12.1 13.9 %copy-start = (bf16[256,2304]{1,0:T(8,128)(2,1)}, bf16[256,2304]{1,0:T(8,128)(2,1)S(1)}, u32[]{:S(2)}) copy-start(bf16[256,2304]{1,0:T(8,128)(2,1)S(1)} %get-tuple-element.123.own_ref) | copy-start | bytes 3538948
  12.1 13.9 %copy-start.10 = (f32[2,128,384]{2,1,0:T(8,128)}, f32[2,128,384]{2,1,0:T(8,128)S(1)}, u32[]{:S(2)}) copy-start(f32[2,128,384]{2,1,0:T(8,128)S(1)} %get-tuple-element.124.mask_ref) | copy-start | bytes 1179652
  12.2 13.9 %copy-start.15 = (f32[2,128,384]{2,1,0:T(8,128)}, f32[2,128,384]{2,1,0:T(8,128)S(1)}, u32[]{:S(2)}) copy-start(f32[2,128,384]{2,1,0:T(8,128)S(1)} %get-tuple-element.138.mask_t_ref) | copy-start | bytes 1179652
  12.2 13.9 %copy-start.6 = (bf16[256,768]{1,0:T(8,128)(2,1)}, bf16[256,768]{1,0:T(8,128)(2,1)S(1)}, u32[]{:S(2)}) copy-start(bf16[256,768]{1,0:T(8,128)(2,1)S(1)} %collective-permute-done.tok_prev) | copy-start | bytes 1179652
  12.2 13.9 %copy-start.8 = (bf16[256,768]{1,0:T(8,128)(2,1)}, bf16[256,768]{1,0:T(8,128)(2,1)S(1)}, u32[]{:S(2)}) copy-start(bf16[256,768]{1,0:T(8,128)(2,1)S(1)} %collective-permute-done.1.tok_next) | copy-start | bytes 1179652
  26.1 8.7 %copy-start.4 = (bf16[2,256,2304]{2,1,0:T(8,128)(2,1)}, bf16[2,256,2304]{2,1,0:T(8,128)(2,1)S(1)}, u32[]{:S(2)}) copy-start(bf16[2,256,2304]{2,1,0:T(8,128)(2,1)S(1)} %get-tuple-element.139.near_ref) | copy-start | bytes 7077892
  26.1 8.6 %copy-start.18 = (bf16[256,384]{1,0:T(8,128)(2,1)}, bf16[256,384]{1,0:T(8,128)(2,1)S(1)}, u32[]{:S(2)}) copy-start(bf16[256,384]{1,0:T(8,128)(2,1)S(1)} %get-tuple-element.144.feed) | copy-start | bytes 589828
  26.1 8.6 %copy-start.23 = (f32[3,768]{1,0:T(4,128)}, f32[3,768]{1,0:T(4,128)S(1)}, u32[]{:S(2)}) copy-start(f32[3,768]{1,0:T(4,128)S(1)} %get-tuple-element.151.small1_ref) | copy-start | bytes 27652
  26.1 14.6 %collective-permute-start.4 = (bf16[256,4992]{1,0:T(8,128)(2,1)S(1)}, bf16[256,4992]{1,0:T(8,128)(2,1)}, u32[]{:S(2)}, u32[]{:S(2)}) collective-permute-start(bf16[256,4992]{1,0:T(8,128)(2,1)S(1)} %get-tuple-element.132.acts_ref.hid.acts.ctx), channel_id=1, source_target_pairs={{0,1},{1,0},{2,3},{3,2},{4,5},{5,4},{6,7},{7,6},{8,9},{9,8},{10,11... | collective-permute-start | bytes 7667720 | tf_op jit(solution)/shard_map/ppermute | solution.py:623
  34.8 0.9 copy-start.13
  35.6 0.6 copy-start.20
  36.2 12.0 %collective-permute-start.5 = (bf16[256,1920]{1,0:T(8,128)(2,1)}, bf16[256,1920]{1,0:T(8,128)(2,1)}, u32[]{:S(2)}, u32[]{:S(2)}) collective-permute-start(bf16[256,1920]{1,0:T(8,128)(2,1)} %get-tuple-element.147), channel_id=1, source_target_pairs={{0,1},{1,0},{2,3},{3,2},{4,5},{5,4},{6,7},{7,6},{8,9},{9,8},{10,11... | collective-permute-start | bytes 2949128 | tf_op jit(solution)/shard_map/ppermute | solution.py:623
  36.3 11.9 %collective-permute-start.2 = (bf16[256,896]{1,0:T(8,128)(2,1)}, bf16[256,896]{1,0:T(8,128)(2,1)}, u32[]{:S(2)}, u32[]{:S(2)}) collective-permute-start(bf16[256,896]{1,0:T(8,128)(2,1)} %get-tuple-element.141.msg_own), channel_id=1, source_target_pairs={{0,1},{1,2},{2,3},{4,5},{5,6},{6,7},{8,9},{9,10},{10,11},{12,13},{... | collective-permute-start | bytes 1376264 | tf_op jit(solution)/shard_map/ppermute | solution.py:751
  39.4 8.8 %collective-permute-start.3 = (bf16[256,896]{1,0:T(8,128)(2,1)}, bf16[256,896]{1,0:T(8,128)(2,1)}, u32[]{:S(2)}, u32[]{:S(2)}) collective-permute-start(bf16[256,896]{1,0:T(8,128)(2,1)} %get-tuple-element.141.msg_own), channel_id=1, source_target_pairs={{1,0},{2,1},{3,2},{5,4},{6,5},{7,6},{9,8},{10,9},{11,10},{13,12},{... | collective-permute-start | bytes 1376264 | tf_op jit(solution)/shard_map/ppermute | solution.py:751
  40.7 0.9 copy-start.19
  45.0 20.6 %collective-permute-start.6 = (bf16[384,768]{1,0:T(8,128)(2,1)S(1)}, bf16[384,768]{1,0:T(8,128)(2,1)S(1)}, u32[]{:S(2)}, u32[]{:S(2)}) collective-permute-start(bf16[384,768]{1,0:T(8,128)(2,1)S(1)} %get-tuple-element.156), channel_id=1, source_target_pairs={{0,4},{1,5},{2,6},{3,7},{4,0},{5,1},{6,2},{7,3},{8,12},{9,13},{10,... | collective-permute-start | bytes 1769480 | tf_op jit(solution)/shard_map/ppermute | solution.py:623
  46.6 19.0 %collective-permute-start.7 = (bf16[384,768]{1,0:T(8,128)(2,1)S(1)}, bf16[384,768]{1,0:T(8,128)(2,1)S(1)}, u32[]{:S(2)}, u32[]{:S(2)}) collective-permute-start(bf16[384,768]{1,0:T(8,128)(2,1)S(1)} %get-tuple-element.158), channel_id=1, source_target_pairs={{0,8},{1,9},{2,10},{3,11},{4,12},{5,13},{6,14},{7,15},{8,0},{9,1},... | collective-permute-start | bytes 1769480 | tf_op jit(solution)/shard_map/ppermute | solution.py:623
  48.2 6.9 %copy-start.1 = (bf16[256,2304]{1,0:T(8,128)(2,1)S(1)}, bf16[256,2304]{1,0:T(8,128)(2,1)}, u32[]{:S(2)}) copy-start(bf16[256,2304]{1,0:T(8,128)(2,1)} %copy-done) | copy-start | bytes 3538948
  48.2 6.9 %copy-start.5 = (bf16[2,256,2304]{2,1,0:T(8,128)(2,1)S(1)}, bf16[2,256,2304]{2,1,0:T(8,128)(2,1)}, u32[]{:S(2)}) copy-start(bf16[2,256,2304]{2,1,0:T(8,128)(2,1)} %copy-done.4) | copy-start | bytes 7077892
  48.2 6.9 %copy-start.11 = (f32[2,128,384]{2,1,0:T(8,128)S(1)}, f32[2,128,384]{2,1,0:T(8,128)}, u32[]{:S(2)}) copy-start(f32[2,128,384]{2,1,0:T(8,128)} %copy-done.10) | copy-start | bytes 1179652
  48.2 6.9 %copy-start.16 = (f32[2,128,384]{2,1,0:T(8,128)S(1)}, f32[2,128,384]{2,1,0:T(8,128)}, u32[]{:S(2)}) copy-start(f32[2,128,384]{2,1,0:T(8,128)} %copy-done.15) | copy-start | bytes 1179652
  48.2 6.9 %copy-start.21 = (f32[7,768]{1,0:T(8,128)S(1)}, f32[7,768]{1,0:T(8,128)}, u32[]{:S(2)}) copy-start(f32[7,768]{1,0:T(8,128)} %copy-done.20) | copy-start | bytes 64516
  48.2 6.9 %copy-start.24 = (f32[3,768]{1,0:T(4,128)S(1)}, f32[3,768]{1,0:T(4,128)}, u32[]{:S(2)}) copy-start(f32[3,768]{1,0:T(4,128)} %copy-done.23) | copy-start | bytes 27652
  51.4 23.4 %collective-permute-start.13 = (bf16[384,768]{1,0:T(8,128)(2,1)S(1)}, bf16[384,768]{1,0:T(8,128)(2,1)S(1)}, u32[]{:S(2)}, u32[]{:S(2)}) collective-permute-start(bf16[384,768]{1,0:T(8,128)(2,1)S(1)} %get-tuple-element.171), channel_id=1, source_target_pairs={{0,2},{1,3},{2,0},{3,1},{4,6},{5,7},{6,4},{7,5},{8,10},{9,11},{10,... | collective-permute-start | bytes 1769480 | tf_op jit(solution)/shard_map/ppermute | solution.py:623
  54.6 20.5 %collective-permute-start.14 = (bf16[384,768]{1,0:T(8,128)(2,1)S(1)}, bf16[384,768]{1,0:T(8,128)(2,1)S(1)}, u32[]{:S(2)}, u32[]{:S(2)}) collective-permute-start(bf16[384,768]{1,0:T(8,128)(2,1)S(1)} %get-tuple-element.173), channel_id=1, source_target_pairs={{0,8},{1,9},{2,10},{3,11},{4,12},{5,13},{6,14},{7,15},{8,0},{9,1},... | collective-permute-start | bytes 1769480 | tf_op jit(solution)/shard_map/ppermute | solution.py:623
  65.6 2.5 %copy-start.3 = (bf16[2,128,768]{2,1,0:T(8,128)(2,1)S(1)}, bf16[2,128,768]{2,1,0:T(8,128)(2,1)}, u32[]{:S(2)}) copy-start(bf16[2,128,768]{2,1,0:T(8,128)(2,1)} %param.17) | copy-start | bytes 1179652
  65.6 2.5 %copy-start.7 = (bf16[256,768]{1,0:T(8,128)(2,1)S(1)}, bf16[256,768]{1,0:T(8,128)(2,1)}, u32[]{:S(2)}) copy-start(bf16[256,768]{1,0:T(8,128)(2,1)} %copy-done.6) | copy-start | bytes 1179652
  65.6 2.4 %copy-start.9 = (bf16[256,768]{1,0:T(8,128)(2,1)S(1)}, bf16[256,768]{1,0:T(8,128)(2,1)}, u32[]{:S(2)}) copy-start(bf16[256,768]{1,0:T(8,128)(2,1)} %copy-done.8) | copy-start | bytes 1179652
  65.9 2.1 %collective-permute-start.11 = (bf16[144,1152]{1,0:T(8,128)(2,1)S(1)}, bf16[144,1152]{1,0:T(8,128)(2,1)S(1)}, u32[]{:S(2)}, u32[]{:S(2)}) collective-permute-start(bf16[144,1152]{1,0:T(8,128)(2,1)S(1)} %get-tuple-element.166), channel_id=1, source_target_pairs={{0,1},{1,0},{2,3},{3,2},{4,5},{5,4},{6,7},{7,6},{8,9},{9,8},{10,11... | collective-permute-start | bytes 995336 | tf_op jit(solution)/shard_map/ppermute | solution.py:623
  66.1 1.9 %collective-permute-start.12 = (bf16[128,1152]{1,0:T(8,128)(2,1)S(1)}, bf16[128,1152]{1,0:T(8,128)(2,1)S(1)}, u32[]{:S(2)}, u32[]{:S(2)}) collective-permute-start(bf16[128,1152]{1,0:T(8,128)(2,1)S(1)} %get-tuple-element.167), channel_id=1, source_target_pairs={{0,1},{1,0},{2,3},{3,2},{4,5},{5,4},{6,7},{7,6},{8,9},{9,8},{10,11... | collective-permute-start | bytes 884744 | tf_op jit(solution)/shard_map/ppermute | solution.py:623
  71.2 29.8 %collective-permute-start.18 = (bf16[400,768]{1,0:T(8,128)(2,1)S(1)}, bf16[400,768]{1,0:T(8,128)(2,1)S(1)}, u32[]{:S(2)}, u32[]{:S(2)}) collective-permute-start(bf16[400,768]{1,0:T(8,128)(2,1)S(1)} %get-tuple-element.185), channel_id=1, source_target_pairs={{0,2},{1,3},{2,0},{3,1},{4,6},{5,7},{6,4},{7,5},{8,10},{9,11},{10,... | collective-permute-start | bytes 1843208 | tf_op jit(solution)/shard_map/ppermute | solution.py:623
  72.8 9.9 %collective-permute-start.8 = (bf16[192,768]{1,0:T(8,128)(2,1)S(1)}, bf16[192,768]{1,0:T(8,128)(2,1)S(1)}, u32[]{:S(2)}, u32[]{:S(2)}) collective-permute-start(bf16[192,768]{1,0:T(8,128)(2,1)S(1)} %get-tuple-element.161), channel_id=1, source_target_pairs={{0,8},{1,9},{2,10},{3,11},{4,12},{5,13},{6,14},{7,15},{8,0},{9,1},... | collective-permute-start | bytes 884744 | tf_op jit(solution)/shard_map/ppermute | solution.py:623
  73.4 11.0 %collective-permute-start.9 = (bf16[192,768]{1,0:T(8,128)(2,1)S(1)}, bf16[192,768]{1,0:T(8,128)(2,1)S(1)}, u32[]{:S(2)}, u32[]{:S(2)}) collective-permute-start(bf16[192,768]{1,0:T(8,128)(2,1)S(1)} %get-tuple-element.163), channel_id=1, source_target_pairs={{0,4},{1,5},{2,6},{3,7},{4,0},{5,1},{6,2},{7,3},{8,12},{9,13},{10,... | collective-permute-start | bytes 884744 | tf_op jit(solution)/shard_map/ppermute | solution.py:623
  75.4 25.7 %collective-permute-start.19 = (bf16[384,768]{1,0:T(8,128)(2,1)S(1)}, bf16[384,768]{1,0:T(8,128)(2,1)S(1)}, u32[]{:S(2)}, u32[]{:S(2)}) collective-permute-start(bf16[384,768]{1,0:T(8,128)(2,1)S(1)} %get-tuple-element.191), channel_id=1, source_target_pairs={{0,8},{1,9},{2,10},{3,11},{4,12},{5,13},{6,14},{7,15},{8,0},{9,1},... | collective-permute-start | bytes 1769480 | tf_op jit(solution)/shard_map/ppermute | solution.py:623
  77.0 23.8 %collective-permute-start.15 = (bf16[192,768]{1,0:T(8,128)(2,1)S(1)}, bf16[192,768]{1,0:T(8,128)(2,1)S(1)}, u32[]{:S(2)}, u32[]{:S(2)}) collective-permute-start(bf16[192,768]{1,0:T(8,128)(2,1)S(1)} %get-tuple-element.176), channel_id=1, source_target_pairs={{0,8},{1,9},{2,10},{3,11},{4,12},{5,13},{6,14},{7,15},{8,0},{9,1},... | collective-permute-start | bytes 884744 | tf_op jit(solution)/shard_map/ppermute | solution.py:623
  82.6 18.2 %collective-permute-start.16 = (bf16[192,768]{1,0:T(8,128)(2,1)S(1)}, bf16[192,768]{1,0:T(8,128)(2,1)S(1)}, u32[]{:S(2)}, u32[]{:S(2)}) collective-permute-start(bf16[192,768]{1,0:T(8,128)(2,1)S(1)} %get-tuple-element.180), channel_id=1, source_target_pairs={{0,2},{1,3},{2,0},{3,1},{4,6},{5,7},{6,4},{7,5},{8,10},{9,11},{10,... | collective-permute-start | bytes 884744 | tf_op jit(solution)/shard_map/ppermute | solution.py:623
  84.5 16.5 %collective-permute-start.10 = (bf16[192,768]{1,0:T(8,128)(2,1)S(1)}, bf16[192,768]{1,0:T(8,128)(2,1)S(1)}, u32[]{:S(2)}, u32[]{:S(2)}) collective-permute-start(bf16[192,768]{1,0:T(8,128)(2,1)S(1)} %get-tuple-element.164), channel_id=1, source_target_pairs={{0,2},{1,3},{2,0},{3,1},{4,6},{5,7},{6,4},{7,5},{8,10},{9,11},{10,... | collective-permute-start | bytes 884744 | tf_op jit(solution)/shard_map/ppermute | solution.py:623
  100.9 14.2 %copy-start.25 = (bf16[768,2304]{1,0:T(8,128)(2,1)S(1)}, bf16[768,2304]{1,0:T(8,128)(2,1)}, u32[]{:S(2)}) copy-start(bf16[768,2304]{1,0:T(8,128)(2,1)} %wqkv_hbm.1) | copy-start | bytes 10616836
  101.3 12.5 %collective-permute-start.22 = (bf16[208,768]{1,0:T(8,128)(2,1)S(1)}, bf16[208,768]{1,0:T(8,128)(2,1)S(1)}, u32[]{:S(2)}, u32[]{:S(2)}) collective-permute-start(bf16[208,768]{1,0:T(8,128)(2,1)S(1)} %get-tuple-element.198), channel_id=1, source_target_pairs={{0,8},{1,9},{2,10},{3,11},{4,12},{5,13},{6,14},{7,15},{8,0},{9,1},... | collective-permute-start | bytes 958472 | tf_op jit(solution)/shard_map/ppermute | solution.py:623
  102.9 8.7 %collective-permute-start.17 = (bf16[192,768]{1,0:T(8,128)(2,1)S(1)}, bf16[192,768]{1,0:T(8,128)(2,1)S(1)}, u32[]{:S(2)}, u32[]{:S(2)}) collective-permute-start(bf16[192,768]{1,0:T(8,128)(2,1)S(1)} %get-tuple-element.183), channel_id=1, source_target_pairs={{0,4},{1,5},{2,6},{3,7},{4,0},{5,1},{6,2},{7,3},{8,12},{9,13},{10,... | collective-permute-start | bytes 884744 | tf_op jit(solution)/shard_map/ppermute | solution.py:623
  103.4 10.4 %collective-permute-start.23 = (bf16[192,768]{1,0:T(8,128)(2,1)S(1)}, bf16[192,768]{1,0:T(8,128)(2,1)S(1)}, u32[]{:S(2)}, u32[]{:S(2)}) collective-permute-start(bf16[192,768]{1,0:T(8,128)(2,1)S(1)} %get-tuple-element.202), channel_id=1, source_target_pairs={{0,2},{1,3},{2,0},{3,1},{4,6},{5,7},{6,4},{7,5},{8,10},{9,11},{10,... | collective-permute-start | bytes 884744 | tf_op jit(solution)/shard_map/ppermute | solution.py:623
  104.9 12.4 %collective-permute-start.21 = (bf16[96,768]{1,0:T(8,128)(2,1)S(1)}, bf16[96,768]{1,0:T(8,128)(2,1)S(1)}, u32[]{:S(2)}, u32[]{:S(2)}) collective-permute-start(bf16[96,768]{1,0:T(8,128)(2,1)S(1)} %get-tuple-element.196), channel_id=1, source_target_pairs={{0,16},{1,17},{2,18},{3,19},{4,20},{5,21},{6,22},{7,23},{8,24},{9,... | collective-permute-start | bytes 442376 | tf_op jit(solution)/shard_map/ppermute | solution.py:623
  114.0 8.5 %collective-permute-start.24 = (bf16[208,768]{1,0:T(8,128)(2,1)S(1)}, bf16[208,768]{1,0:T(8,128)(2,1)S(1)}, u32[]{:S(2)}, u32[]{:S(2)}) collective-permute-start(bf16[208,768]{1,0:T(8,128)(2,1)S(1)} %get-tuple-element.206), channel_id=1, source_target_pairs={{0,4},{1,5},{2,6},{3,7},{4,0},{5,1},{6,2},{7,3},{8,12},{9,13},{10,... | collective-permute-start | bytes 958472 | tf_op jit(solution)/shard_map/ppermute | solution.py:623
  115.1 9.7 %copy-start.14 = (f32[256,768]{1,0:T(8,128)S(1)}, f32[256,768]{1,0:T(8,128)}, u32[]{:S(2)}) copy-start(f32[256,768]{1,0:T(8,128)} %copy-done.13) | copy-start | bytes 2359300
  116.2 9.4 %collective-permute-start.20 = (bf16[96,768]{1,0:T(8,128)(2,1)S(1)}, bf16[96,768]{1,0:T(8,128)(2,1)S(1)}, u32[]{:S(2)}, u32[]{:S(2)}) collective-permute-start(bf16[96,768]{1,0:T(8,128)(2,1)S(1)} %get-tuple-element.195), channel_id=1, source_target_pairs={{0,16},{1,17},{2,18},{3,19},{4,20},{5,21},{6,22},{7,23},{8,24},{9,... | collective-permute-start | bytes 442376 | tf_op jit(solution)/shard_map/ppermute | solution.py:623
  122.6 9.0 %collective-permute-start.25 = (bf16[112,768]{1,0:T(8,128)(2,1)S(1)}, bf16[112,768]{1,0:T(8,128)(2,1)S(1)}, u32[]{:S(2)}, u32[]{:S(2)}) collective-permute-start(bf16[112,768]{1,0:T(8,128)(2,1)S(1)} %get-tuple-element.213), channel_id=1, source_target_pairs={{0,16},{1,17},{2,18},{3,19},{4,20},{5,21},{6,22},{7,23},{8,24},{9,... | collective-permute-start | bytes 516104 | tf_op jit(solution)/shard_map/ppermute | solution.py:623
